TPU v7x, 32 devices: a whole 2x2x4 slice. The times are simulated.
32 devices in a mesh: wide: 8 (over z, y), narrow: 4 (over x, core).
Axes of the slice: x: 2, y: 2, z: 4, core: 2. Of those that a mesh axis runs over, the one named last changes fastest.
Arguments:
- char_ids: int32 [4096, 50], P(('wide', 'narrow')), may hold values from 0 to 261
- char_mask: int32 [4096, 50], P(('wide', 'narrow')), may hold values 0 or 1
- position_ids: int32 [4096], P(('wide', 'narrow')), may hold values from 0 to 511
- type_ids: int32 [4096], P(('wide', 'narrow')), may hold values from 0 to 1
- key_mask: int32 [8, 512], P('wide'), may hold values from 0 to 1, as said below
- char_table: bfloat16 [262, 16], replicated, may hold values from -6 to 6
- conv_weight: bfloat16 [112, 2048], P(None, ('wide', 'narrow')), may hold values from -0.5 to 0.5
- conv_bias: bfloat16 [2048], P(('wide', 'narrow')), may hold values from -3 to 3
- highway_weight: bfloat16 [2, 2048, 4096], P(None, None, ('wide', 'narrow')), may hold values from -0.125 to 0.125
- highway_bias: bfloat16 [2, 4096], P(None, ('wide', 'narrow')), may hold values from -3 to 3
- proj_weight: bfloat16 [2048, 768], P(None, ('wide', 'narrow')), may hold values from -0.125 to 0.125
- proj_bias: bfloat16 [768], P(('wide', 'narrow')), may hold values from -3 to 3
- position_table: bfloat16 [512, 768], P(None, ('wide', 'narrow')), may hold values from -3 to 3
- type_table: bfloat16 [2, 768], P(None, ('wide', 'narrow')), may hold values from -3 to 3
- embed_gain: bfloat16 [768], P(('wide', 'narrow')), may hold values from 0.5 to 1.5
- embed_shift: bfloat16 [768], P(('wide', 'narrow')), may hold values from -2 to 2
- qkv_weight: bfloat16 [3, 768, 768], P(None, None, 'narrow'), may hold values from -0.21875 to 0.21875
- qv_bias: bfloat16 [2, 768], P(None, 'narrow'), may hold values from -3 to 3
- out_weight: bfloat16 [768, 768], P('narrow'), may hold values from -0.875 to 0.875
- out_bias: bfloat16 [768], replicated, may hold values from -3 to 3
- ln1_gain: bfloat16 [768], replicated, may hold values from 0.5 to 1.5
- ln1_shift: bfloat16 [768], replicated, may hold values from -2 to 2
- up_weight: bfloat16 [768, 3072], P(None, 'narrow'), may hold values from -0.21875 to 0.21875
- up_bias: bfloat16 [3072], P('narrow'), may hold values from -3 to 3
- down_weight: bfloat16 [3072, 768], P('narrow'), may hold values from -0.109375 to 0.109375
- down_bias: bfloat16 [768], replicated, may hold values from -3 to 3
- ln2_gain: bfloat16 [768], replicated, may hold values from 0.5 to 1.5
- ln2_shift: bfloat16 [768], replicated, may hold values from -2 to 2
- cotangent: float32 [4096, 768], P(('wide', 'narrow')), may hold values from -6 to 6
Outputs:
- layer_out: float32 [4096, 768], P(('wide', 'narrow'))
- char_table_grad: float32 [262, 16], replicated
- conv_weight_grad: float32 [112, 2048], P(None, ('wide', 'narrow'))
- conv_bias_grad: float32 [2048], P(('wide', 'narrow'))
- highway_weight_grad: float32 [2, 2048, 4096], P(None, None, ('wide', 'narrow'))
- highway_bias_grad: float32 [2, 4096], P(None, ('wide', 'narrow'))
- proj_weight_grad: float32 [2048, 768], P(None, ('wide', 'narrow'))
- proj_bias_grad: float32 [768], P(('wide', 'narrow'))
- position_table_grad: float32 [512, 768], P(None, ('wide', 'narrow'))
- type_table_grad: float32 [2, 768], P(None, ('wide', 'narrow'))
- embed_gain_grad: float32 [768], P(('wide', 'narrow'))
- embed_shift_grad: float32 [768], P(('wide', 'narrow'))
- qkv_weight_grad: float32 [3, 768, 768], P(None, None, 'narrow')
- qv_bias_grad: float32 [2, 768], P(None, 'narrow')
- out_weight_grad: float32 [768, 768], P('narrow')
- out_bias_grad: float32 [768], replicated
- ln1_gain_grad: float32 [768], replicated
- ln1_shift_grad: float32 [768], replicated
- up_weight_grad: float32 [768, 3072], P(None, 'narrow')
- up_bias_grad: float32 [3072], P('narrow')
- down_weight_grad: float32 [3072, 768], P('narrow')
- down_bias_grad: float32 [768], replicated
- ln2_gain_grad: float32 [768], replicated
- ln2_shift_grad: float32 [768], replicated
Inputs may be any that keep to these rules, and one draw needn't show every extreme that they name: `key_mask`: the ones of each sequence form a prefix that covers half of its 512 words or more.
All inputs are finite; a program needn't handle non-finite values. No bound on the sum of `char_mask` on one device may be relied on, other than what follows from the above.
Results may differ from a plain program's by a relative error of at most 0.02.
Values may be sent and summed in bfloat16 or wider, within the bound.
No kernel may reach another device: no remote copies, remote signals or barrier semaphores. Data moves between devices by JAX's collectives and lax.ppermute only.
A program may use at most 320 MiB of HBM per device.

v0:
```python
import jax
import jax.numpy as jnp
from jax import lax
from jax.sharding import PartitionSpec as P

HEAD_DIM = 64


EPSILON = 1e-05
NEG_FILL = -1000000000.0


def layer_norm(values, gain, shift):
    centre = values - jnp.mean(values, axis=-1, keepdims=True)
    spread = jnp.mean(centre * centre, axis=-1, keepdims=True)
    return centre * lax.rsqrt(spread + EPSILON) * gain + shift


def smooth_gelu(values):
    return jax.nn.gelu(values, approximate=False)


def as_three(item):
    return item.reshape((1,) * (3 - item.ndim) + item.shape)


def from_three(item, rank):
    return item.reshape(item.shape[3 - rank :])


def filter_widths(filter_total):
    index = jnp.arange(filter_total)
    widths = jnp.ones((filter_total,), jnp.int32)
    for level in range(6):
        widths = widths + (index >= filter_total * 2**level // 64).astype(jnp.int32)
    return widths


def pool_masks(word_mask, widths):
    letters = word_mask.shape[1]
    place = jnp.arange(letters)
    usable = (word_mask == 1) | (place[None, :] == 0)
    valid_mask = usable[:, :, None] & (place[None, :, None] <= letters - widths[None, None, :])
    valid_count = jnp.sum(valid_mask.astype(jnp.float32), axis=1)
    return (valid_mask, valid_count)


def pool_feats(conv_out, conv_shift, valid_mask, valid_count):
    pooled = (
        jax.nn.logsumexp(conv_out, axis=1, where=valid_mask) - jnp.log(valid_count) + conv_shift
    )
    return smooth_gelu(pooled)


def char_columns(word_ids, table, tap_count):
    letters = word_ids.shape[1]
    one_hot = (word_ids[:, :, None] == jnp.arange(table.shape[0])[None, None, :]).astype(
        jnp.bfloat16
    )
    embedded = jnp.einsum("bcv,ve->bce", one_hot, table, preferred_element_type=jnp.float32).astype(
        jnp.bfloat16
    )
    padded = jnp.pad(embedded, ((0, 0), (0, tap_count), (0, 0)))
    columns = jnp.concatenate(
        [padded[:, offset : offset + letters] for offset in range(tap_count)], axis=-1
    )
    return (columns, one_hot)


def highway_mix(hidden, mixture):
    width_half = hidden.shape[1]
    nonlinear = smooth_gelu(mixture[:, :width_half])
    opening = jax.nn.sigmoid(mixture[:, width_half:])
    return opening * hidden + (1.0 - opening) * nonlinear


def masked_scores(query_heads, key_heads, keep_mask, score_scale):
    scores = (
        jnp.einsum("qhd,khd->hqk", query_heads, key_heads, preferred_element_type=jnp.float32)
        * score_scale
    )
    return jnp.where(keep_mask[None, None, :] == 1, scores, NEG_FILL)


def attend(query_heads, key_heads, value_heads, keep_mask, score_scale):
    scores = masked_scores(query_heads, key_heads, keep_mask, score_scale)
    row_peak = jnp.max(scores, axis=-1, keepdims=True)
    raised = jnp.exp(scores - row_peak)
    row_total = jnp.sum(raised, axis=-1, keepdims=True)
    attn_weights = (raised / row_total).astype(jnp.bfloat16)
    context = jnp.einsum(
        "hqk,khd->qhd", attn_weights, value_heads, preferred_element_type=jnp.float32
    )
    return (context.astype(jnp.bfloat16), row_peak, row_total)


def attend_back(
    query_heads, key_heads, value_heads, keep_mask, row_peak, row_total, grad_context, score_scale
):
    scores = masked_scores(query_heads, key_heads, keep_mask, score_scale)
    probs_full = jnp.exp(scores - row_peak) / row_total
    attn_weights = probs_full.astype(jnp.bfloat16)
    grad_value = jnp.einsum(
        "hqk,qhd->khd", attn_weights, grad_context, preferred_element_type=jnp.float32
    )
    grad_weights = jnp.einsum(
        "qhd,khd->hqk", grad_context, value_heads, preferred_element_type=jnp.float32
    )
    inner_sum = jnp.sum(grad_weights * probs_full, axis=-1, keepdims=True)
    grad_scores = (probs_full * (grad_weights - inner_sum)).astype(jnp.bfloat16)
    grad_query = (
        jnp.einsum("hqk,khd->qhd", grad_scores, key_heads, preferred_element_type=jnp.float32)
        * score_scale
    )
    grad_key = (
        jnp.einsum("hqk,qhd->khd", grad_scores, query_heads, preferred_element_type=jnp.float32)
        * score_scale
    )
    return (
        grad_query.astype(jnp.bfloat16),
        grad_key.astype(jnp.bfloat16),
        grad_value.astype(jnp.bfloat16),
    )


def per_device(
    char_ids,
    char_mask,
    position_ids,
    type_ids,
    key_mask,
    char_table,
    conv_weight,
    conv_bias,
    highway_weight,
    highway_bias,
    proj_weight,
    proj_bias,
    position_table,
    type_table,
    embed_gain,
    embed_shift,
    qkv_weight,
    qv_bias,
    out_weight,
    out_bias,
    ln1_gain,
    ln1_shift,
    up_weight,
    up_bias,
    down_weight,
    down_bias,
    ln2_gain,
    ln2_shift,
    cotangent,
):
    (
        conv_full,
        conv_bias_full,
        highway_full,
        highway_bias_full,
        proj_full,
        proj_bias_full,
        position_full,
        type_full,
        embed_gain_full,
        embed_shift_full,
    ) = (
        lax.all_gather(conv_weight, ("wide", "narrow"), axis=1, tiled=True),
        lax.all_gather(conv_bias, ("wide", "narrow"), axis=0, tiled=True),
        lax.all_gather(highway_weight, ("wide", "narrow"), axis=2, tiled=True),
        lax.all_gather(highway_bias, ("wide", "narrow"), axis=1, tiled=True),
        lax.all_gather(proj_weight, ("wide", "narrow"), axis=1, tiled=True),
        lax.all_gather(proj_bias, ("wide", "narrow"), axis=0, tiled=True),
        lax.all_gather(position_table, ("wide", "narrow"), axis=1, tiled=True),
        lax.all_gather(type_table, ("wide", "narrow"), axis=1, tiled=True),
        lax.all_gather(embed_gain, ("wide", "narrow"), axis=0, tiled=True),
        lax.all_gather(embed_shift, ("wide", "narrow"), axis=0, tiled=True),
    )
    filters = conv_full.shape[1]
    char_depth = char_table.shape[1]
    tap_count = conv_full.shape[0] // char_depth
    widths = filter_widths(filters)
    tap_keep = (jnp.arange(tap_count * char_depth) // char_depth)[:, None] < widths[None, :]
    conv_masked = jnp.where(tap_keep, conv_full, jnp.zeros_like(conv_full))
    conv_shift = conv_bias_full.astype(jnp.float32)
    word_total = char_ids.shape[0]
    letters = char_ids.shape[1]
    block_words = 64
    block_count = word_total // block_words
    id_blocks = char_ids.reshape(block_count, block_words, letters)
    mask_blocks = char_mask.reshape(block_count, block_words, letters)

    def conv_forward(word_ids, word_mask):
        columns, one_hot = char_columns(word_ids, char_table, tap_count)
        conv_out = jnp.einsum(
            "bcx,xf->bcf", columns, conv_masked, preferred_element_type=jnp.float32
        )
        valid_mask, valid_count = pool_masks(word_mask, widths)
        return (conv_out, columns, one_hot, valid_mask, valid_count)

    def feature_block(block_pair):
        conv_out, columns, one_hot, valid_mask, valid_count = conv_forward(
            block_pair[0], block_pair[1]
        )
        return pool_feats(conv_out, conv_shift, valid_mask, valid_count)

    features = lax.map(feature_block, (id_blocks, mask_blocks)).reshape(word_total, filters)
    hidden = features
    highway_saved = []
    for layer_index in range(2):
        low_input = hidden.astype(jnp.bfloat16)
        mixture = jnp.dot(low_input, highway_full[layer_index], preferred_element_type=jnp.float32)
        mixture = mixture + highway_bias_full[layer_index].astype(jnp.float32)
        highway_saved.append((hidden, low_input, mixture))
        hidden = highway_mix(hidden, mixture)
    proj_input = hidden.astype(jnp.bfloat16)
    projected = jnp.dot(
        proj_input, proj_full, preferred_element_type=jnp.float32
    ) + proj_bias_full.astype(jnp.float32)
    seq_length = position_full.shape[0]
    position_hot = (position_ids[:, None] == jnp.arange(seq_length)[None, :]).astype(jnp.bfloat16)
    type_rows = jnp.where(
        type_ids[:, None] == 1, type_full[1].astype(jnp.float32), type_full[0].astype(jnp.float32)
    )
    summed = (
        projected
        + jnp.dot(position_hot, position_full, preferred_element_type=jnp.float32)
        + type_rows
    )
    first_state, first_pull = jax.vjp(
        layer_norm,
        summed,
        embed_gain_full.astype(jnp.float32),
        embed_shift_full.astype(jnp.float32),
    )
    gathered = lax.all_gather(first_state.astype(jnp.bfloat16), "narrow", axis=0, tiled=True)
    group_rows = gathered.shape[0]
    qkv_out = jnp.einsum("gd,kdc->gkc", gathered, qkv_weight, preferred_element_type=jnp.float32)
    local_width = qkv_out.shape[2]
    head_count = local_width // HEAD_DIM
    sequences = group_rows // seq_length
    seq_shape = (sequences, seq_length, head_count, HEAD_DIM)
    query_heads = (
        (qkv_out[:, 0] + qv_bias[0].astype(jnp.float32)).astype(jnp.bfloat16).reshape(seq_shape)
    )
    key_heads = qkv_out[:, 1].astype(jnp.bfloat16).reshape(seq_shape)
    value_heads = (
        (qkv_out[:, 2] + qv_bias[1].astype(jnp.float32)).astype(jnp.bfloat16).reshape(seq_shape)
    )
    score_scale = HEAD_DIM ** (-0.5)
    context, row_peak, row_total = lax.map(
        lambda seq_block: attend(
            seq_block[0], seq_block[1], seq_block[2], seq_block[3], score_scale
        ),
        (query_heads, key_heads, value_heads, key_mask),
    )
    context_rows = context.reshape(group_rows, local_width)
    piece = context_rows
    attn_branch = lax.psum_scatter(
        jnp.dot(piece, out_weight, preferred_element_type=jnp.float32).astype(jnp.bfloat16),
        "narrow",
        scatter_dimension=0,
        tiled=True,
    ).astype(jnp.float32) + out_bias.astype(jnp.float32)
    second_state, second_pull = jax.vjp(
        layer_norm,
        first_state + attn_branch,
        ln1_gain.astype(jnp.float32),
        ln1_shift.astype(jnp.float32),
    )
    ffn_input = lax.all_gather(second_state.astype(jnp.bfloat16), "narrow", axis=0, tiled=True)
    up_value = jnp.dot(ffn_input, up_weight, preferred_element_type=jnp.float32) + up_bias.astype(
        jnp.float32
    )
    activated = smooth_gelu(up_value).astype(jnp.bfloat16)
    piece = activated
    ffn_branch = lax.psum_scatter(
        jnp.dot(piece, down_weight, preferred_element_type=jnp.float32).astype(jnp.bfloat16),
        "narrow",
        scatter_dimension=0,
        tiled=True,
    ).astype(jnp.float32) + down_bias.astype(jnp.float32)
    layer_out, third_pull = jax.vjp(
        layer_norm,
        second_state + ffn_branch,
        ln2_gain.astype(jnp.float32),
        ln2_shift.astype(jnp.float32),
    )
    grad_third, grad_ln2_gain, grad_ln2_shift = third_pull(cotangent)
    grad_ffn = grad_third.astype(jnp.bfloat16)
    grad_down_bias = jnp.sum(grad_ffn.astype(jnp.float32), axis=0)
    grad_ffn_rows = lax.all_gather(grad_ffn, "narrow", axis=0, tiled=True)
    grad_down_weight = jnp.einsum(
        "gf,gd->fd", activated, grad_ffn_rows, preferred_element_type=jnp.float32
    )
    grad_active = jnp.einsum(
        "gd,fd->gf", grad_ffn_rows, down_weight, preferred_element_type=jnp.float32
    )
    grad_up = jax.vjp(smooth_gelu, up_value)[1](grad_active)[0].astype(jnp.bfloat16)
    grad_up_bias = jnp.sum(grad_up.astype(jnp.float32), axis=0)
    grad_up_weight = jnp.einsum("gd,gf->df", ffn_input, grad_up, preferred_element_type=jnp.float32)
    piece = grad_up
    grad_second = grad_third + lax.psum_scatter(
        jnp.einsum("gf,df->gd", piece, up_weight, preferred_element_type=jnp.float32).astype(
            jnp.bfloat16
        ),
        "narrow",
        scatter_dimension=0,
        tiled=True,
    ).astype(jnp.float32)
    grad_first_branch, grad_ln1_gain, grad_ln1_shift = second_pull(grad_second)
    grad_attn = grad_first_branch.astype(jnp.bfloat16)
    grad_out_bias = jnp.sum(grad_attn.astype(jnp.float32), axis=0)
    grad_attn_rows = lax.all_gather(grad_attn, "narrow", axis=0, tiled=True)
    grad_out_weight = jnp.einsum(
        "gc,gd->cd", context_rows, grad_attn_rows, preferred_element_type=jnp.float32
    )
    grad_context = jnp.einsum(
        "gd,cd->gc", grad_attn_rows, out_weight, preferred_element_type=jnp.float32
    )
    grad_context = grad_context.astype(jnp.bfloat16).reshape(seq_shape)
    grad_query, grad_key, grad_value = lax.map(
        lambda seq_block: attend_back(
            seq_block[0],
            seq_block[1],
            seq_block[2],
            seq_block[3],
            seq_block[4],
            seq_block[5],
            seq_block[6],
            score_scale,
        ),
        (query_heads, key_heads, value_heads, key_mask, row_peak, row_total, grad_context),
    )
    grad_joined = jnp.stack(
        [
            grad_query.reshape(group_rows, local_width),
            grad_key.reshape(group_rows, local_width),
            grad_value.reshape(group_rows, local_width),
        ],
        axis=1,
    )
    grad_qv_bias = jnp.stack(
        [
            jnp.sum(grad_joined[:, 0].astype(jnp.float32), axis=0),
            jnp.sum(grad_joined[:, 2].astype(jnp.float32), axis=0),
        ]
    )
    grad_qkv_weight = jnp.einsum(
        "gd,gkc->kdc", gathered, grad_joined, preferred_element_type=jnp.float32
    )
    (
        grad_qkv_all,
        grad_qv_bias_all,
        grad_out_weight_all,
        grad_up_weight_all,
        grad_up_bias_all,
        grad_down_weight_all,
    ) = lax.psum(
        (
            grad_qkv_weight,
            grad_qv_bias,
            grad_out_weight,
            grad_up_weight,
            grad_up_bias,
            grad_down_weight,
        ),
        "wide",
    )
    piece = grad_joined
    grad_first = grad_first_branch + lax.psum_scatter(
        jnp.einsum("gkc,kdc->gd", piece, qkv_weight, preferred_element_type=jnp.float32).astype(
            jnp.bfloat16
        ),
        "narrow",
        scatter_dimension=0,
        tiled=True,
    ).astype(jnp.float32)
    grad_summed, grad_embed_gain, grad_embed_shift = first_pull(grad_first)
    grad_position = jnp.einsum("rl,rd->ld", position_hot.astype(jnp.float32), grad_summed)
    grad_type = jnp.stack(
        [
            jnp.sum(jnp.where(type_ids[:, None] == 0, grad_summed, 0.0), axis=0),
            jnp.sum(jnp.where(type_ids[:, None] == 1, grad_summed, 0.0), axis=0),
        ]
    )
    grad_proj_low = grad_summed.astype(jnp.bfloat16)
    grad_proj_bias = jnp.sum(grad_proj_low.astype(jnp.float32), axis=0)
    grad_proj_weight = jnp.einsum(
        "rf,rd->fd", proj_input, grad_proj_low, preferred_element_type=jnp.float32
    )
    grad_hidden = jnp.einsum(
        "rd,fd->rf", grad_proj_low, proj_full, preferred_element_type=jnp.float32
    )
    highway_grads = [None, None]
    highway_bias_grads = [None, None]
    for layer_index in (1, 0):
        hidden_in, low_input, mixture = highway_saved[layer_index]
        mix_pull = jax.vjp(highway_mix, hidden_in, mixture)[1]
        grad_direct, grad_mixture = mix_pull(grad_hidden)
        grad_mix_low = grad_mixture.astype(jnp.bfloat16)
        highway_bias_grads[layer_index] = jnp.sum(grad_mix_low.astype(jnp.float32), axis=0)
        highway_grads[layer_index] = jnp.einsum(
            "rf,rm->fm", low_input, grad_mix_low, preferred_element_type=jnp.float32
        )
        grad_hidden = grad_direct + jnp.einsum(
            "rm,fm->rf", grad_mix_low, highway_full[layer_index], preferred_element_type=jnp.float32
        )
    grad_highway = jnp.stack(highway_grads)
    grad_highway_bias = jnp.stack(highway_bias_grads)

    def conv_backward():
        feature_blocks = grad_hidden.reshape(block_count, block_words, filters)

        def conv_step(running, block_inputs):
            sum_weight, sum_bias, sum_table = running
            word_ids, word_mask, grad_block = block_inputs
            conv_out, columns, one_hot, valid_mask, valid_count = conv_forward(word_ids, word_mask)
            pool_pull = jax.vjp(
                lambda conv_value, bias_value: pool_feats(
                    conv_value, bias_value, valid_mask, valid_count
                ),
                conv_out,
                conv_shift,
            )[1]
            grad_conv, grad_bias = pool_pull(grad_block)
            grad_conv_low = grad_conv.astype(jnp.bfloat16)
            sum_weight = sum_weight + jnp.einsum(
                "bcx,bcf->xf", columns, grad_conv_low, preferred_element_type=jnp.float32
            )
            grad_columns = jnp.einsum(
                "bcf,xf->bcx", grad_conv_low, conv_masked, preferred_element_type=jnp.float32
            )
            split_taps = grad_columns.reshape(block_words, letters, tap_count, char_depth)
            grad_embedded = jnp.zeros((block_words, letters, char_depth), jnp.float32)
            for offset in range(tap_count):
                moved = jnp.pad(split_taps[:, :, offset], ((0, 0), (offset, 0), (0, 0)))[
                    :, :letters
                ]
                grad_embedded = grad_embedded + moved
            sum_table = sum_table + jnp.einsum(
                "bcv,bce->ve", one_hot.astype(jnp.float32), grad_embedded
            )
            return ((sum_weight, sum_bias + grad_bias, sum_table), None)

        start_state = (
            jnp.zeros(conv_full.shape, jnp.float32),
            jnp.zeros((filters,), jnp.float32),
            jnp.zeros(char_table.shape, jnp.float32),
        )
        final_state = lax.scan(conv_step, start_state, (id_blocks, mask_blocks, feature_blocks))[0]
        grad_conv_weight = jnp.where(tap_keep, final_state[0], 0.0)
        return (grad_conv_weight, final_state[1], final_state[2])

    grad_conv_weight, grad_conv_bias, grad_table = conv_backward()
    all_parts = (
        grad_conv_weight,
        grad_conv_bias,
        grad_highway,
        grad_highway_bias,
        grad_proj_weight,
        grad_proj_bias,
        grad_position,
        grad_type,
        grad_embed_gain,
        grad_embed_shift,
    )
    all_ranks = tuple((item.ndim for item in all_parts))
    all_owned = (
        lax.psum_scatter(
            as_three(all_parts[0]), ("wide", "narrow"), scatter_dimension=2, tiled=True
        ),
        lax.psum_scatter(
            as_three(all_parts[1]), ("wide", "narrow"), scatter_dimension=2, tiled=True
        ),
        lax.psum_scatter(
            as_three(all_parts[2]), ("wide", "narrow"), scatter_dimension=2, tiled=True
        ),
        lax.psum_scatter(
            as_three(all_parts[3]), ("wide", "narrow"), scatter_dimension=2, tiled=True
        ),
        lax.psum_scatter(
            as_three(all_parts[4]), ("wide", "narrow"), scatter_dimension=2, tiled=True
        ),
        lax.psum_scatter(
            as_three(all_parts[5]), ("wide", "narrow"), scatter_dimension=2, tiled=True
        ),
        lax.psum_scatter(
            as_three(all_parts[6]), ("wide", "narrow"), scatter_dimension=2, tiled=True
        ),
        lax.psum_scatter(
            as_three(all_parts[7]), ("wide", "narrow"), scatter_dimension=2, tiled=True
        ),
        lax.psum_scatter(
            as_three(all_parts[8]), ("wide", "narrow"), scatter_dimension=2, tiled=True
        ),
        lax.psum_scatter(
            as_three(all_parts[9]), ("wide", "narrow"), scatter_dimension=2, tiled=True
        ),
    )
    (
        owned_conv,
        owned_conv_bias,
        owned_highway,
        owned_highway_bias,
        owned_proj,
        owned_proj_bias,
        owned_position,
        owned_type,
        owned_gain,
        owned_shift,
    ) = tuple((from_three(item, rank) for item, rank in zip(all_owned, all_ranks)))
    (
        grad_table_all,
        grad_out_bias_all,
        grad_ln1_gain_all,
        grad_ln1_shift_all,
        grad_down_bias_all,
        grad_ln2_gain_all,
        grad_ln2_shift_all,
    ) = lax.psum(
        (
            grad_table,
            grad_out_bias,
            grad_ln1_gain,
            grad_ln1_shift,
            grad_down_bias,
            grad_ln2_gain,
            grad_ln2_shift,
        ),
        ("wide", "narrow"),
    )
    return (
        layer_out,
        grad_table_all,
        owned_conv,
        owned_conv_bias,
        owned_highway,
        owned_highway_bias,
        owned_proj,
        owned_proj_bias,
        owned_position,
        owned_type,
        owned_gain,
        owned_shift,
        grad_qkv_all,
        grad_qv_bias_all,
        grad_out_weight_all,
        grad_out_bias_all,
        grad_ln1_gain_all,
        grad_ln1_shift_all,
        grad_up_weight_all,
        grad_up_bias_all,
        grad_down_weight_all,
        grad_down_bias_all,
        grad_ln2_gain_all,
        grad_ln2_shift_all,
    )


def solution(mesh):
    return jax.shard_map(
        per_device,
        mesh=mesh,
        in_specs=(
            P(("wide", "narrow"), None),
            P(("wide", "narrow"), None),
            P(("wide", "narrow")),
            P(("wide", "narrow")),
            P("wide", None),
            P(),
            P(None, ("wide", "narrow")),
            P(("wide", "narrow")),
            P(None, None, ("wide", "narrow")),
            P(None, ("wide", "narrow")),
            P(None, ("wide", "narrow")),
            P(("wide", "narrow")),
            P(None, ("wide", "narrow")),
            P(None, ("wide", "narrow")),
            P(("wide", "narrow")),
            P(("wide", "narrow")),
            P(None, None, "narrow"),
            P(None, "narrow"),
            P("narrow", None),
            P(),
            P(),
            P(),
            P(None, "narrow"),
            P("narrow"),
            P("narrow", None),
            P(),
            P(),
            P(),
            P(("wide", "narrow"), None),
        ),
        out_specs=(
            P(("wide", "narrow"), None),
            P(),
            P(None, ("wide", "narrow")),
            P(("wide", "narrow")),
            P(None, None, ("wide", "narrow")),
            P(None, ("wide", "narrow")),
            P(None, ("wide", "narrow")),
            P(("wide", "narrow")),
            P(None, ("wide", "narrow")),
            P(None, ("wide", "narrow")),
            P(("wide", "narrow")),
            P(("wide", "narrow")),
            P(None, None, "narrow"),
            P(None, "narrow"),
            P("narrow", None),
            P(),
            P(),
            P(),
            P(None, "narrow"),
            P("narrow"),
            P("narrow", None),
            P(),
            P(),
            P(),
        ),
        check_vma=False,
    )
```

profile of v0, /device:TPU:0, one launch (start us, length us, event | category | flops | bytes accessed | tf_op | source)
XLA Modules:
  0.0 2167.7 jit_solution(13708151995436950932)
XLA Ops:
  16.6 43.0 %all-reduce.26 = (bf16[2048]{0:T(1024)(128)(2,1)S(1)}, bf16[768]{0:T(1024)(128)(2,1)S(1)}, bf16[768]{0:T(1024)(128)(2,1)S(1)}, bf16[768]{0:T(1024)(128)(2,1)S(1)}) all-reduce(bf16[2048]{0:T(1024)(128)(2,1)S(1)} %dynamic-update-slice, bf16[768]{0:T(1024)(128)(2,1)S(1)} %dynamic-update-slice.1, ...), channel_id=1, replica_groups=mesh['wide'=8,'narrow'=4] {'wide','narrow'}, use_global_device_ids=true, to_apply=%add.12 | all-reduce | flops 4352 | bytes 17408
  60.3 40.3 %all_gather.45 = bf16[2,4096]{1,0:T(2,128)(2,1)S(1)} all-gather(bf16[2,128]{1,0:T(2,128)(2,1)} %param.42), channel_id=1, replica_groups=mesh['wide'=8,'narrow'=4] {'wide','narrow'}, dimensions={1}, use_global_device_ids=true | all-gather | bytes 16896 | tf_op jit(solution)/shard_map/all_gather | solution.py:172
  100.5 36.6 %all-gather = bf16[32,24,2]{1,2,0:T(2,128)(2,1)S(1)} all-gather(bf16[1,24,2]{1,2,0:T(2,128)(2,1)} %bitcast.338), channel_id=1, replica_groups=mesh['wide'=8,'narrow'=4] {'wide','narrow'}, dimensions={0}, use_global_device_ids=true | all-gather | bytes 3168 | tf_op jit(solution)/shard_map/all_gather | solution.py:176
  139.0 40.6 %all_gather.42 = bf16[112,2048]{0,1:T(8,128)(2,1)S(1)} all-gather(bf16[112,64]{0,1:T(8,128)(2,1)S(1)} %copy-done.87), channel_id=1, replica_groups=mesh['wide'=8,'narrow'=4] {'wide','narrow'}, dimensions={1}, use_global_device_ids=true | all-gather | bytes 473088 | tf_op jit(solution)/shard_map/all_gather | solution.py:169
  181.0 60.3 %while.20 = (s32[]{:T(128)}, f32[2,64,2048]{2,1,0:T(8,128)S(1)}, s32[2,64,50]{1,2,0:T(8,128)S(1)}, s32[2,64,50]{1,2,0:T(8,128)S(1)}, bf16[262,16]{0,1:T(8,128)(2...) while((s32[]{:T(128)}, f32[2,64,2048]{2,1,0:T(8,128)S(1)}, ...), condition=%wide.region_4.5_spmd.clone, body=%wide.region_0.4_spmd.clone.sunk | while | flops 1577006080 | bytes 62115596 | solution.py:208
  195.1 14.8 fusion.230
  225.4 14.4 fusion.230
  241.3 40.3 %all_gather.48 = bf16[512,768]{0,1:T(8,128)(2,1)S(1)} all-gather(bf16[512,24]{0,1:T(8,128)(2,1)S(1)} %copy-done.73), channel_id=1, replica_groups=mesh['wide'=8,'narrow'=4] {'wide','narrow'}, dimensions={1}, use_global_device_ids=true | all-gather | bytes 811008 | tf_op jit(solution)/shard_map/all_gather | solution.py:175
  328.2 20.1 reduce-scatter.17.cloned.1.call-done
  366.6 23.7 %reduce-scatter.19.cloned.1.call-done = bf16[128,768]{1,0:T(8,128)(2,1)} async-done(((bf16[512,768]{1,0:T(8,128)(2,1)}), bf16[128,768]{1,0:T(8,128)(2,1)}) %reduce-scatter.19.cloned.1.call-update) | async-done | bytes 196624 | tf_op jit(solution)/shard_map/reduce_scatter | solution.py:278
  406.8 23.8 %reduce-scatter.21.cloned.1.call-done = bf16[128,768]{1,0:T(8,128)(2,1)} async-done(((bf16[512,768]{1,0:T(8,128)(2,1)}), bf16[128,768]{1,0:T(8,128)(2,1)}) %reduce-scatter.21.cloned.1.call-update) | async-done | bytes 196624 | tf_op jit(solution)/shard_map/reduce_scatter | solution.py:304
  450.1 23.6 %reduce-scatter.23.cloned.1.call-done = bf16[128,768]{1,0:T(8,128)(2,1)} async-done(((bf16[512,768]{1,0:T(8,128)(2,1)}), bf16[128,768]{1,0:T(8,128)(2,1)}) %reduce-scatter.23.cloned.1.call-update) | async-done | bytes 196624 | tf_op jit(solution)/shard_map/reduce_scatter | solution.py:372
  510.5 115.6 %while.21 = (s32[]{:T(128)}, f32[112,2048]{1,0:T(8,128)}, f32[2048]{0:T(1024)S(1)}, f32[262,16]{0,1:T(8,128)S(1)}, s32[2,64,50]{1,2,0:T(8,128)S(1)}, /*index=5*/...) while((s32[]{:T(128)}, f32[112,2048]{1,0:T(8,128)}, ...), condition=%wide.region_29.30_spmd.clone, body=%wide.region_24.29_spmd.clone.sunk | while | flops 4615518208 | bytes 136161792 | solution.py:452
  553.1 13.8 fusion.243
  639.9 15.9 copy.118
  668.2 14.4 convolution_bitcast_fusion.2
  695.9 44.7 %pad_maximum_fusion = f32[2,2048,4096]{2,1,0:T(8,128)} fusion(f32[1,2048,4096]{2,1,0:T(8,128)} %convolution_bitcast_fusion.1, f32[1,2048,4096]{2,1,0:T(8,128)} %convolution_bitcast_fusion.2), kind=kLoop, calls=%fused_computation.156 | loop fusion | flops 16777216 | bytes 134217728 | tf_op jit(solution)/shard_map/stack | solution.py:410
  741.4 22.5 %all-reduce.24 = (f32[2,192]{1,0:T(2,128)}, f32[768]{0:T(1024)}) all-reduce(f32[2,192]{1,0:T(2,128)S(1)} %pad_maximum_fusion.4, f32[768]{0:T(1024)S(1)} %copy-done.90), channel_id=1, replica_groups=mesh['wide'=8,'narrow'=4] {'wide'}, use_global_device_ids=true, to_apply=%region_51.52 | all-reduce | flops 1152 | bytes 9216 | tf_op jit(solution)/shard_map/psum | solution.py:360
  764.1 39.0 %all-reduce.22 = (f32[262,16]{0,1:T(8,128)}, f32[1,1,768]{2,1,0:T(1,128)S(1)}, f32[1,2,768]{2,1,0:T(2,128)S(1)}, f32[1,1,768]{2,1,0:T(1,128)S(1)}, f32[1,1,768]{...) all-reduce(f32[262,16]{0,1:T(8,128)S(1)} %copy-done.75, ...), channel_id=1, replica_groups=mesh['wide'=8,'narrow'=4] {'wide','narrow'}, use_global_device_ids=true, to_apply=%region_30.31 | all-reduce | flops 12640 | bytes 101120 | tf_op jit(solution)/shard_map/psum | solution.py:522
  806.2 91.8 %reduce-scatter.31.cloned.1.call-done = f32[128,2]{1,0:T(8,128)} async-done(((f32[4096,2]{1,0:T(8,128)}), f32[128,2]{1,0:T(8,128)}) %reduce-scatter.31.cloned.1.call-update) | async-done | bytes 1040
  899.6 173.3 %all-reduce.30.cloned.1.call-done = (f32[1,2048,768]{1,0,2:T(1,128)}, f32[1,512,768]{1,0,2:T(1,128)}) async-done(((f32[1,2048,768]{1,0,2:T(1,128)}, f32[1,512,768]{1,0,2:T(1,128)}), (f32[1,2048,768]{1,0,2:T(1,128)}, f32[1,512,768]{1,0,2:T(1,128)})) %all-reduce.30.cloned.1.call-update) | async-done | bytes 7864336
  1076.0 134.4 %reduce-scatter.25.cloned.1.call-done = f32[1,112,64]{1,2,0:T(8,128)} async-done(((f32[1,112,2048]{1,2,0:T(8,128)}), f32[1,112,64]{1,2,0:T(8,128)}) %reduce-scatter.25.cloned.1.call-update) | async-done | bytes 28688 | tf_op jit(solution)/shard_map/reduce_scatter | solution.py:471
  1210.4 238.0 %all-reduce.32.cloned.1.call-done = (f32[3,768,192]{1,2,0:T(8,128)}, f32[192,768]{1,0:T(8,128)}, f32[768,768]{1,0:T(8,128)}, f32[768,768]{1,0:T(8,128)}) async-done(((f32[3,768,192]{1,2,0:T(8,128)}, f32[192,768]{1,0:T(8,128)}, f32[768,768]{1,0:T(8,128)}, f32[768,768]{1,0:T(8,128)}), (f32[3,768,192]{1,2,0:T(8,128)}, f32[192,768]{1,0:T(8,128)}, f32[768,768]{1,0:T(8,128)}, ...) | async-done | bytes 7077904 | tf_op jit(solution)/shard_map/psum | solution.py:360
  1448.4 704.3 %reduce-scatter.27.cloned.1.call-done = f32[2,2048,128]{2,1,0:T(8,128)} async-done(((f32[2,2048,4096]{2,1,0:T(8,128)}), f32[2,2048,128]{2,1,0:T(8,128)}) %reduce-scatter.27.cloned.1.call-update) | async-done | bytes 2097168 | tf_op jit(solution)/shard_map/reduce_scatter | solution.py:477
  (476 shorter events, 337.8 us)
Async XLA Ops:
  7.2 351.2 %copy-start = (bf16[768,768]{1,0:T(8,128)(2,1)S(1)}, bf16[768,768]{1,0:T(8,128)(2,1)}, u32[]{:S(2)}) copy-start(bf16[768,768]{1,0:T(8,128)(2,1)} %param.55) | copy-start | bytes 3538948
  7.2 131.8 %copy-start.87 = (bf16[112,64]{0,1:T(8,128)(2,1)S(1)}, bf16[112,64]{0,1:T(8,128)(2,1)}, u32[]{:S(2)}) copy-start(bf16[112,64]{0,1:T(8,128)(2,1)} %param.39) | copy-start | bytes 43012
  7.2 276.5 %all-gather.4.cloned.1.call-start = ((), (), s32[]{:S(2)}) async-start(), calls=%async_computation.8 | async-start | bytes 34603008 | tf_op jit(solution)/shard_map/all_gather | solution.py:171
  8.0 298.4 %all-gather.6.cloned.1.call-start = ((), (), s32[]{:S(2)}) async-start(), calls=%async_computation.9 | async-start | bytes 3244032 | tf_op jit(solution)/shard_map/all_gather | solution.py:173
  8.7 339.6 %reduce-scatter.17.cloned.1.call-start = ((), (), s32[]{:S(2)}) async-start(), calls=%async_computation.10 | async-start | bytes 983040 | tf_op jit(solution)/shard_map/reduce_scatter | solution.py:260
  8.8 172.2 %copy-start.93 = (s32[112]{0:T(128)}, s32[112]{0:T(128)S(1)}, u32[]{:S(2)}) copy-start(s32[112]{0:T(128)S(1)} %and_select_fusion.8) | copy-start | bytes 1348
  8.8 172.2 %copy-start.69 = (s32[2048]{0:T(1024)}, s32[2048]{0:T(1024)S(1)}, u32[]{:S(2)}) copy-start(s32[2048]{0:T(1024)S(1)} %convert_add_fusion.2) | copy-start | bytes 24580
  11.2 169.7 %copy-start.111 = (bf16[262,16]{0,1:T(8,128)(2,1)S(1)}, bf16[262,16]{0,1:T(8,128)(2,1)}, u32[]{:S(2)}) copy-start(bf16[262,16]{0,1:T(8,128)(2,1)} %param.38) | copy-start | bytes 25156
  181.0 60.3 %copy-start.73 = (bf16[512,24]{0,1:T(8,128)(2,1)S(1)}, bf16[512,24]{0,1:T(8,128)(2,1)}, u32[]{:S(2)}) copy-start(bf16[512,24]{0,1:T(8,128)(2,1)} %param.45) | copy-start | bytes 73732
  181.0 100.6 %copy-start.91 = (s32[128]{0:T(128)S(1)}, s32[128]{0:T(128)}, u32[]{:S(2)}) copy-start(s32[128]{0:T(128)} %param.35) | copy-start | bytes 1540
  241.3 42.4 %copy-start.14 = (f32[2,64,2048]{2,1,0:T(8,128)}, f32[2,64,2048]{2,1,0:T(8,128)S(1)}, u32[]{:S(2)}) copy-start(f32[2,64,2048]{2,1,0:T(8,128)S(1)} %get-tuple-element.323) | copy-start | bytes 3145732
  241.3 42.4 %copy-start.36 = (s32[2,64,50]{1,2,0:T(8,128)}, s32[2,64,50]{1,2,0:T(8,128)S(1)}, u32[]{:S(2)}) copy-start(s32[2,64,50]{1,2,0:T(8,128)S(1)} %get-tuple-element.892) | copy-start | bytes 76804
  241.3 42.4 %copy-start.38 = (s32[2,64,50]{1,2,0:T(8,128)}, s32[2,64,50]{1,2,0:T(8,128)S(1)}, u32[]{:S(2)}) copy-start(s32[2,64,50]{1,2,0:T(8,128)S(1)} %get-tuple-element.893) | copy-start | bytes 76804
  241.3 42.4 %copy-start.48 = (f32[2048]{0:T(1024)}, f32[2048]{0:T(1024)S(1)}, u32[]{:S(2)}) copy-start(f32[2048]{0:T(1024)S(1)} %get-tuple-element.898) | copy-start | bytes 24580
  294.3 183.4 %copy-start.2 = (f32[128,2048]{1,0:T(8,128)}, f32[128,2048]{1,0:T(8,128)S(1)}, u32[]{:S(2)}) copy-start(f32[128,2048]{1,0:T(8,128)S(1)} %get-tuple-element.577) | copy-start | bytes 3145732
  328.1 62.2 %reduce-scatter.19.cloned.1.call-start = ((), (), s32[]{:S(2)}) async-start(), calls=%async_computation.11 | async-start | bytes 983040 | tf_op jit(solution)/shard_map/reduce_scatter | solution.py:278
  366.5 64.1 %reduce-scatter.21.cloned.1.call-start = ((), (), s32[]{:S(2)}) async-start(), calls=%async_computation.12 | async-start | bytes 983040 | tf_op jit(solution)/shard_map/reduce_scatter | solution.py:304
  406.8 66.9 %reduce-scatter.23.cloned.1.call-start = ((), (), s32[]{:S(2)}) async-start(), calls=%async_computation.13 | async-start | bytes 983040 | tf_op jit(solution)/shard_map/reduce_scatter | solution.py:372
  449.9 355.0 %reduce-scatter.29.cloned.1.call-start = ((), (), s32[]{:S(2)}) async-start(), calls=%async_computation.16 | async-start | bytes 1081344
  628.0 270.0 %reduce-scatter.31.cloned.1.call-start = ((), (), s32[]{:S(2)}) async-start(), calls=%async_computation.17 | async-start | bytes 2162688
  635.7 437.2 %all-reduce.30.cloned.1.call-start = ((), (), s32[]{:S(2)}) async-start(), calls=%async_computation.18 | async-start | bytes 15728640
  655.9 554.5 %reduce-scatter.25.cloned.1.call-start = ((), (), s32[]{:S(2)}) async-start(), calls=%async_computation.14 | async-start | bytes 1081344 | tf_op jit(solution)/shard_map/reduce_scatter | solution.py:471
  658.7 789.7 %all-reduce.32.cloned.1.call-start = ((), (), s32[]{:S(2)}) async-start(), calls=%async_computation.19 | async-start | bytes 14155776 | tf_op jit(solution)/shard_map/psum | solution.py:360
  666.7 1486.1 %reduce-scatter.27.cloned.1.call-start = ((), (), s32[]{:S(2)}) async-start(), calls=%async_computation.15 | async-start | bytes 69206016 | tf_op jit(solution)/shard_map/reduce_scatter | solution.py:477
  (108 other events, 753.4 us)
Sparse Core Ops, SparseCore 0:
  9.6 201.4 all-gather.3
  214.0 60.6 all-gather.5
  328.2 20.0 reduce-scatter.16
  366.6 23.6 reduce-scatter.18
  406.9 23.6 reduce-scatter.20
  450.0 23.6 reduce-scatter.22
  628.2 134.9 reduce-scatter.28
  765.5 132.5 reduce-scatter.30
  903.9 168.9 all-reduce.29
  1075.5 134.7 reduce-scatter.24
  1216.6 231.7 all-reduce.31
  1451.2 701.5 reduce-scatter.26
where the time goes:
time: 2180 us; the launch traced here: 2170 us
  waiting for transfers between devices  1430 us (66%)
  blocking collectives  296 us (14%)
  matrix products  220 us (10%)
  other arithmetic  137 us (6%)
  local copies, waits for them, and re-layouts  63 us (3%)
    reduce_scatter x1, waiting for transfers between devices, per_device(): lax.psum_scatter(as_three(all_parts[2]), ('wide', 'narrow'), scatter_dime...  704 us
    unnamed x15, waiting for transfers between devices  267 us
    psum x1, waiting for transfers between devices, per_device(): lax.psum((grad_qkv_weight, grad_qv_bias, grad_out_weight, grad_up_weight,...  238 us
    reduce_scatter x1, waiting for transfers between devices, per_device(): lax.psum_scatter(as_three(all_parts[0]), ('wide', 'narrow'), scatter_dime...  134 us
    reduce_sum x6, other arithmetic, pool_feats(): jax.nn.logsumexp(conv_out, axis=1, where=valid_mask) - jnp.log(valid_count)  59.5 us
    dot_general x4, matrix products, conv_forward(): jnp.einsum('bcx,xf->bcf', columns, conv_masked, preferred_element_type=jn...  47.5 us
    another operation x1, other arithmetic, per_device(): grad_highway = jnp.stack(highway_grads)  44.7 us
  transfers between devices with their start and end apart: 12, of which 9 were waited for; matrix products, arithmetic and copies ran while one was open for 10% of the time, Pallas kernels for 0%

commit v1 on v0

v1 whole, which is shorter than its diff:
```python
import functools

import jax
import jax.numpy as jnp
from jax import lax
from jax.experimental import pallas as pl
from jax.experimental.pallas import tpu as pltpu
from jax.sharding import PartitionSpec as P

HEAD_DIM = 64
EPSILON = 1e-05
NEG_FILL = -1000000000.0
SHUT = -1e30
LANES = 128


def layer_norm(values, gain, shift):
    centre = values - jnp.mean(values, axis=-1, keepdims=True)
    spread = jnp.mean(centre * centre, axis=-1, keepdims=True)
    return centre * lax.rsqrt(spread + EPSILON) * gain + shift


def smooth_gelu(values):
    return jax.nn.gelu(values, approximate=False)


def low(values):
    return values.astype(jnp.bfloat16)


def full(values):
    return values.astype(jnp.float32)


def filter_widths(filter_total):
    index = jnp.arange(filter_total)
    widths = jnp.ones((filter_total,), jnp.int32)
    for level in range(6):
        widths = widths + (index >= filter_total * 2**level // 64).astype(jnp.int32)
    return widths


def highway_mix(hidden, mixture):
    width_half = hidden.shape[1]
    nonlinear = smooth_gelu(mixture[:, :width_half])
    opening = jax.nn.sigmoid(mixture[:, width_half:])
    return opening * hidden + (1.0 - opening) * nonlinear


def swap(block, axis, bit):
    size = lax.axis_size(axis)
    return lax.ppermute(block, axis, [(i, i ^ (1 << bit)) for i in range(size)])


def my_bit(axis, bit):
    return (lax.axis_index(axis) >> bit) & 1


def bits_of(axis):
    return [(axis, bit) for bit in range(lax.axis_size(axis).bit_length() - 1)]


def spread(block, bits):
    shape = block.shape
    held = block[None]
    for axis, bit in bits:
        other = swap(held, axis, bit)
        high = my_bit(axis, bit) == 1
        held = jnp.stack([jnp.where(high, other, held), jnp.where(high, held, other)], axis=1)
        held = held.reshape((-1,) + shape)
    return held


def fold(parts, bits):
    shape = parts.shape[1:]
    for axis, bit in bits:
        pairs = parts.reshape((-1, 2) + shape)
        mine = my_bit(axis, bit)
        kept = lax.dynamic_index_in_dim(pairs, mine, 1, keepdims=False)
        sent = low(lax.dynamic_index_in_dim(pairs, 1 - mine, 1, keepdims=False))
        parts = full(kept) + full(swap(sent, axis, bit))
    return parts[0]


def total(value, bits):
    for axis, bit in bits:
        value = value + swap(value, axis, bit)
    return value


def dot_nt(left, right):
    return lax.dot_general(left, right, (((1,), (1,)), ((), ())), preferred_element_type=jnp.float32)


def pool_kernel(cols_ref, filt_ref, lse_ref, *, group):
    letters = cols_ref.shape[0]
    filt = filt_ref[...]
    peak = None
    for first in range(0, letters, group):
        scores = [dot_nt(cols_ref[p], filt) for p in range(first, min(first + group, letters))]
        top = functools.reduce(jnp.maximum, scores)
        if peak is None:
            peak = top
            mass = functools.reduce(jnp.add, [jnp.exp(s - peak) for s in scores])
        else:
            later = jnp.maximum(peak, top)
            fresh = functools.reduce(jnp.add, [jnp.exp(s - later) for s in scores])
            mass = mass * jnp.exp(peak - later) + fresh
            peak = later
    lse_ref[...] = peak + jnp.log(mass)


def pool_forward(columns, filt_rows, block=256):
    letters, words, depth = columns.shape
    filters = filt_rows.shape[0]
    return pl.pallas_call(
        functools.partial(pool_kernel, group=5),
        grid=(filters // block,),
        in_specs=[
            pl.BlockSpec(columns.shape, lambda i: (0, 0, 0)),
            pl.BlockSpec((block, depth), lambda i: (i, 0)),
        ],
        out_specs=pl.BlockSpec((words, block), lambda i: (0, i)),
        out_shape=jax.ShapeDtypeStruct((words, filters), jnp.float32),
        compiler_params=pltpu.CompilerParams(vmem_limit_bytes=48 * 2**20),
        cost_estimate=pl.CostEstimate(
            flops=2 * letters * words * depth * filters,
            bytes_accessed=4 * words * filters,
            transcendentals=letters * words * filters,
        ),
        name="pool_forward",
    )(columns, filt_rows)


def back_kernel(
    cols_ref, cols_t_ref, hot_ref, filt_ref, lse_ref, grad_ref, dw_ref, table_ref, gcol_ref, *, depth, taps
):
    letters, words, lanes = cols_ref.shape
    step = pl.program_id(0)
    filt = filt_ref[...]
    lse = lse_ref[...]
    grad = grad_ref[...]

    @pl.when(step == 0)
    def _():
        gcol_ref[...] = jnp.zeros_like(gcol_ref)

    half = letters // 2
    weight_sum = jnp.zeros((lanes, filt.shape[0]), jnp.float32)
    for first, last in ((0, half), (half, letters)):
        slots = jnp.concatenate(
            [low(grad * jnp.exp(dot_nt(cols_ref[p], filt) - lse)) for p in range(first, last)], axis=0
        )
        at = slice(first * words, last * words)
        gcol_ref[at, :] += jnp.dot(slots, filt, preferred_element_type=jnp.float32)
        weight_sum += jnp.dot(cols_t_ref[:, at], slots, preferred_element_type=jnp.float32)
    dw_ref[...] = weight_sum.T

    @pl.when(step == pl.num_programs(0) - 1)
    def _():
        tap = lax.broadcasted_iota(jnp.int32, (words, lanes), 1) // depth
        table_ref[...] = jnp.zeros_like(table_ref)
        for c in range(letters):
            moved = jnp.where(tap == 0, gcol_ref[c * words : (c + 1) * words, :], 0.0)
            for t in range(1, min(taps, c + 1)):
                moved = jnp.where(tap == t, gcol_ref[(c - t) * words : (c - t + 1) * words, :], moved)
            table_ref[...] += jnp.dot(
                hot_ref[:, c * words : (c + 1) * words], low(moved), preferred_element_type=jnp.float32
            )


def pool_backward(columns, columns_t, hot, filt_rows, lse, grad, depth, taps, block=256):
    letters, words, lanes = columns.shape
    filters = filt_rows.shape[0]
    whole = lambda item: pl.BlockSpec(item.shape, lambda i: (0,) * item.ndim)
    return pl.pallas_call(
        functools.partial(back_kernel, depth=depth, taps=taps),
        grid=(filters // block,),
        in_specs=[
            whole(columns),
            whole(columns_t),
            whole(hot),
            pl.BlockSpec((block, lanes), lambda i: (i, 0)),
            pl.BlockSpec((words, block), lambda i: (0, i)),
            pl.BlockSpec((words, block), lambda i: (0, i)),
        ],
        out_specs=[
            pl.BlockSpec((block, lanes), lambda i: (i, 0)),
            pl.BlockSpec((hot.shape[0], lanes), lambda i: (0, 0)),
        ],
        out_shape=[
            jax.ShapeDtypeStruct((filters, lanes), jnp.float32),
            jax.ShapeDtypeStruct((hot.shape[0], lanes), jnp.float32),
        ],
        scratch_shapes=[pltpu.VMEM((letters * words, lanes), jnp.float32)],
        compiler_params=pltpu.CompilerParams(vmem_limit_bytes=48 * 2**20),
        cost_estimate=pl.CostEstimate(
            flops=6 * letters * words * lanes * filters,
            bytes_accessed=8 * words * filters,
            transcendentals=letters * words * filters,
        ),
        name="pool_backward",
    )(columns, columns_t, hot, filt_rows, lse, grad)


def masked_scores(query_heads, key_heads, keep_mask, score_scale):
    scores = (
        jnp.einsum("qhd,khd->hqk", query_heads, key_heads, preferred_element_type=jnp.float32)
        * score_scale
    )
    return jnp.where(keep_mask[None, None, :] == 1, scores, NEG_FILL)


def attend(query_heads, key_heads, value_heads, keep_mask, score_scale):
    scores = masked_scores(query_heads, key_heads, keep_mask, score_scale)
    row_peak = jnp.max(scores, axis=-1, keepdims=True)
    raised = jnp.exp(scores - row_peak)
    row_total = jnp.sum(raised, axis=-1, keepdims=True)
    attn_weights = (raised / row_total).astype(jnp.bfloat16)
    context = jnp.einsum(
        "hqk,khd->qhd", attn_weights, value_heads, preferred_element_type=jnp.float32
    )
    return (context.astype(jnp.bfloat16), row_peak, row_total)


def attend_back(
    query_heads, key_heads, value_heads, keep_mask, row_peak, row_total, grad_context, score_scale
):
    scores = masked_scores(query_heads, key_heads, keep_mask, score_scale)
    probs_full = jnp.exp(scores - row_peak) / row_total
    attn_weights = probs_full.astype(jnp.bfloat16)
    grad_value = jnp.einsum(
        "hqk,qhd->khd", attn_weights, grad_context, preferred_element_type=jnp.float32
    )
    grad_weights = jnp.einsum(
        "qhd,khd->hqk", grad_context, value_heads, preferred_element_type=jnp.float32
    )
    inner_sum = jnp.sum(grad_weights * probs_full, axis=-1, keepdims=True)
    grad_scores = (probs_full * (grad_weights - inner_sum)).astype(jnp.bfloat16)
    grad_query = (
        jnp.einsum("hqk,khd->qhd", grad_scores, key_heads, preferred_element_type=jnp.float32)
        * score_scale
    )
    grad_key = (
        jnp.einsum("hqk,qhd->khd", grad_scores, query_heads, preferred_element_type=jnp.float32)
        * score_scale
    )
    return (
        grad_query.astype(jnp.bfloat16),
        grad_key.astype(jnp.bfloat16),
        grad_value.astype(jnp.bfloat16),
    )


def per_device(
    char_ids,
    char_mask,
    position_ids,
    type_ids,
    key_mask,
    char_table,
    conv_weight,
    conv_bias,
    highway_weight,
    highway_bias,
    proj_weight,
    proj_bias,
    position_table,
    type_table,
    embed_gain,
    embed_shift,
    qkv_weight,
    qv_bias,
    out_weight,
    out_bias,
    ln1_gain,
    ln1_shift,
    up_weight,
    up_bias,
    down_weight,
    down_bias,
    ln2_gain,
    ln2_shift,
    cotangent,
):
    n_wide, n_narrow = lax.axis_size("wide"), lax.axis_size("narrow")
    half_wide = n_wide // 2
    me_narrow = lax.axis_index("narrow")
    wide_bits, narrow_bits = bits_of("wide"), bits_of("narrow")
    every_bit = narrow_bits + wide_bits
    falling = every_bit[::-1]
    word_total, letters = char_ids.shape
    tap_rows, own_filters = conv_weight.shape
    char_depth = char_table.shape[1]
    tap_count = tap_rows // char_depth
    filters = highway_weight.shape[1]
    own_mix = highway_weight.shape[2]
    own_width = proj_weight.shape[1]
    seq_length = position_table.shape[0]
    group = word_total * n_narrow
    own_hidden = half_wide * own_mix

    conv_block = jnp.zeros((own_filters, LANES), jnp.bfloat16)
    conv_block = conv_block.at[:, :tap_rows].set(conv_weight.T)
    conv_block = conv_block.at[:, tap_rows + tap_count].set(conv_bias)
    bias_block = jnp.pad(highway_bias, ((0, 0), (0, LANES - own_mix)))
    conv_spread = spread(jnp.concatenate([conv_block, bias_block]), falling)
    filt_rows = conv_spread[:, :own_filters].reshape(filters, LANES)
    mix_bias = conv_spread[:, own_filters:, :own_mix].reshape(n_wide, n_narrow, 2, own_mix)
    mix_bias = full(lax.dynamic_index_in_dim(mix_bias, me_narrow, 1, keepdims=False))
    mix_bias = mix_bias.transpose(1, 0, 2).reshape(2, n_wide * own_mix)
    second_rows = (
        highway_weight[1]
        .reshape(half_wide, n_narrow, own_mix, own_mix)
        .transpose(1, 0, 2, 3)
        .reshape(filters, own_mix)
    )
    mix_weights = [
        lax.all_gather(highway_weight[0], "wide", axis=1, tiled=True),
        lax.all_gather(second_rows, "wide", axis=1, tiled=True),
    ]
    vector_block = jnp.stack([proj_bias, type_table[0], type_table[1], embed_gain, embed_shift], axis=1)
    vector_block = jnp.pad(vector_block, ((0, 0), (0, LANES - vector_block.shape[1])))
    rest = spread(jnp.concatenate([proj_weight.T, position_table.T, vector_block], axis=1), falling)
    rest = rest.reshape(n_wide * n_narrow * own_width, -1)
    model_width = rest.shape[0]
    proj_rows = rest[:, :filters].reshape(model_width, half_wide, n_narrow, own_mix)
    proj_own = lax.dynamic_index_in_dim(proj_rows, me_narrow, 2, keepdims=False)
    proj_own = proj_own.reshape(model_width, own_hidden)
    position_rows = rest[:, filters : filters + seq_length]
    vectors = full(rest[:, filters + seq_length :].T)
    proj_shift, type_low, type_high, first_gain, first_shift = (vectors[i] for i in range(5))

    widths = filter_widths(filters)
    lane = jnp.arange(LANES)
    tap_keep = (lane[None, :] // char_depth) < widths[:, None]
    late = lane - tap_rows
    shut = (late == 0)[None, :] | (
        (late >= 1)[None, :] & (late < tap_count)[None, :] & (widths[:, None] > late[None, :])
    )
    is_bias = (late == tap_count)[None, :]
    filt_rows = jnp.where(
        (tap_keep & (late < 0)[None, :]) | is_bias,
        filt_rows,
        jnp.where(shut, jnp.bfloat16(SHUT), jnp.bfloat16(0.0)),
    )
    vocab = char_table.shape[0]
    vocab_rows = -(-vocab // 16) * 16
    id_row = char_ids.T.reshape(1, letters * word_total)
    hot = (jnp.arange(vocab_rows)[:, None] == id_row).astype(jnp.bfloat16)
    table_t = jnp.pad(char_table, ((0, vocab_rows - vocab), (0, 0))).T
    embedded = low(jnp.dot(table_t, hot, preferred_element_type=jnp.float32))
    embedded = jnp.pad(embedded, ((0, 0), (0, tap_count * word_total)))
    span = letters * word_total
    tap_blocks = [embedded[:, t * word_total : t * word_total + span] for t in range(tap_count)]
    place = jnp.arange(letters)
    usable = (char_mask == 1) | (place[None, :] == 0)
    unusable_row = low(~usable).T.reshape(1, span)
    late_rows = low(place[None, :] == letters - jnp.arange(1, tap_count)[:, None])
    late_rows = jnp.repeat(late_rows, word_total, axis=1)
    columns_t = jnp.concatenate(
        tap_blocks
        + [
            unusable_row,
            late_rows,
            jnp.ones((1, span), jnp.bfloat16),
            jnp.zeros((LANES - tap_rows - tap_count - 1, span), jnp.bfloat16),
        ]
    )
    columns = columns_t.T.reshape(letters, word_total, LANES)
    tally = jnp.stack(
        [jnp.sum(full(usable[:, : letters - w + 1]), axis=1) for w in range(1, tap_count + 1)], axis=1
    )
    width_hot = full(jnp.arange(1, tap_count + 1)[:, None] == widths[None, :])
    valid_count = jnp.dot(tally, width_hot)

    lse = pool_forward(columns, filt_rows)
    pooled = lse - jnp.log(valid_count)
    features = low(smooth_gelu(pooled))

    first_low = spread(features, narrow_bits[::-1]).reshape(group, filters)
    first_own = lax.dynamic_index_in_dim(
        first_low.reshape(group, half_wide, n_narrow, own_mix), me_narrow, 2, keepdims=False
    )
    hidden = full(first_own.reshape(group, own_hidden))
    low_input = first_low
    highway_saved = []
    for layer_index in range(2):
        mixture = jnp.dot(low_input, mix_weights[layer_index], preferred_element_type=jnp.float32)
        mixture = mixture + mix_bias[layer_index]
        highway_saved.append((hidden, low_input, mixture))
        hidden = highway_mix(hidden, mixture)
        if layer_index == 0:
            blocks = spread(low(hidden), narrow_bits[::-1])
            low_input = jnp.concatenate([blocks[m] for m in range(n_narrow)], axis=1)
    proj_input = low(hidden)
    projected = fold(dot_nt(proj_input, proj_own).reshape(n_narrow, word_total, model_width), narrow_bits)
    position_hot = (position_ids[:, None] == jnp.arange(seq_length)[None, :]).astype(jnp.bfloat16)
    type_rows = jnp.where(type_ids[:, None] == 1, type_high, type_low)
    summed = projected + proj_shift + dot_nt(position_hot, position_rows) + type_rows
    first_state, first_pull = jax.vjp(layer_norm, summed, first_gain, first_shift)

    gathered = lax.all_gather(low(first_state), "narrow", axis=0, tiled=True)
    group_rows = gathered.shape[0]
    qkv_out = jnp.einsum("gd,kdc->kgc", gathered, qkv_weight, preferred_element_type=jnp.float32)
    local_width = qkv_out.shape[2]
    head_count = local_width // HEAD_DIM
    seq_shape = (group_rows, head_count, HEAD_DIM)
    query_heads = low(qkv_out[0] + full(qv_bias[0])).reshape(seq_shape)
    key_heads = low(qkv_out[1]).reshape(seq_shape)
    value_heads = low(qkv_out[2] + full(qv_bias[1])).reshape(seq_shape)
    score_scale = HEAD_DIM ** (-0.5)
    keep_mask = key_mask[0]
    context, row_peak, row_total = attend(query_heads, key_heads, value_heads, keep_mask, score_scale)
    context_rows = context.reshape(group_rows, local_width)

    def by_owner(partial):
        return fold(partial.reshape(n_narrow, word_total, model_width), narrow_bits)

    attn_branch = by_owner(jnp.dot(context_rows, out_weight, preferred_element_type=jnp.float32))
    attn_branch = attn_branch + full(out_bias)
    second_state, second_pull = jax.vjp(
        layer_norm, first_state + attn_branch, full(ln1_gain), full(ln1_shift)
    )
    ffn_input = lax.all_gather(low(second_state), "narrow", axis=0, tiled=True)
    up_value = jnp.dot(ffn_input, up_weight, preferred_element_type=jnp.float32) + full(up_bias)
    activated = low(smooth_gelu(up_value))
    ffn_branch = by_owner(jnp.dot(activated, down_weight, preferred_element_type=jnp.float32))
    ffn_branch = ffn_branch + full(down_bias)
    layer_out, third_pull = jax.vjp(
        layer_norm, second_state + ffn_branch, full(ln2_gain), full(ln2_shift)
    )

    grad_third, grad_ln2_gain, grad_ln2_shift = third_pull(cotangent)
    grad_ffn = low(grad_third)
    grad_down_bias = jnp.sum(full(grad_ffn), axis=0)
    grad_ffn_rows = lax.all_gather(grad_ffn, "narrow", axis=0, tiled=True)
    grad_down_weight = jnp.einsum(
        "gf,gd->fd", activated, grad_ffn_rows, preferred_element_type=jnp.float32
    )
    grad_active = dot_nt(grad_ffn_rows, down_weight)
    grad_up = low(jax.vjp(smooth_gelu, up_value)[1](grad_active)[0])
    grad_up_bias = jnp.sum(full(grad_up), axis=0)
    grad_up_weight = jnp.einsum("gd,gf->df", ffn_input, grad_up, preferred_element_type=jnp.float32)
    grad_second = grad_third + by_owner(dot_nt(grad_up, up_weight))
    ffn_sums = lax.psum((low(grad_up_weight), low(grad_down_weight)), "wide")
    grad_first_branch, grad_ln1_gain, grad_ln1_shift = second_pull(grad_second)
    grad_attn = low(grad_first_branch)
    grad_out_bias = jnp.sum(full(grad_attn), axis=0)
    grad_attn_rows = lax.all_gather(grad_attn, "narrow", axis=0, tiled=True)
    grad_out_weight = jnp.einsum(
        "gc,gd->cd", context_rows, grad_attn_rows, preferred_element_type=jnp.float32
    )
    grad_context = low(dot_nt(grad_attn_rows, out_weight)).reshape(seq_shape)
    grad_query, grad_key, grad_value = attend_back(
        query_heads, key_heads, value_heads, keep_mask, row_peak, row_total, grad_context, score_scale
    )
    grad_joined = jnp.stack(
        [item.reshape(group_rows, local_width) for item in (grad_query, grad_key, grad_value)]
    )
    grad_qv_bias = jnp.stack(
        [jnp.sum(full(grad_joined[0]), axis=0), jnp.sum(full(grad_joined[2]), axis=0)]
    )
    grad_qkv_weight = jnp.einsum(
        "gd,kgc->kdc", gathered, grad_joined, preferred_element_type=jnp.float32
    )
    attn_sums = lax.psum((low(grad_qkv_weight), low(grad_out_weight)), "wide")
    grad_first = grad_first_branch + by_owner(
        jnp.einsum("kgc,kdc->gd", grad_joined, qkv_weight, preferred_element_type=jnp.float32)
    )
    grad_summed, grad_embed_gain, grad_embed_shift = first_pull(grad_first)

    grad_proj_low = low(grad_summed)
    grad_position = jnp.einsum(
        "td,tl->dl", grad_proj_low, position_hot, preferred_element_type=jnp.float32
    )
    is_high = type_ids[:, None] == 1
    vector_grads = jnp.stack(
        [
            jnp.sum(full(grad_proj_low), axis=0),
            jnp.sum(jnp.where(is_high, 0.0, grad_summed), axis=0),
            jnp.sum(jnp.where(is_high, grad_summed, 0.0), axis=0),
            grad_embed_gain,
            grad_embed_shift,
        ],
        axis=1,
    )
    vector_grads = jnp.pad(vector_grads, ((0, 0), (0, LANES - vector_grads.shape[1])))
    table_grads = jnp.concatenate([grad_position, vector_grads], axis=1)
    table_grads = fold(table_grads.reshape(n_wide * n_narrow, own_width, -1), every_bit)
    grad_proj_rows = lax.all_gather(grad_proj_low, "narrow", axis=0, tiled=True)
    grad_proj_weight = jnp.einsum(
        "gd,gh->dh", grad_proj_rows, proj_input, preferred_element_type=jnp.float32
    )
    grad_proj_weight = fold(
        grad_proj_weight.reshape(n_wide, n_narrow * own_width, own_hidden), wide_bits
    )
    grad_proj_weight = lax.all_to_all(
        low(grad_proj_weight).reshape(n_narrow, own_width, own_hidden), "narrow", 0, 0, tiled=True
    )
    owned_proj = full(
        grad_proj_weight.reshape(n_narrow, own_width, half_wide, own_mix)
        .transpose(2, 0, 3, 1)
        .reshape(filters, own_width)
    )
    grad_hidden = jnp.dot(grad_proj_rows, proj_own, preferred_element_type=jnp.float32)

    owned_highway = [None, None]
    mix_bias_grads = [None, None]
    for layer_index in (1, 0):
        hidden_in, low_input, mixture = highway_saved[layer_index]
        grad_direct, grad_mixture = jax.vjp(highway_mix, hidden_in, mixture)[1](grad_hidden)
        grad_mix_low = low(grad_mixture)
        mix_bias_grads[layer_index] = jnp.sum(full(grad_mix_low), axis=0)
        weight = mix_weights[layer_index]
        if layer_index == 1:
            partial = jnp.einsum(
                "tf,mcf->mtc",
                grad_mix_low,
                weight.reshape(n_narrow, own_hidden, -1),
                preferred_element_type=jnp.float32,
            )
            grad_hidden = grad_direct + fold(partial, narrow_bits)
        else:
            partial = dot_nt(grad_mix_low, weight).reshape(group, half_wide, n_narrow, own_mix)
            mine = (jnp.arange(n_narrow) == me_narrow)[None, None, :, None]
            direct = grad_direct.reshape(group, half_wide, 1, own_mix)
            partial = partial + jnp.where(mine, direct, 0.0)
            grad_features = fold(partial.reshape(n_narrow, word_total, filters), narrow_bits)
        weight_grad = jnp.einsum(
            "tk,twc->wkc",
            low_input,
            grad_mix_low.reshape(group, n_wide, own_mix),
            preferred_element_type=jnp.float32,
        )
        weight_grad = full(lax.psum_scatter(low(weight_grad), "wide", scatter_dimension=0))
        if layer_index == 1:
            weight_grad = (
                weight_grad.reshape(n_narrow, half_wide, own_mix, own_mix)
                .transpose(1, 0, 2, 3)
                .reshape(filters, own_mix)
            )
        owned_highway[layer_index] = weight_grad
    owned_highway = jnp.stack(owned_highway)

    grad_pooled = jax.vjp(smooth_gelu, pooled)[1](grad_features)[0]
    filt_grads, hot_grads = pool_backward(
        columns, columns_t, hot, filt_rows, lse, grad_pooled, char_depth, tap_count
    )
    filt_grads = jnp.where(tap_keep | is_bias, filt_grads, 0.0)
    owned_filt = fold(filt_grads.reshape(n_wide * n_narrow, own_filters, LANES), every_bit)
    owned_conv = owned_filt[:, :tap_rows].T
    owned_conv_bias = owned_filt[:, tap_rows + tap_count]
    grad_table = hot_grads[:vocab, :tap_rows].reshape(vocab, tap_count, char_depth).sum(axis=1)

    mix_bias_grads = jnp.stack(mix_bias_grads).reshape(2, n_wide, own_mix)
    wide_parts = [mix_bias_grads, grad_up_bias, grad_qv_bias]
    all_parts = [
        grad_out_bias,
        grad_ln1_gain,
        grad_ln1_shift,
        grad_down_bias,
        grad_ln2_gain,
        grad_ln2_shift,
        grad_table,
    ]

    def joined(parts):
        flat = jnp.concatenate([item.reshape(-1) for item in parts])
        return jnp.pad(flat, (0, -flat.shape[0] % LANES)).reshape(-1, LANES)

    def parted(flat, parts):
        flat, done, start = flat.reshape(-1), [], 0
        for item in parts:
            done.append(flat[start : start + item.size].reshape(item.shape))
            start += item.size
        return done

    wide_flat, all_flat = joined(wide_parts), joined(all_parts)
    flat = total(jnp.concatenate([wide_flat, all_flat]), wide_bits)
    mix_sums, sum_up_bias, sum_qv_bias = parted(flat[: wide_flat.shape[0]], wide_parts)
    owned_mix_bias = lax.dynamic_index_in_dim(mix_sums, lax.axis_index("wide"), 1, keepdims=False)
    (
        sum_out_bias,
        sum_ln1_gain,
        sum_ln1_shift,
        sum_down_bias,
        sum_ln2_gain,
        sum_ln2_shift,
        sum_table,
    ) = parted(total(flat[wide_flat.shape[0] :], narrow_bits), all_parts)
    owned_vectors = table_grads[:, seq_length : seq_length + 5].T
    return (
        layer_out,
        sum_table,
        owned_conv,
        owned_conv_bias,
        owned_highway,
        owned_mix_bias,
        owned_proj,
        owned_vectors[0],
        table_grads[:, :seq_length].T,
        owned_vectors[1:3],
        owned_vectors[3],
        owned_vectors[4],
        full(attn_sums[0]),
        sum_qv_bias,
        full(attn_sums[1]),
        sum_out_bias,
        sum_ln1_gain,
        sum_ln1_shift,
        full(ffn_sums[0]),
        sum_up_bias,
        full(ffn_sums[1]),
        sum_down_bias,
        sum_ln2_gain,
        sum_ln2_shift,
    )


def solution(mesh):
    return jax.shard_map(
        per_device,
        mesh=mesh,
        in_specs=(
            P(("wide", "narrow"), None),
            P(("wide", "narrow"), None),
            P(("wide", "narrow")),
            P(("wide", "narrow")),
            P("wide", None),
            P(),
            P(None, ("wide", "narrow")),
            P(("wide", "narrow")),
            P(None, None, ("wide", "narrow")),
            P(None, ("wide", "narrow")),
            P(None, ("wide", "narrow")),
            P(("wide", "narrow")),
            P(None, ("wide", "narrow")),
            P(None, ("wide", "narrow")),
            P(("wide", "narrow")),
            P(("wide", "narrow")),
            P(None, None, "narrow"),
            P(None, "narrow"),
            P("narrow", None),
            P(),
            P(),
            P(),
            P(None, "narrow"),
            P("narrow"),
            P("narrow", None),
            P(),
            P(),
            P(),
            P(("wide", "narrow"), None),
        ),
        out_specs=(
            P(("wide", "narrow"), None),
            P(),
            P(None, ("wide", "narrow")),
            P(("wide", "narrow")),
            P(None, None, ("wide", "narrow")),
            P(None, ("wide", "narrow")),
            P(None, ("wide", "narrow")),
            P(("wide", "narrow")),
            P(None, ("wide", "narrow")),
            P(None, ("wide", "narrow")),
            P(("wide", "narrow")),
            P(("wide", "narrow")),
            P(None, None, "narrow"),
            P(None, "narrow"),
            P("narrow", None),
            P(),
            P(),
            P(),
            P(None, "narrow"),
            P("narrow"),
            P("narrow", None),
            P(),
            P(),
            P(),
        ),
        check_vma=False,
    )
```

time: 2180 us -> 651 us (0.30)
  waiting for transfers between devices: 1430 us -> 259 us
  blocking collectives: 296 us -> 41.7 us
  matrix products: 220 us -> 70.9 us
  other arithmetic: 137 us -> 70.8 us
  starting transfers between devices: 0.92 us -> 42 us
  local copies, waits for them, and re-layouts: 63 us -> 102 us
  Pallas kernels: 0 us -> 38.3 us
    reduce_scatter x6 -> x2, waiting for transfers between devices: 930 us -> 109 us  [per_device(): lax.psum_scatter(low(weight_grad), 'wide', scatter_dimension=0)]
    unnamed x15 -> x5, waiting for transfers between devices: 267 us -> 0.08 us
    psum x1, waiting for transfers between devices: 238 us -> 0.01 us  [per_device(): attn_sums = lax.psum((low(grad_qkv_weight), low(grad_out_weight)), 'wide')]
    dot_general x32 -> x20, matrix products: 199 us -> 44.5 us  [the longest x2 10.6 us: per_device(): jnp.einsum('tk,twc->wkc', low_input, grad_mix_low.reshape(group, n_wide,...]
    all_gather x6 -> x3, blocking collectives: 175 us -> 25 us  [the longest x1 8.59 us: per_device(): gathered = lax.all_gather(low(first_state), 'narrow', axis=0, tiled=True)]
    ppermute x0 -> x46, waiting for transfers between devices: none -> 138 us  [swap(): return lax.ppermute(block, axis, [(i, i ^ 1 << bit) for i in range(size)])]
    psum x2 -> x0, blocking collectives: 61.5 us -> none  [the longest x1 39 us: per_device(): lax.psum((grad_table, grad_out_bias, grad_ln1_gain, grad_ln1_shift, grad_...]
    reduce_sum x11 -> x13, other arithmetic: 63.1 us -> 3.58 us  [the longest x2 1.08 us: per_device(): mix_bias_grads[layer_index] = jnp.sum(full(grad_mix_low), axis=0)]
  transfers between devices with their start and end apart: 12 -> 52, of which waited for: 9 -> 31; matrix products, arithmetic and copies ran while one was open for 10% -> 27% of each run, Pallas kernels for 0% -> 6%
where the time goes in v1:
time: 651 us; the launch traced here: 642 us
  waiting for transfers between devices  259 us (40%)
  local copies, waits for them, and re-layouts  102 us (16%)
  matrix products  70.9 us (11%)
  other arithmetic  70.8 us (11%)
  starting transfers between devices  42 us (6%)
  blocking collectives  41.7 us (6%)
  Pallas kernels  38.3 us (6%)
  between operations  16.5 us (3%)
    ppermute x46, waiting for transfers between devices, swap(): return lax.ppermute(block, axis, [(i, i ^ 1 << bit) for i in range(size)])  138 us
    reduce_scatter x2, waiting for transfers between devices, per_device(): lax.psum_scatter(low(weight_grad), 'wide', scatter_dimension=0)  109 us
    ppermute x46, starting transfers between devices, swap(): return lax.ppermute(block, axis, [(i, i ^ 1 << bit) for i in range(size)])  38.3 us
    unnamed x251, local copies, waits for them, and re-layouts  28.3 us
    pallas_call x1, Pallas kernels, pool_backward(): pl.pallas_call(functools.partial(back_kernel, depth=depth, taps=taps), gr...  24.6 us
    pallas_call x1, Pallas kernels, pool_forward(): pl.pallas_call(functools.partial(pool_kernel, group=5), grid=(filters //...  13.8 us
    convert_element_type x13, other arithmetic, full(): return values.astype(jnp.float32)  13.6 us
  transfers between devices with their start and end apart: 52, of which 31 were waited for; matrix products, arithmetic and copies ran while one was open for 27% of the time, Pallas kernels for 6%

profile of v1, /device:TPU:0, one launch (start us, length us, event | category | flops | bytes accessed | tf_op | source)
XLA Modules:
  0.0 641.5 jit_solution(12452871085783484996)
XLA Ops:
  22.4 6.4 concatenate.28.cols_t_ref
  42.0 9.0 %collective-permute-done.10 = bf16[2,24,2688]{2,1,0:T(8,128)(2,1)S(1)} collective-permute-done((bf16[2,24,2688]{2,1,0:T(8,128)(2,1)S(1)}, bf16[2,24,2688]{2,1,0:T(8,128)(2,1)S(1)}, u32[]{:S(2)}, u32[]{:S(2)}) %collective-permute-start.10) | collective-permute-done | bytes 258080 | tf_op jit(solution)/shard_map/ppermute | solution.py:52
  54.1 13.8 %pool_forward.1.lse_ref = f32[128,2048]{1,0:T(8,128)S(1)} custom-call(bf16[50,128,128]{2,1,0:T(8,128)(2,1)S(1)} %bitcast.511, bf16[2048,128]{1,0:T(8,128)(2,1)S(1)} %fusion.65.filt_ref), custom_call_target="tpu_custom_call" | custom-call | flops 3355443200 | bytes 1048576 | tf_op jit(solution)/shard_map/pool_forward/pallas_call | solution.py:116
  73.8 12.4 %collective-permute-done.5 = bf16[1,128,2048]{2,1,0:T(8,128)(2,1)S(1)} collective-permute-done((bf16[1,128,2048]{2,1,0:T(8,128)(2,1)S(1)}, bf16[1,128,2048]{2,1,0:T(8,128)(2,1)S(1)}, u32[]{:S(2)}, u32[]{:S(2)}) %collective-permute-start.5) | collective-permute-done | bytes 524320 | tf_op jit(solution)/shard_map/ppermute | solution.py:52
  86.4 19.7 %collective-permute-done.12 = bf16[8,24,2688]{2,1,0:T(8,128)(2,1)S(1)} collective-permute-done((bf16[8,24,2688]{2,1,0:T(8,128)(2,1)S(1)}, bf16[8,24,2688]{2,1,0:T(8,128)(2,1)S(1)}, u32[]{:S(2)}, u32[]{:S(2)}) %collective-permute-start.12) | collective-permute-done | bytes 1032224 | tf_op jit(solution)/shard_map/ppermute | solution.py:52
  114.5 5.9 convert_reduce_fusion.3
  129.8 14.3 %collective-permute-done.7 = bf16[1,512,512]{2,1,0:T(8,128)(2,1)} collective-permute-done((bf16[1,512,512]{2,1,0:T(8,128)(2,1)}, bf16[1,512,512]{2,1,0:T(8,128)(2,1)}, u32[]{:S(2)}, u32[]{:S(2)}) %collective-permute-start.7) | collective-permute-done | bytes 524320 | tf_op jit(solution)/shard_map/ppermute | solution.py:52
  164.2 10.9 %all-gather.4.cloned.1.call-done = bf16[2048,1024]{1,0:T(8,128)(2,1)} async-done(((bf16[2048,128]{1,0:T(8,128)(2,1)}), bf16[2048,1024]{1,0:T(8,128)(2,1)}) %all-gather.4.cloned.1.call-update) | async-done | bytes 4194320 | tf_op jit(solution)/shard_map/all_gather | solution.py:320
  199.4 8.6 %all_gather.23 = bf16[512,768]{1,0:T(8,128)(2,1)S(1)} all-gather(bf16[128,768]{1,0:T(8,128)(2,1)S(1)} %fusion.88), channel_id=1, replica_groups=mesh['wide'=8,'narrow'=4] {'narrow'}, dimensions={0}, use_global_device_ids=true | all-gather | bytes 983040 | tf_op jit(solution)/shard_map/all_gather | solution.py:403
  221.9 6.3 collective-permute-done.17
  228.8 7.9 %all_gather.24 = bf16[512,768]{1,0:T(8,128)(2,1)S(1)} all-gather(bf16[128,768]{1,0:T(8,128)(2,1)S(1)} %fusion.89), channel_id=1, replica_groups=mesh['wide'=8,'narrow'=4] {'narrow'}, dimensions={0}, use_global_device_ids=true | all-gather | bytes 983040 | tf_op jit(solution)/shard_map/all_gather | solution.py:425
  236.7 10.2 %multiply_convert_fusion.1 = (bf16[512,768]{1,0:T(8,128)(2,1)S(1)}, f32[512,768]{1,0:T(8,128)S(1)}, f32[512,768]{1,0:T(8,128)S(1)}) fusion(f32[768]{0:T(1024)S(1)} %convert_element_type.637, bf16[512,768]{1,0:T(8,128)(2,1)S(1)} %all_gather.24, bf16[768,768]{1,0:T(8,128)(2,1)S(1)} %copy-done), kind=kOutput, calls=%fused_computation.41 | convolution fusion | flops 629932032 | bytes 5901312 | tf_op jit(solution)/shard_map/dot_general | solution.py:426
  251.0 5.9 collective-permute-done.19
  259.8 8.7 %all_gather.25 = bf16[512,768]{1,0:T(8,128)(2,1)S(1)} all-gather(bf16[128,768]{1,0:T(8,128)(2,1)S(1)} %get-tuple-element.235), channel_id=1, replica_groups=mesh['wide'=8,'narrow'=4] {'narrow'}, dimensions={0}, use_global_device_ids=true | all-gather | bytes 983040 | tf_op jit(solution)/shard_map/all_gather | solution.py:437
  282.4 8.0 %all_gather.26 = bf16[512,768]{1,0:T(8,128)(2,1)S(1)} all-gather(bf16[128,768]{1,0:T(8,128)(2,1)S(1)} %get-tuple-element.237), channel_id=1, replica_groups=mesh['wide'=8,'narrow'=4] {'narrow'}, dimensions={0}, use_global_device_ids=true | all-gather | bytes 983040 | tf_op jit(solution)/shard_map/all_gather | solution.py:450
  313.9 8.5 %all_gather.27 = bf16[512,768]{1,0:T(8,128)(2,1)S(1)} all-gather(bf16[128,768]{1,0:T(8,128)(2,1)S(1)} %get-tuple-element.290), channel_id=1, replica_groups=mesh['wide'=8,'narrow'=4] {'narrow'}, dimensions={0}, use_global_device_ids=true | all-gather | bytes 983040 | tf_op jit(solution)/shard_map/all_gather | solution.py:491
  328.3 6.3 convert_bitcast_fusion
  382.0 9.6 %collective-permute-done.25 = bf16[1,512,512]{2,1,0:T(8,128)(2,1)S(1)} collective-permute-done((bf16[1,512,512]{2,1,0:T(8,128)(2,1)S(1)}, bf16[1,512,512]{2,1,0:T(8,128)(2,1)S(1)}, u32[]{:S(2)}, u32[]{:S(2)}) %collective-permute-start.25) | collective-permute-done | bytes 524320 | tf_op jit(solution)/shard_map/ppermute | solution.py:52
  399.9 5.9 broadcast_in_dim.197
  441.1 11.7 %collective-permute-done.27 = bf16[1,128,2048]{2,1,0:T(8,128)(2,1)S(1)} collective-permute-done((bf16[1,128,2048]{2,1,0:T(8,128)(2,1)S(1)}, bf16[1,128,2048]{2,1,0:T(8,128)(2,1)S(1)}, u32[]{:S(2)}, u32[]{:S(2)}) %collective-permute-start.27) | collective-permute-done | bytes 524320 | tf_op jit(solution)/shard_map/ppermute | solution.py:52
  454.0 24.6 %pool_backward.1 = (f32[2048,128]{1,0:T(8,128)S(1)}, f32[272,128]{1,0:T(8,128)S(1)}) custom-call(bf16[50,128,128]{2,1,0:T(8,128)(2,1)S(1)} %bitcast.512, bf16[128,6400]{1,0:T(8,128)(2,1)} %concatenate.28.cols_t_ref, bf16[272,6400]{1,0:T(8,128)(2,1)} %fusion.1.hot_ref, bf16[2048,128]{1,0:T(8,128)(2,1)S(1)} %fusion.65.filt_ref, f32[128,2048]{1,0:T(8,128)S(1)} %copy-done.3, ...), custom_call_target="tpu_custom_call" | custom-call | flops 10066329600 | bytes 2097152 | tf_op jit(solution)/shard_map/pool_backward/pallas_call | solution.py:176
  484.1 5.9 collective-permute-done.29
  519.8 20.3 %reduce-scatter.5.cloned.1.call-done = bf16[1,2048,128]{1,2,0:T(8,128)(2,1)} async-done(((bf16[8,2048,128]{1,2,0:T(8,128)(2,1)}), bf16[1,2048,128]{1,2,0:T(8,128)(2,1)}) %reduce-scatter.5.cloned.1.call-update) | async-done | bytes 524304 | tf_op jit(solution)/shard_map/reduce_scatter | solution.py:536
  542.9 88.4 %reduce-scatter.3.cloned.1.call-done = bf16[1,2048,128]{1,2,0:T(8,128)(2,1)} async-done(((bf16[8,2048,128]{1,2,0:T(8,128)(2,1)}), bf16[1,2048,128]{1,2,0:T(8,128)(2,1)}) %reduce-scatter.3.cloned.1.call-update) | async-done | bytes 524304 | tf_op jit(solution)/shard_map/reduce_scatter | solution.py:536
  (624 shorter events, 296.0 us)
Async XLA Ops:
  7.3 113.0 %all-gather.6.cloned.1.call-start = ((), (), s32[]{:S(2)}) async-start(), calls=%async_computation.6 | async-start | bytes 4718592 | tf_op jit(solution)/shard_map/all_gather | solution.py:319
  9.6 165.6 %all-gather.4.cloned.1.call-start = ((), (), s32[]{:S(2)}) async-start(), calls=%async_computation.3 | async-start | bytes 4718592 | tf_op jit(solution)/shard_map/all_gather | solution.py:320
  17.5 20.6 %collective-permute-start.9 = (bf16[1,24,2688]{2,1,0:T(8,128)(2,1)}, bf16[1,24,2688]{2,1,0:T(8,128)(2,1)S(1)}, u32[]{:S(2)}, u32[]{:S(2)}) collective-permute-start(bf16[1,24,2688]{2,1,0:T(8,128)(2,1)} %fusion.105), channel_id=1, source_target_pairs={{0,16},{4,20},{8,24},{12,28},{16,0},{20,4},{24,8},{28,12},{1,17},{... | collective-permute-start | bytes 387080 | tf_op jit(solution)/shard_map/ppermute | solution.py:52
  18.4 473.1 %all-reduce.13.cloned.1.call-start = ((), (), s32[]{:S(2)}) async-start(), calls=%async_computation.7 | async-start | bytes 7077888 | tf_op jit(solution)/shard_map/psum | solution.py:467
  20.4 11.4 %collective-permute-start.1 = (bf16[2,66,128]{2,1,0:T(8,128)(2,1)S(1)}, bf16[2,66,128]{2,1,0:T(8,128)(2,1)S(1)}, u32[]{:S(2)}, u32[]{:S(2)}) collective-permute-start(bf16[2,66,128]{2,1,0:T(8,128)(2,1)S(1)} %maximum_bitcast_fusion.3), channel_id=1, source_target_pairs={{0,8},{4,12},{8,0},{12,4},{16,24},{20,28},{24,16},{28,20},{1,9},{5... | collective-permute-start | bytes 101384 | tf_op jit(solution)/shard_map/ppermute | solution.py:52
  38.2 12.8 %collective-permute-start.10 = (bf16[2,24,2688]{2,1,0:T(8,128)(2,1)S(1)}, bf16[2,24,2688]{2,1,0:T(8,128)(2,1)S(1)}, u32[]{:S(2)}, u32[]{:S(2)}) collective-permute-start(bf16[2,24,2688]{2,1,0:T(8,128)(2,1)S(1)} %maximum_bitcast_fusion.2), channel_id=1, source_target_pairs={{0,8},{4,12},{8,0},{12,4},{16,24},{20,28},{24,16},{28,20},{1,9},{5... | collective-permute-start | bytes 774152 | tf_op jit(solution)/shard_map/ppermute | solution.py:52
  41.9 10.7 %collective-permute-start.4 = (bf16[16,66,128]{2,0,1:T(8,128)(2,1)S(1)}, bf16[16,66,128]{2,0,1:T(8,128)(2,1)S(1)}, u32[]{:S(2)}, u32[]{:S(2)}) collective-permute-start(bf16[16,66,128]{2,0,1:T(8,128)(2,1)S(1)} %bitcast.555), channel_id=1, source_target_pairs={{0,1},{1,0},{2,3},{3,2},{4,5},{5,4},{6,7},{7,6},{8,9},{9,8},{10,11... | collective-permute-start | bytes 811016 | tf_op jit(solution)/shard_map/ppermute | solution.py:52
  51.1 21.0 %collective-permute-start.11 = (bf16[4,24,2688]{2,1,0:T(8,128)(2,1)S(1)}, bf16[4,24,2688]{2,1,0:T(8,128)(2,1)S(1)}, u32[]{:S(2)}, u32[]{:S(2)}) collective-permute-start(bf16[4,24,2688]{2,1,0:T(8,128)(2,1)S(1)} %bitcast.548), channel_id=1, source_target_pairs={{0,4},{4,0},{8,12},{12,8},{16,20},{20,16},{24,28},{28,24},{1,5},{5... | collective-permute-start | bytes 1548296 | tf_op jit(solution)/shard_map/ppermute | solution.py:52
  71.3 14.9 %collective-permute-start.5 = (bf16[1,128,2048]{2,1,0:T(8,128)(2,1)S(1)}, bf16[1,128,2048]{2,1,0:T(8,128)(2,1)S(1)}, u32[]{:S(2)}, u32[]{:S(2)}) collective-permute-start(bf16[1,128,2048]{2,1,0:T(8,128)(2,1)S(1)} %get-tuple-element.254), channel_id=1, source_target_pairs={{0,2},{1,3},{2,0},{3,1},{4,6},{5,7},{6,4},{7,5},{8,10},{9,11},{10,... | collective-permute-start | bytes 1572872 | tf_op jit(solution)/shard_map/ppermute | solution.py:52
  72.4 33.7 %collective-permute-start.12 = (bf16[8,24,2688]{2,1,0:T(8,128)(2,1)S(1)}, bf16[8,24,2688]{2,1,0:T(8,128)(2,1)S(1)}, u32[]{:S(2)}, u32[]{:S(2)}) collective-permute-start(bf16[8,24,2688]{2,1,0:T(8,128)(2,1)S(1)} %bitcast.532), channel_id=1, source_target_pairs={{0,2},{1,3},{2,0},{3,1},{4,6},{5,7},{6,4},{7,5},{8,10},{9,11},{10,... | collective-permute-start | bytes 3096584 | tf_op jit(solution)/shard_map/ppermute | solution.py:52
  86.4 21.8 %collective-permute-start.6 = (bf16[2,128,2048]{2,1,0:T(8,128)(2,1)S(1)}, bf16[2,128,2048]{2,1,0:T(8,128)(2,1)S(1)}, u32[]{:S(2)}, u32[]{:S(2)}) collective-permute-start(bf16[2,128,2048]{2,1,0:T(8,128)(2,1)S(1)} %maximum_bitcast_fusion), channel_id=1, source_target_pairs={{0,1},{1,0},{2,3},{3,2},{4,5},{5,4},{6,7},{7,6},{8,9},{9,8},{10,11... | collective-permute-start | bytes 3145736 | tf_op jit(solution)/shard_map/ppermute | solution.py:52
  108.1 38.5 %collective-permute-start.13 = (bf16[16,24,2688]{2,1,0:T(8,128)(2,1)}, bf16[16,24,2688]{2,1,0:T(8,128)(2,1)}, u32[]{:S(2)}, u32[]{:S(2)}) collective-permute-start(bf16[16,24,2688]{2,1,0:T(8,128)(2,1)} %bitcast.80), channel_id=1, source_target_pairs={{0,1},{1,0},{2,3},{3,2},{4,5},{5,4},{6,7},{7,6},{8,9},{9,8},{10,11... | collective-permute-start | bytes 6193160 | tf_op jit(solution)/shard_map/ppermute | solution.py:52
  129.4 14.7 %collective-permute-start.7 = (bf16[1,512,512]{2,1,0:T(8,128)(2,1)}, bf16[1,512,512]{2,1,0:T(8,128)(2,1)}, u32[]{:S(2)}, u32[]{:S(2)}) collective-permute-start(bf16[1,512,512]{2,1,0:T(8,128)(2,1)} %get-tuple-element.251), channel_id=1, source_target_pairs={{0,2},{1,3},{2,0},{3,1},{4,6},{5,7},{6,4},{7,5},{8,10},{9,11},{10,... | collective-permute-start | bytes 1572872 | tf_op jit(solution)/shard_map/ppermute | solution.py:52
  146.6 14.3 %collective-permute-start.8 = (bf16[2,512,512]{2,1,0:T(8,128)(2,1)}, bf16[2,512,512]{2,1,0:T(8,128)(2,1)}, u32[]{:S(2)}, u32[]{:S(2)}) collective-permute-start(bf16[2,512,512]{2,1,0:T(8,128)(2,1)} %maximum_bitcast_fusion.1), channel_id=1, source_target_pairs={{0,1},{1,0},{2,3},{3,2},{4,5},{5,4},{6,7},{7,6},{8,9},{9,8},{10,11... | collective-permute-start | bytes 3145736 | tf_op jit(solution)/shard_map/ppermute | solution.py:52
  301.4 238.7 %reduce-scatter.5.cloned.1.call-start = ((), (), s32[]{:S(2)}) async-start(), calls=%async_computation.5 | async-start | bytes 4718592 | tf_op jit(solution)/shard_map/reduce_scatter | solution.py:536
  334.7 296.6 %reduce-scatter.3.cloned.1.call-start = ((), (), s32[]{:S(2)}) async-start(), calls=%async_computation.4 | async-start | bytes 4718592 | tf_op jit(solution)/shard_map/reduce_scatter | solution.py:536
  345.5 23.7 %collective-permute-start.38 = (bf16[4,96,512]{2,1,0:T(8,128)(2,1)}, bf16[4,96,512]{2,1,0:T(8,128)(2,1)}, u32[]{:S(2)}, u32[]{:S(2)}) collective-permute-start(bf16[4,96,512]{2,1,0:T(8,128)(2,1)} %fusion.77), channel_id=1, source_target_pairs={{0,4},{4,0},{8,12},{12,8},{16,20},{20,16},{24,28},{28,24},{1,5},{5... | collective-permute-start | bytes 1179656 | tf_op jit(solution)/shard_map/ppermute | solution.py:52
  359.3 14.1 %collective-permute-start.24 = (bf16[2,512,512]{2,1,0:T(8,128)(2,1)}, bf16[2,512,512]{2,1,0:T(8,128)(2,1)}, u32[]{:S(2)}, u32[]{:S(2)}) collective-permute-start(bf16[2,512,512]{2,1,0:T(8,128)(2,1)} %bitcast.557), channel_id=1, source_target_pairs={{0,1},{1,0},{2,3},{3,2},{4,5},{5,4},{6,7},{7,6},{8,9},{9,8},{10,11... | collective-permute-start | bytes 3145736 | tf_op jit(solution)/shard_map/ppermute | solution.py:52
  375.2 16.3 %collective-permute-start.25 = (bf16[1,512,512]{2,1,0:T(8,128)(2,1)S(1)}, bf16[1,512,512]{2,1,0:T(8,128)(2,1)S(1)}, u32[]{:S(2)}, u32[]{:S(2)}) collective-permute-start(bf16[1,512,512]{2,1,0:T(8,128)(2,1)S(1)} %dynamic-slice_convert_fusion.2), channel_id=1, source_target_pairs={{0,2},{1,3},{2,0},{3,1},{4,6},{5,7},{6,4},{7,5},{8,10},{9,11},{10,... | collective-permute-start | bytes 1572872 | tf_op jit(solution)/shard_map/ppermute | solution.py:52
  378.5 44.5 %collective-permute-start.40 = (bf16[1,96,512]{2,1,0:T(8,128)(2,1)}, bf16[1,96,512]{2,1,0:T(8,128)(2,1)}, u32[]{:S(2)}, u32[]{:S(2)}) collective-permute-start(bf16[1,96,512]{2,1,0:T(8,128)(2,1)} %dynamic-slice_convert_fusion.12), channel_id=1, source_target_pairs={{0,16},{4,20},{8,24},{12,28},{16,0},{20,4},{24,8},{28,12},{1,17},{... | collective-permute-start | bytes 294920 | tf_op jit(solution)/shard_map/ppermute | solution.py:52
  381.4 38.8 %collective-permute-start.43 = (bf16[4,24,640]{2,1,0:T(8,128)(2,1)S(1)}, bf16[4,24,640]{2,1,0:T(8,128)(2,1)S(1)}, u32[]{:S(2)}, u32[]{:S(2)}) collective-permute-start(bf16[4,24,640]{2,1,0:T(8,128)(2,1)S(1)} %fusion.106), channel_id=1, source_target_pairs={{0,4},{4,0},{8,12},{12,8},{16,20},{20,16},{24,28},{28,24},{1,5},{5... | collective-permute-start | bytes 368648 | tf_op jit(solution)/shard_map/ppermute | solution.py:52
  414.9 21.7 %collective-permute-start.26 = (bf16[2,128,2048]{2,1,0:T(8,128)(2,1)}, bf16[2,128,2048]{2,1,0:T(8,128)(2,1)}, u32[]{:S(2)}, u32[]{:S(2)}) collective-permute-start(bf16[2,128,2048]{2,1,0:T(8,128)(2,1)} %fusion.33), channel_id=1, source_target_pairs={{0,1},{1,0},{2,3},{3,2},{4,5},{5,4},{6,7},{7,6},{8,9},{9,8},{10,11... | collective-permute-start | bytes 3145736 | tf_op jit(solution)/shard_map/ppermute | solution.py:52
  439.1 13.7 %collective-permute-start.27 = (bf16[1,128,2048]{2,1,0:T(8,128)(2,1)S(1)}, bf16[1,128,2048]{2,1,0:T(8,128)(2,1)S(1)}, u32[]{:S(2)}, u32[]{:S(2)}) collective-permute-start(bf16[1,128,2048]{2,1,0:T(8,128)(2,1)S(1)} %dynamic-slice_convert_fusion.1), channel_id=1, source_target_pairs={{0,2},{1,3},{2,0},{3,1},{4,6},{5,7},{6,4},{7,5},{8,10},{9,11},{10,... | collective-permute-start | bytes 1572872 | tf_op jit(solution)/shard_map/ppermute | solution.py:52
  484.1 14.3 %collective-permute-start.33 = (bf16[16,64,128]{2,1,0:T(8,128)(2,1)}, bf16[16,64,128]{2,1,0:T(8,128)(2,1)}, u32[]{:S(2)}, u32[]{:S(2)}) collective-permute-start(bf16[16,64,128]{2,1,0:T(8,128)(2,1)} %fusion.92), channel_id=1, source_target_pairs={{0,1},{1,0},{2,3},{3,2},{4,5},{5,4},{6,7},{7,6},{8,9},{9,8},{10,11... | collective-permute-start | bytes 786440 | tf_op jit(solution)/shard_map/ppermute | solution.py:52
  (146 other events, 1322.3 us)
Sparse Core Ops, SparseCore 0:
  10.8 89.1 all-gather.5
  102.0 73.1 all-gather.3
  301.5 144.0 all-reduce.12
  449.5 90.5 reduce-scatter.4
  543.6 87.6 reduce-scatter.2

commit v2 on v1

--- a/solution.py
+++ b/solution.py
@@ -12,6 +12,7 @@
 NEG_FILL = -1000000000.0
 SHUT = -1e30
 LANES = 128
+LIGHT = pl.CostEstimate(flops=1000, bytes_accessed=1000, transcendentals=0)
 
 
 def layer_norm(values, gain, shift):
@@ -40,16 +41,13 @@
     return widths
 
 
-def highway_mix(hidden, mixture):
-    width_half = hidden.shape[1]
-    nonlinear = smooth_gelu(mixture[:, :width_half])
-    opening = jax.nn.sigmoid(mixture[:, width_half:])
-    return opening * hidden + (1.0 - opening) * nonlinear
-
-
 def swap(block, axis, bit):
     size = lax.axis_size(axis)
     return lax.ppermute(block, axis, [(i, i ^ (1 << bit)) for i in range(size)])
+
+
+def after(value, *others):
+    return lax.optimization_barrier((value,) + others)[0]
 
 
 def my_bit(axis, bit):
@@ -71,15 +69,51 @@
     return held
 
 
+def doubled(block, axis, bit, depth):
+    other = swap(block, axis, bit)
+    high = my_bit(axis, bit) == 1
+    return jnp.stack([jnp.where(high, other, block), jnp.where(high, block, other)], axis=depth)
+
+
+def halved(parts, axis, bit):
+    pairs = parts.reshape((-1, 2) + parts.shape[1:])
+    mine = my_bit(axis, bit)
+    kept = lax.dynamic_index_in_dim(pairs, mine, 1, keepdims=False)
+    sent = low(lax.dynamic_index_in_dim(pairs, 1 - mine, 1, keepdims=False))
+    return full(kept) + full(swap(sent, axis, bit))
+
+
 def fold(parts, bits):
-    shape = parts.shape[1:]
     for axis, bit in bits:
-        pairs = parts.reshape((-1, 2) + shape)
-        mine = my_bit(axis, bit)
-        kept = lax.dynamic_index_in_dim(pairs, mine, 1, keepdims=False)
-        sent = low(lax.dynamic_index_in_dim(pairs, 1 - mine, 1, keepdims=False))
-        parts = full(kept) + full(swap(sent, axis, bit))
+        parts = halved(parts, axis, bit)
     return parts[0]
+
+
+def near_parts(block, axis):
+    parts = [block]
+    for bit in reversed(range(lax.axis_size(axis).bit_length() - 1)):
+        parts = [item for part in parts for item in (part, swap(part, axis, bit))]
+    return parts
+
+
+def in_order(parts, axis, dim):
+    mine = lax.axis_index(axis)
+    blocks = []
+    for m in range(len(parts)):
+        held, count = parts, len(parts)
+        for bit in range(count.bit_length() - 1):
+            here = ((mine >> bit) & 1) == ((m >> bit) & 1)
+            held = [jnp.where(here, even, odd) for even, odd in zip(held[::2], held[1::2])]
+        blocks.append(held[0])
+    return jnp.concatenate(blocks, axis=dim)
+
+
+def fold_near(sent, kept, axis):
+    whole = full(kept) + full(swap(sent, axis, 0))
+    for bit in range(1, lax.axis_size(axis).bit_length() - 1):
+        pairs = whole.reshape((-1, 2) + whole.shape[1:])
+        whole = pairs[:, 0] + full(swap(low(pairs[:, 1]), axis, bit))
+    return whole[0]
 
 
 def total(value, bits):
@@ -123,11 +157,7 @@
         out_specs=pl.BlockSpec((words, block), lambda i: (0, i)),
         out_shape=jax.ShapeDtypeStruct((words, filters), jnp.float32),
         compiler_params=pltpu.CompilerParams(vmem_limit_bytes=48 * 2**20),
-        cost_estimate=pl.CostEstimate(
-            flops=2 * letters * words * depth * filters,
-            bytes_accessed=4 * words * filters,
-            transcendentals=letters * words * filters,
-        ),
+        cost_estimate=LIGHT,
         name="pool_forward",
     )(columns, filt_rows)
 
@@ -194,13 +224,344 @@
         ],
         scratch_shapes=[pltpu.VMEM((letters * words, lanes), jnp.float32)],
         compiler_params=pltpu.CompilerParams(vmem_limit_bytes=48 * 2**20),
-        cost_estimate=pl.CostEstimate(
-            flops=6 * letters * words * lanes * filters,
-            bytes_accessed=8 * words * filters,
-            transcendentals=letters * words * filters,
-        ),
+        cost_estimate=LIGHT,
         name="pool_backward",
     )(columns, columns_t, hot, filt_rows, lse, grad)
+
+
+def gelu_parts(values):
+    spread_part = 0.5 * (1.0 + lax.erf(values * 0.7071067811865476))
+    return spread_part, values * spread_part
+
+
+def opening_of(values):
+    return 1.0 / (1.0 + jnp.exp(-values))
+
+
+def mix_kernel(place_ref, *refs, parts, by_rows, plain, tile):
+    part_refs = refs[:parts]
+    weight_a, weight_t, bias_ref, joined_ref, hidden_ref, a_ref, t_ref = refs[parts:]
+    half, column = pl.program_id(0), pl.program_id(1)
+    mine, pair = place_ref[0], place_ref[1]
+
+    @pl.when((half == 0) & (column == 0))
+    def _():
+        for k, part in enumerate(part_refs):
+            extent = part.shape[0 if by_rows else 1]
+            at = pl.ds(pl.multiple_of((mine ^ k) * extent, extent), extent)
+            if by_rows:
+                joined_ref[at, :] = part[...]
+            else:
+                joined_ref[:, at] = part[...]
+
+    columns = pl.num_programs(1)
+    if plain:
+        first = ((column * 2 + (pair ^ half)) * parts + mine) * tile
+    else:
+        first = ((mine * 2 + (pair ^ half)) * columns + column) * tile
+
+    weight = jnp.concatenate([weight_a[0], weight_t[0]], axis=1)
+    mixture = jnp.dot(joined_ref[...], weight, preferred_element_type=jnp.float32)
+    a = mixture[:, :tile] + bias_ref[0, 0:1, :]
+    t = mixture[:, tile:] + bias_ref[0, 1:2, :]
+    skip = full(joined_ref[:, pl.ds(pl.multiple_of(first, tile), tile)])
+    opening = opening_of(t)
+    hidden_ref[...] = low(opening * skip + (1.0 - opening) * gelu_parts(a)[1])
+    a_ref[...] = a
+    t_ref[...] = t
+
+
+def mix_forward(place, parts, weights, bias, by_rows, plain):
+    blocks, depth, tile = weights.shape
+    columns = blocks // 4
+    piece = columns * tile
+    rows = sum(p.shape[0] for p in parts) if by_rows else parts[0].shape[0]
+
+    def weight_spec(gate):
+        return pl.BlockSpec(
+            (1, depth, tile),
+            lambda half, column, place: (2 * (column + gate * columns) + (place[1] ^ half), 0, 0),
+        )
+
+    def placed(half, column, place):
+        return (0, (place[1] ^ half) * columns + column)
+
+    out_block = pl.BlockSpec((rows, tile), placed)
+    whole = lambda item: pl.BlockSpec(item.shape, lambda half, column, place: (0,) * item.ndim)
+    return pl.pallas_call(
+        functools.partial(mix_kernel, parts=len(parts), by_rows=by_rows, plain=plain, tile=tile),
+        grid_spec=pltpu.PrefetchScalarGridSpec(
+            num_scalar_prefetch=1,
+            grid=(2, columns),
+            in_specs=[whole(p) for p in parts]
+            + [weight_spec(0), weight_spec(1)]
+            + [pl.BlockSpec((1, 2, tile), lambda half, column, place: (half, 0, column))],
+            out_specs=[
+                pl.BlockSpec((rows, depth), lambda half, column, place: (0, 0)),
+                out_block,
+                out_block,
+                out_block,
+            ],
+        ),
+        out_shape=[
+            jax.ShapeDtypeStruct((rows, depth), jnp.bfloat16),
+            jax.ShapeDtypeStruct((rows, 2 * piece), jnp.bfloat16),
+            jax.ShapeDtypeStruct((rows, 2 * piece), jnp.float32),
+            jax.ShapeDtypeStruct((rows, 2 * piece), jnp.float32),
+        ],
+        compiler_params=pltpu.CompilerParams(vmem_limit_bytes=40 * 2**20),
+        cost_estimate=LIGHT,
+        name="mix_forward",
+    )(place, *parts, weights, weights, bias)
+
+
+def mix_back_kernel(place_ref, grad_ref, a_ref, t_ref, *refs):
+    mixed_ref, direct_ref, sums_ref = refs[-3:]
+    grad = grad_ref[...]
+    a = a_ref[...]
+    piece = a.shape[1]
+    skip = full(jnp.concatenate([ref[...] for ref in refs[:-3]], axis=1))
+    opening = opening_of(t_ref[...])
+    phi, bent = gelu_parts(a)
+    slope = phi + a * (0.3989422804014327 * jnp.exp(-0.5 * a * a))
+    grad_a = low((1.0 - opening) * slope * grad)
+    grad_t = low((skip - bent) * opening * (1.0 - opening) * grad)
+    mixed_ref[0, :, :piece] = grad_a
+    mixed_ref[0, :, piece:] = grad_t
+    direct_ref[...] = opening * grad
+    sums_ref[0, :, :piece] = jnp.sum(full(grad_a), axis=0, keepdims=True)
+    sums_ref[0, :, piece:] = jnp.sum(full(grad_t), axis=0, keepdims=True)
+
+
+def mix_back(place, grad, a, t, joined, parts, plain, tile=LANES):
+    rows, own = grad.shape
+    piece = own // 2
+    placed = pl.BlockSpec((rows, piece), lambda half, place: (0, place[1] ^ half))
+    if plain:
+        skips = [
+            pl.BlockSpec((rows, tile), lambda half, place, z=z: (0, (z * 2 + (place[1] ^ half)) * parts + place[0]))
+            for z in range(piece // tile)
+        ]
+    else:
+        skips = [pl.BlockSpec((rows, piece), lambda half, place: (0, place[0] * 2 + (place[1] ^ half)))]
+    return pl.pallas_call(
+        mix_back_kernel,
+        grid_spec=pltpu.PrefetchScalarGridSpec(
+            num_scalar_prefetch=1,
+            grid=(2,),
+            in_specs=[placed, placed, placed] + skips,
+            out_specs=[
+                pl.BlockSpec((1, rows, own), lambda half, place: (half, 0, 0)),
+                placed,
+                pl.BlockSpec((1, 1, own), lambda half, place: (half, 0, 0)),
+            ],
+        ),
+        out_shape=[
+            jax.ShapeDtypeStruct((2, rows, own), jnp.bfloat16),
+            jax.ShapeDtypeStruct((rows, own), jnp.float32),
+            jax.ShapeDtypeStruct((2, 1, own), jnp.float32),
+        ],
+        compiler_params=pltpu.CompilerParams(vmem_limit_bytes=40 * 2**20),
+        cost_estimate=LIGHT,
+        name="mix_backward",
+    )(place, grad, a, t, *[joined] * len(skips))
+
+
+def inner_product(mixed_ref, weight_refs):
+    blocks = len(weight_refs) // 2
+    own = jnp.concatenate([ref[0] for ref in weight_refs[:blocks]], axis=1)
+    other = jnp.concatenate([ref[0] for ref in weight_refs[blocks:]], axis=1)
+    return dot_nt(mixed_ref[0], own) + dot_nt(mixed_ref[1], other)
+
+
+def inner_specs(blocks, depth, tile, row_block):
+    specs = []
+    for flip in (0, 1):
+        for z in range(blocks):
+            specs.append(
+                pl.BlockSpec(
+                    (1, depth, tile),
+                    lambda i, place, z=z, flip=flip: (2 * z + (place[1] ^ flip), row_block(i, place), 0),
+                )
+            )
+    return specs
+
+
+def inner_columns_kernel(place_ref, mixed_ref, *refs):
+    out_ref = refs[-1]
+    out_ref[0] = inner_product(mixed_ref, refs[:-1]).astype(out_ref.dtype)
+
+
+def inner_columns(place, mixed, weights, odd, parts, dtype):
+    _, rows, wide_columns = mixed.shape
+    blocks, filters, tile = weights.shape
+    blocks = blocks // 2
+    depth = filters // parts
+    return pl.pallas_call(
+        inner_columns_kernel,
+        grid_spec=pltpu.PrefetchScalarGridSpec(
+            num_scalar_prefetch=1,
+            grid=(parts // 2,),
+            in_specs=[pl.BlockSpec(mixed.shape, lambda i, place: (0, 0, 0))]
+            + inner_specs(blocks, depth, tile, lambda i, place: place[0] ^ (2 * i + odd)),
+            out_specs=pl.BlockSpec((1, rows, depth), lambda i, place: (i, 0, 0)),
+        ),
+        out_shape=jax.ShapeDtypeStruct((parts // 2, rows, depth), dtype),
+        compiler_params=pltpu.CompilerParams(vmem_limit_bytes=40 * 2**20),
+        cost_estimate=LIGHT,
+        name="inner_columns",
+    )(place, mixed, *[weights] * (2 * blocks))
+
+
+def inner_rows_kernel(place_ref, mixed_ref, *refs, parts, plain, tile):
+    direct_ref, sent_ref, kept_ref, held_ref = refs[-4:]
+    mine = place_ref[0]
+    held_ref[...] = inner_product(mixed_ref, refs[:-4])
+
+    step = pl.program_id(0)
+    if plain:
+        at = pl.ds(pl.multiple_of(mine * tile, tile), tile)
+        column = (step % 2) * (pl.num_programs(0) // 2) + step // 2
+        held_ref[:, at] += direct_ref[:, pl.ds(pl.multiple_of(column * tile, tile), tile)]
+    else:
+
+        @pl.when(step == mine)
+        def _():
+            held_ref[...] += direct_ref[...]
+
+    extent = held_ref.shape[0] // parts
+    for k in range(parts):
+        got = held_ref[pl.ds(pl.multiple_of((mine ^ k) * extent, extent), extent), :]
+        if k % 2:
+            sent_ref[k // 2] = low(got)
+        else:
+            kept_ref[k // 2] = got
+
+
+def inner_rows(place, mixed, weights, direct, parts, plain):
+    _, rows, wide_columns = mixed.shape
+    blocks, filters, tile = weights.shape
+    blocks = blocks // 2
+    depth = filters // parts
+    extent = rows // parts
+    out = pl.BlockSpec((parts // 2, extent, depth), lambda j, place: (0, 0, j))
+    return pl.pallas_call(
+        functools.partial(inner_rows_kernel, parts=parts, plain=plain, tile=tile),
+        grid_spec=pltpu.PrefetchScalarGridSpec(
+            num_scalar_prefetch=1,
+            grid=(parts,),
+            in_specs=[pl.BlockSpec(mixed.shape, lambda j, place: (0, 0, 0))]
+            + inner_specs(blocks, depth, tile, lambda j, place: j)
+            + [pl.BlockSpec(direct.shape, lambda j, place: (0, 0))],
+            out_specs=[out, out],
+            scratch_shapes=[pltpu.VMEM((rows, depth), jnp.float32)],
+        ),
+        out_shape=[
+            jax.ShapeDtypeStruct((parts // 2, extent, filters), jnp.bfloat16),
+            jax.ShapeDtypeStruct((parts // 2, extent, filters), jnp.float32),
+        ],
+        compiler_params=pltpu.CompilerParams(vmem_limit_bytes=40 * 2**20),
+        cost_estimate=LIGHT,
+        name="inner_rows",
+    )(place, mixed, *[weights] * (2 * blocks), direct)
+
+
+def slope_of(values):
+    phi = 0.5 * (1.0 + lax.erf(values * 0.7071067811865476))
+    return phi + values * (0.3989422804014327 * jnp.exp(-0.5 * values * values))
+
+
+def ffn_forward_kernel(x_ref, *refs, tile):
+    out_ref, own_ref = refs[-2:]
+    step = pl.program_id(0)
+    for k, (up_ref, down_ref, bias_ref) in enumerate(zip(refs[:-2:3], refs[1:-2:3], refs[2:-2:3])):
+
+        @pl.when(step == k)
+        def _(k=k, up_ref=up_ref, down_ref=down_ref, bias_ref=bias_ref):
+            for first in range(0, x_ref.shape[0], tile):
+                at = slice(first, first + tile)
+                value = jnp.dot(x_ref[at, :], up_ref[...], preferred_element_type=jnp.float32)
+                active = low(gelu_parts(value + full(bias_ref[0:1, :]))[1])
+                added = jnp.dot(active, down_ref[...], preferred_element_type=jnp.float32)
+                if k == 0:
+                    out_ref[at, :] = added
+                    own_ref[at, :] = active
+                else:
+                    out_ref[at, :] += added
+
+
+def ffn_operands(parts, units):
+    width = parts[0].shape[1]
+    last = (parts[0].shape[0] - 16) // 16
+    specs = [
+        pl.BlockSpec((units, width), lambda k: (0, 0)),
+        pl.BlockSpec((units, width), lambda k: (1, 0)),
+        pl.BlockSpec((16, width), lambda k: (last, 0)),
+    ]
+    return specs * len(parts), [part for part in parts for _ in range(3)]
+
+
+def ffn_forward(x, parts, units, tile=256):
+    rows, width = x.shape
+    whole = lambda shape: pl.BlockSpec(shape, lambda k: (0,) * len(shape))
+    specs, operands = ffn_operands(parts, units)
+    return pl.pallas_call(
+        functools.partial(ffn_forward_kernel, tile=tile),
+        grid=(len(parts),),
+        in_specs=[whole(x.shape)] + specs,
+        out_specs=[whole((rows, width)), whole((rows, units))],
+        out_shape=[
+            jax.ShapeDtypeStruct((rows, width), jnp.float32),
+            jax.ShapeDtypeStruct((rows, units), jnp.bfloat16),
+        ],
+        compiler_params=pltpu.CompilerParams(vmem_limit_bytes=48 * 2**20),
+        cost_estimate=LIGHT,
+        name="ffn_forward",
+    )(x, *operands)
+
+
+def ffn_backward_kernel(x_ref, grad_ref, *refs, tile):
+    out_ref, own_ref, sums_ref = refs[-3:]
+    step = pl.program_id(0)
+    for k, (up_ref, down_ref, bias_ref) in enumerate(zip(refs[:-3:3], refs[1:-3:3], refs[2:-3:3])):
+
+        @pl.when(step == k)
+        def _(k=k, up_ref=up_ref, down_ref=down_ref, bias_ref=bias_ref):
+            sums = jnp.zeros(sums_ref.shape, jnp.float32)
+            for first in range(0, x_ref.shape[0], tile):
+                at = slice(first, first + tile)
+                value = jnp.dot(x_ref[at, :], up_ref[...], preferred_element_type=jnp.float32)
+                value = value + full(bias_ref[0:1, :])
+                inner = low(dot_nt(grad_ref[at, :], down_ref[...]) * slope_of(value))
+                added = dot_nt(inner, up_ref[...])
+                if k == 0:
+                    out_ref[at, :] = added
+                    own_ref[at, :] = inner
+                    sums = sums + jnp.sum(full(inner), axis=0, keepdims=True)
+                else:
+                    out_ref[at, :] += added
+            if k == 0:
+                sums_ref[...] = sums
+
+
+def ffn_backward(x, parts, units, grad, tile=256):
+    rows, width = x.shape
+    whole = lambda shape: pl.BlockSpec(shape, lambda k: (0,) * len(shape))
+    specs, operands = ffn_operands(parts, units)
+    return pl.pallas_call(
+        functools.partial(ffn_backward_kernel, tile=tile),
+        grid=(len(parts),),
+        in_specs=[whole(x.shape), whole(grad.shape)] + specs,
+        out_specs=[whole((rows, width)), whole((rows, units)), whole((1, units))],
+        out_shape=[
+            jax.ShapeDtypeStruct((rows, width), jnp.float32),
+            jax.ShapeDtypeStruct((rows, units), jnp.bfloat16),
+            jax.ShapeDtypeStruct((1, units), jnp.float32),
+        ],
+        compiler_params=pltpu.CompilerParams(vmem_limit_bytes=48 * 2**20),
+        cost_estimate=LIGHT,
+        name="ffn_backward",
+    )(x, grad, *operands)
 
 
 def masked_scores(query_heads, key_heads, keep_mask, score_scale):
@@ -300,38 +661,49 @@
     group = word_total * n_narrow
     own_hidden = half_wide * own_mix
 
+    outer = n_wide // 2
+    quarter = outer // 2
+    outer_groups = [[2 * z + y for z in range(outer)] for y in range(2)]
+    me_pair = my_bit("wide", 0)
+
+    def grouped(item):
+        split = item.reshape((quarter, 2, n_narrow, own_mix) + item.shape[1:])
+        return split.transpose((2, 1, 0, 3) + tuple(range(4, split.ndim))).reshape(item.shape)
+
+    def ungrouped(item):
+        split = item.reshape((n_narrow, 2, quarter, own_mix) + item.shape[1:])
+        return split.transpose((2, 1, 0, 3) + tuple(range(4, split.ndim))).reshape(item.shape)
+
+    tiled = own_mix == LANES
+    corner = jnp.stack([me_narrow, me_pair]).astype(jnp.int32)
+
+    def gather_mix(shard):
+        blocks = lax.all_gather(shard, "wide", axis=0)
+        if tiled:
+            return blocks
+        blocks = blocks.reshape(-1, LANES // own_mix, 2, filters, own_mix).transpose(0, 2, 3, 1, 4)
+        return blocks.reshape(-1, filters, LANES)
+
+    plain = tiled and half_wide == n_narrow
+    ordered, unordered = (lambda item: item, lambda item: item) if plain else (grouped, ungrouped)
+    mix_weights = [gather_mix(ordered(highway_weight[0]))]
+    mix_weights.append(gather_mix(after(grouped(highway_weight[1]), mix_weights[0])))
     conv_block = jnp.zeros((own_filters, LANES), jnp.bfloat16)
     conv_block = conv_block.at[:, :tap_rows].set(conv_weight.T)
     conv_block = conv_block.at[:, tap_rows + tap_count].set(conv_bias)
     bias_block = jnp.pad(highway_bias, ((0, 0), (0, LANES - own_mix)))
     conv_spread = spread(jnp.concatenate([conv_block, bias_block]), falling)
-    filt_rows = conv_spread[:, :own_filters].reshape(filters, LANES)
-    mix_bias = conv_spread[:, own_filters:, :own_mix].reshape(n_wide, n_narrow, 2, own_mix)
-    mix_bias = full(lax.dynamic_index_in_dim(mix_bias, me_narrow, 1, keepdims=False))
-    mix_bias = mix_bias.transpose(1, 0, 2).reshape(2, n_wide * own_mix)
-    second_rows = (
-        highway_weight[1]
-        .reshape(half_wide, n_narrow, own_mix, own_mix)
-        .transpose(1, 0, 2, 3)
-        .reshape(filters, own_mix)
-    )
-    mix_weights = [
-        lax.all_gather(highway_weight[0], "wide", axis=1, tiled=True),
-        lax.all_gather(second_rows, "wide", axis=1, tiled=True),
-    ]
+    filt_rows = ordered(conv_spread[:, :own_filters].reshape(filters, LANES))
+    mix_bias = conv_spread[:, own_filters:, :own_mix].reshape(outer, 2, n_narrow, 2, own_mix)
+    mix_bias = full(lax.dynamic_index_in_dim(mix_bias, me_narrow, 2, keepdims=False))
+    mix_bias = [lax.dynamic_index_in_dim(mix_bias, me_pair ^ half, 1, keepdims=False) for half in range(2)]
+    mix_bias = jnp.stack(mix_bias).transpose(2, 0, 1, 3).reshape(2, 2, 2, quarter * own_mix)
     vector_block = jnp.stack([proj_bias, type_table[0], type_table[1], embed_gain, embed_shift], axis=1)
     vector_block = jnp.pad(vector_block, ((0, 0), (0, LANES - vector_block.shape[1])))
-    rest = spread(jnp.concatenate([proj_weight.T, position_table.T, vector_block], axis=1), falling)
-    rest = rest.reshape(n_wide * n_narrow * own_width, -1)
-    model_width = rest.shape[0]
-    proj_rows = rest[:, :filters].reshape(model_width, half_wide, n_narrow, own_mix)
-    proj_own = lax.dynamic_index_in_dim(proj_rows, me_narrow, 2, keepdims=False)
-    proj_own = proj_own.reshape(model_width, own_hidden)
-    position_rows = rest[:, filters : filters + seq_length]
-    vectors = full(rest[:, filters + seq_length :].T)
-    proj_shift, type_low, type_high, first_gain, first_shift = (vectors[i] for i in range(5))
-
-    widths = filter_widths(filters)
+    rest = jnp.concatenate([grouped(proj_weight).T, position_table.T, vector_block], axis=1)[None]
+    rest_bits = wide_bits[::-1]
+    rest = doubled(rest, *rest_bits[0], 1).reshape((-1,) + rest.shape[1:])
+    widths = ordered(filter_widths(filters))
     lane = jnp.arange(LANES)
     tap_keep = (lane[None, :] // char_depth) < widths[:, None]
     late = lane - tap_rows
@@ -374,27 +746,66 @@
     width_hot = full(jnp.arange(1, tap_count + 1)[:, None] == widths[None, :])
     valid_count = jnp.dot(tally, width_hot)
 
+    def rest_step(rest, which):
+        return doubled(rest, *which, 1).reshape((-1,) + rest.shape[1:])
+
+    rest = after(rest, conv_spread)
+    for which in rest_bits[1:-1]:
+        rest = rest_step(rest, which)
+    units = up_weight.shape[1]
+    encoder_pack = jnp.concatenate(
+        [up_weight, down_weight, out_weight, jnp.broadcast_to(up_bias[None], (16, units))]
+    )
+    encoder_parts = [encoder_pack, swap(encoder_pack, "narrow", 1)]
+    filt_rows, encoder_parts = lax.optimization_barrier((filt_rows, encoder_parts))
     lse = pool_forward(columns, filt_rows)
+    rest = rest_step(after(rest, lse), rest_bits[-1])
     pooled = lse - jnp.log(valid_count)
     features = low(smooth_gelu(pooled))
 
-    first_low = spread(features, narrow_bits[::-1]).reshape(group, filters)
-    first_own = lax.dynamic_index_in_dim(
-        first_low.reshape(group, half_wide, n_narrow, own_mix), me_narrow, 2, keepdims=False
-    )
-    hidden = full(first_own.reshape(group, own_hidden))
-    low_input = first_low
-    highway_saved = []
+    parts = near_parts(features, "narrow")
+    near_order = [0, 2, 1, 3]
+    cotangent_rows = lax.all_gather(
+        after(cotangent, mix_weights[1]), "narrow", axis=0, tiled=True
+    )
+    rest = after(rest, parts[-1])
+
+    def narrowed(rest, bit):
+        width = own_hidden << bit
+        mine = my_bit("narrow", bit)
+        tail = rest[..., 2 * width :]
+        kept = lax.dynamic_slice_in_dim(rest, mine * width, width, rest.ndim - 1)
+        sent = lax.dynamic_slice_in_dim(rest, (1 - mine) * width, width, rest.ndim - 1)
+        kept, sent = (jnp.concatenate([item, tail], axis=-1) for item in (kept, sent))
+        got = swap(sent, "narrow", bit)
+        high = mine == 1
+        pair = jnp.stack([jnp.where(high, got, kept), jnp.where(high, kept, got)], axis=1)
+        return pair.reshape((-1,) + pair.shape[2:])
+
+    rest = narrowed(rest, 1)
+    highway_saved, pair_parts = [], [swap(features, "wide", 0)]
     for layer_index in range(2):
-        mixture = jnp.dot(low_input, mix_weights[layer_index], preferred_element_type=jnp.float32)
-        mixture = mixture + mix_bias[layer_index]
-        highway_saved.append((hidden, low_input, mixture))
-        hidden = highway_mix(hidden, mixture)
+        joined, hidden, kept_a, kept_t = mix_forward(
+            corner, parts, mix_weights[layer_index], mix_bias[layer_index], layer_index == 0, plain and layer_index == 0
+        )
+        highway_saved.append((joined, kept_a, kept_t))
         if layer_index == 0:
-            blocks = spread(low(hidden), narrow_bits[::-1])
-            low_input = jnp.concatenate([blocks[m] for m in range(n_narrow)], axis=1)
-    proj_input = low(hidden)
+            parts = near_parts(hidden, "narrow")
+            pair_parts.append(swap(hidden, "wide", 0))
+            rest = narrowed(after(rest, hidden), 0)
+            encoder_parts = encoder_parts + [
+                swap(item, "narrow", 0) for item in after(encoder_parts, hidden)
+            ]
+            parts, encoder_parts = lax.optimization_barrier((parts, encoder_parts))
+    rest, proj_input = lax.optimization_barrier((rest, hidden))
+    rest = rest.reshape(n_wide * n_narrow * own_width, -1)
+    model_width = rest.shape[0]
+    proj_own = rest[:, :own_hidden]
+    position_rows = rest[:, own_hidden : own_hidden + seq_length]
+    vectors = full(rest[:, own_hidden + seq_length :].T)
+    proj_shift, type_low, type_high, first_gain, first_shift = (vectors[i] for i in range(5))
     projected = fold(dot_nt(proj_input, proj_own).reshape(n_narrow, word_total, model_width), narrow_bits)
+    projected, cotangent_rows = lax.optimization_barrier((projected, cotangent_rows))
     position_hot = (position_ids[:, None] == jnp.arange(seq_length)[None, :]).astype(jnp.bfloat16)
     type_rows = jnp.where(type_ids[:, None] == 1, type_high, type_low)
     summed = projected + proj_shift + dot_nt(position_hot, position_rows) + type_rows
@@ -417,37 +828,48 @@
     def by_owner(partial):
         return fold(partial.reshape(n_narrow, word_total, model_width), narrow_bits)
 
-    attn_branch = by_owner(jnp.dot(context_rows, out_weight, preferred_element_type=jnp.float32))
-    attn_branch = attn_branch + full(out_bias)
+    def own_words(rows):
+        return lax.dynamic_slice_in_dim(rows, me_narrow * word_total, word_total, 0)
+
+    attn_branch = full(out_bias)
+    for k, part in zip(near_order, near_parts(context_rows, "narrow")):
+        weight = encoder_parts[k][2 * units : 2 * units + local_width]
+        attn_branch = attn_branch + jnp.dot(part, weight, preferred_element_type=jnp.float32)
     second_state, second_pull = jax.vjp(
-        layer_norm, first_state + attn_branch, full(ln1_gain), full(ln1_shift)
-    )
-    ffn_input = lax.all_gather(low(second_state), "narrow", axis=0, tiled=True)
-    up_value = jnp.dot(ffn_input, up_weight, preferred_element_type=jnp.float32) + full(up_bias)
-    activated = low(smooth_gelu(up_value))
-    ffn_branch = by_owner(jnp.dot(activated, down_weight, preferred_element_type=jnp.float32))
-    ffn_branch = ffn_branch + full(down_bias)
+        layer_norm, full(gathered) + attn_branch, full(ln1_gain), full(ln1_shift)
+    )
+    pair_parts, ffn_input = lax.optimization_barrier((pair_parts, low(second_state)))
+    ffn_branch, activated = ffn_forward(ffn_input, encoder_parts, units)
     layer_out, third_pull = jax.vjp(
-        layer_norm, second_state + ffn_branch, full(ln2_gain), full(ln2_shift)
-    )
-
-    grad_third, grad_ln2_gain, grad_ln2_shift = third_pull(cotangent)
+        layer_norm, second_state + (ffn_branch + full(down_bias)), full(ln2_gain), full(ln2_shift)
+    )
+    layer_out = own_words(layer_out)
+
+    def pair_start(halves):
+        kept = lax.dynamic_index_in_dim(halves, me_pair, 0, keepdims=False)
+        sent = lax.dynamic_index_in_dim(halves, 1 - me_pair, 0, keepdims=False)
+        return kept, swap(sent, "wide", 0)
+
+    def pair_end(mine, back):
+        first = me_pair == 0
+        return jnp.stack([full(jnp.where(first, mine, back)), full(jnp.where(first, back, mine))])
+
+    grad_third, grad_ln2_gain, grad_ln2_shift = third_pull(cotangent_rows)
     grad_ffn = low(grad_third)
     grad_down_bias = jnp.sum(full(grad_ffn), axis=0)
-    grad_ffn_rows = lax.all_gather(grad_ffn, "narrow", axis=0, tiled=True)
-    grad_down_weight = jnp.einsum(
-        "gf,gd->fd", activated, grad_ffn_rows, preferred_element_type=jnp.float32
-    )
-    grad_active = dot_nt(grad_ffn_rows, down_weight)
-    grad_up = low(jax.vjp(smooth_gelu, up_value)[1](grad_active)[0])
-    grad_up_bias = jnp.sum(full(grad_up), axis=0)
+    grad_down_weight = jnp.einsum("gf,gd->fd", activated, grad_ffn, preferred_element_type=jnp.float32)
+    grad_inner, grad_up, grad_up_bias = ffn_backward(ffn_input, encoder_parts, units, grad_ffn)
     grad_up_weight = jnp.einsum("gd,gf->df", ffn_input, grad_up, preferred_element_type=jnp.float32)
-    grad_second = grad_third + by_owner(dot_nt(grad_up, up_weight))
-    ffn_sums = lax.psum((low(grad_up_weight), low(grad_down_weight)), "wide")
+    grad_second = grad_third + grad_inner
+    ffn_kept, ffn_received = pair_start(jnp.stack([low(grad_up_weight), low(grad_down_weight)]))
     grad_first_branch, grad_ln1_gain, grad_ln1_shift = second_pull(grad_second)
-    grad_attn = low(grad_first_branch)
+    pair_parts = [near_parts(after(item, ffn_branch), "narrow") for item in pair_parts]
+    pair_parts, grad_attn = lax.optimization_barrier((pair_parts, low(grad_first_branch)))
+    pair_joined = [
+        in_order(item, "narrow", layer_index) for layer_index, item in enumerate(pair_parts)
+    ]
     grad_out_bias = jnp.sum(full(grad_attn), axis=0)
-    grad_attn_rows = lax.all_gather(grad_attn, "narrow", axis=0, tiled=True)
+    grad_attn_rows = grad_attn
     grad_out_weight = jnp.einsum(
         "gc,gd->cd", context_rows, grad_attn_rows, preferred_element_type=jnp.float32
     )
@@ -462,10 +884,12 @@
         [jnp.sum(full(grad_joined[0]), axis=0), jnp.sum(full(grad_joined[2]), axis=0)]
     )
     grad_qkv_weight = jnp.einsum(
-        "gd,kgc->kdc", gathered, grad_joined, preferred_element_type=jnp.float32
-    )
-    attn_sums = lax.psum((low(grad_qkv_weight), low(grad_out_weight)), "wide")
-    grad_first = grad_first_branch + by_owner(
+        "kgc,gd->kcd", grad_joined, gathered, preferred_element_type=jnp.float32
+    )
+    attn_kept, attn_received = pair_start(
+        jnp.concatenate([low(grad_qkv_weight), low(grad_out_weight)[None]]).reshape(2, -1, model_width)
+    )
+    grad_first = own_words(grad_first_branch) + by_owner(
         jnp.einsum("kgc,kdc->gd", grad_joined, qkv_weight, preferred_element_type=jnp.float32)
     )
     grad_summed, grad_embed_gain, grad_embed_shift = first_pull(grad_first)
@@ -487,85 +911,105 @@
     )
     vector_grads = jnp.pad(vector_grads, ((0, 0), (0, LANES - vector_grads.shape[1])))
     table_grads = jnp.concatenate([grad_position, vector_grads], axis=1)
-    table_grads = fold(table_grads.reshape(n_wide * n_narrow, own_width, -1), every_bit)
     grad_proj_rows = lax.all_gather(grad_proj_low, "narrow", axis=0, tiled=True)
     grad_proj_weight = jnp.einsum(
         "gd,gh->dh", grad_proj_rows, proj_input, preferred_element_type=jnp.float32
     )
-    grad_proj_weight = fold(
-        grad_proj_weight.reshape(n_wide, n_narrow * own_width, own_hidden), wide_bits
-    )
-    grad_proj_weight = lax.all_to_all(
-        low(grad_proj_weight).reshape(n_narrow, own_width, own_hidden), "narrow", 0, 0, tiled=True
-    )
-    owned_proj = full(
-        grad_proj_weight.reshape(n_narrow, own_width, half_wide, own_mix)
-        .transpose(2, 0, 3, 1)
-        .reshape(filters, own_width)
-    )
+    table_grads = jnp.concatenate([low(table_grads), low(grad_proj_weight)], axis=1)
+    table_grads = table_grads.reshape(n_wide, n_narrow, own_width, -1).transpose(1, 0, 2, 3)
+    table_grads = lax.all_to_all(table_grads, "narrow", 0, 0, tiled=True)
+    table_width = seq_length + LANES
+    table_sums = jnp.sum(full(table_grads[..., :table_width]), axis=0)
+    proj_parts = table_grads[..., table_width:].transpose(1, 0, 2, 3)
+    rest_grads = [item.reshape(n_wide, -1, LANES) for item in (low(table_sums), proj_parts)]
+    table_rows = rest_grads[0].shape[1]
+    rest_grads = jnp.concatenate(rest_grads, axis=1)
     grad_hidden = jnp.dot(grad_proj_rows, proj_own, preferred_element_type=jnp.float32)
 
-    owned_highway = [None, None]
     mix_bias_grads = [None, None]
-    for layer_index in (1, 0):
-        hidden_in, low_input, mixture = highway_saved[layer_index]
-        grad_direct, grad_mixture = jax.vjp(highway_mix, hidden_in, mixture)[1](grad_hidden)
-        grad_mix_low = low(grad_mixture)
-        mix_bias_grads[layer_index] = jnp.sum(full(grad_mix_low), axis=0)
-        weight = mix_weights[layer_index]
-        if layer_index == 1:
-            partial = jnp.einsum(
-                "tf,mcf->mtc",
-                grad_mix_low,
-                weight.reshape(n_narrow, own_hidden, -1),
-                preferred_element_type=jnp.float32,
-            )
-            grad_hidden = grad_direct + fold(partial, narrow_bits)
-        else:
-            partial = dot_nt(grad_mix_low, weight).reshape(group, half_wide, n_narrow, own_mix)
-            mine = (jnp.arange(n_narrow) == me_narrow)[None, None, :, None]
-            direct = grad_direct.reshape(group, half_wide, 1, own_mix)
-            partial = partial + jnp.where(mine, direct, 0.0)
-            grad_features = fold(partial.reshape(n_narrow, word_total, filters), narrow_bits)
-        weight_grad = jnp.einsum(
-            "tk,twc->wkc",
-            low_input,
-            grad_mix_low.reshape(group, n_wide, own_mix),
+
+    def weight_part(joined, mixed):
+        return jnp.einsum(
+            "tk,tzc->zkc",
+            joined,
+            mixed.reshape(group, outer, own_mix),
             preferred_element_type=jnp.float32,
         )
-        weight_grad = full(lax.psum_scatter(low(weight_grad), "wide", scatter_dimension=0))
-        if layer_index == 1:
-            weight_grad = (
-                weight_grad.reshape(n_narrow, half_wide, own_mix, own_mix)
-                .transpose(1, 0, 2, 3)
-                .reshape(filters, own_mix)
-            )
-        owned_highway[layer_index] = weight_grad
-    owned_highway = jnp.stack(owned_highway)
+
+    def pair_weight(layer_index, mixed, met):
+        joined = highway_saved[layer_index][0]
+        return low(weight_part(joined, mixed[0]) + weight_part(pair_joined[layer_index], met))
+
+    ffn_received, attn_received = after((ffn_received, attn_received), grad_hidden)
+    pair_sums = lax.psum(
+        (low(full(ffn_kept) + full(ffn_received)), low(full(attn_kept) + full(attn_received))),
+        "wide",
+        axis_index_groups=outer_groups,
+    )
+    joined, kept_a, kept_t = highway_saved[1]
+    mixed, direct, mix_bias_grads[1] = mix_back(corner, grad_hidden, kept_a, kept_t, joined, n_narrow, False)
+    met = swap(mixed[1], "wide", 0)
+    sent = inner_columns(corner, mixed, mix_weights[1], 1, n_narrow, jnp.bfloat16)
+    kept = inner_columns(corner, mixed, mix_weights[1], 0, n_narrow, jnp.float32)
+    grad_hidden = direct + fold_near(sent, kept, "narrow")
+    weight_second = pair_weight(1, mixed, after(met, grad_hidden))
+    joined, kept_a, kept_t = highway_saved[0]
+    mixed, direct, mix_bias_grads[0] = mix_back(corner, grad_hidden, kept_a, kept_t, joined, n_narrow, plain)
+    met = swap(mixed[1], "wide", 0)
+    sent, kept = inner_rows(corner, mixed, mix_weights[0], direct, n_narrow, plain)
+    grad_features = fold_near(sent, kept, "narrow")
+
+    rest_grads = low(halved(after(rest_grads, direct), *wide_bits[0]))
+    weight_first = pair_weight(0, mixed, met)
+    both = [item.reshape(outer, -1, LANES) for item in (weight_first, weight_second)]
+    weight_rows = both[0].shape[1]
+    both = jnp.concatenate(both + [rest_grads], axis=1)
+    grad_features, both, pair_sums = lax.optimization_barrier((grad_features, both, pair_sums))
+    pair_backs = [swap(item, "wide", 0) for item in pair_sums]
 
     grad_pooled = jax.vjp(smooth_gelu, pooled)[1](grad_features)[0]
     filt_grads, hot_grads = pool_backward(
         columns, columns_t, hot, filt_rows, lse, grad_pooled, char_depth, tap_count
     )
-    filt_grads = jnp.where(tap_keep | is_bias, filt_grads, 0.0)
-    owned_filt = fold(filt_grads.reshape(n_wide * n_narrow, own_filters, LANES), every_bit)
+    both = lax.psum_scatter(both, "wide", scatter_dimension=0, axis_index_groups=outer_groups)
+    both = full(both)
+    owned_highway = jnp.stack(
+        [
+            unordered(both[:weight_rows].reshape(filters, own_mix)),
+            ungrouped(both[weight_rows : 2 * weight_rows].reshape(filters, own_mix)),
+        ]
+    )
+    owned_rest = both[2 * weight_rows :]
+    table_grads = owned_rest[:table_rows].reshape(own_width, table_width)
+    owned_proj = owned_rest[table_rows:].reshape(n_narrow, own_width, own_hidden).transpose(0, 2, 1)
+    owned_proj = ungrouped(owned_proj.reshape(filters, own_width))
+    filt_grads = unordered(low(jnp.where(tap_keep | is_bias, filt_grads, 0.0)))
+    filt_grads = fold(filt_grads.reshape(n_wide, -1, LANES), wide_bits)
+    owned_filt = lax.all_to_all(
+        low(filt_grads).reshape(n_narrow, own_filters, LANES), "narrow", 0, 0, tiled=True
+    )
+    owned_filt = jnp.sum(full(owned_filt), axis=0)
     owned_conv = owned_filt[:, :tap_rows].T
     owned_conv_bias = owned_filt[:, tap_rows + tap_count]
     grad_table = hot_grads[:vocab, :tap_rows].reshape(vocab, tap_count, char_depth).sum(axis=1)
 
-    mix_bias_grads = jnp.stack(mix_bias_grads).reshape(2, n_wide, own_mix)
-    wide_parts = [mix_bias_grads, grad_up_bias, grad_qv_bias]
-    all_parts = [
+    mix_bias_grads = jnp.stack(mix_bias_grads).reshape(2, 2, outer, own_mix)
+    swapped = jnp.stack([jnp.where(me_pair == 0, mix_bias_grads[:, y], mix_bias_grads[:, 1 - y]) for y in range(2)], axis=2)
+    mix_bias_grads = swapped.reshape(2, n_wide, own_mix)
+    wide_parts = [
+        mix_bias_grads,
+        grad_up_bias[0],
+        grad_qv_bias,
         grad_out_bias,
         grad_ln1_gain,
         grad_ln1_shift,
         grad_down_bias,
         grad_ln2_gain,
         grad_ln2_shift,
-        grad_table,
     ]
-
-    def joined(parts):
+    all_parts = [grad_table]
+
+    def joined_rows(parts):
         flat = jnp.concatenate([item.reshape(-1) for item in parts])
         return jnp.pad(flat, (0, -flat.shape[0] % LANES)).reshape(-1, LANES)
 
@@ -576,19 +1020,24 @@
             start += item.size
         return done
 
-    wide_flat, all_flat = joined(wide_parts), joined(all_parts)
-    flat = total(jnp.concatenate([wide_flat, all_flat]), wide_bits)
-    mix_sums, sum_up_bias, sum_qv_bias = parted(flat[: wide_flat.shape[0]], wide_parts)
-    owned_mix_bias = lax.dynamic_index_in_dim(mix_sums, lax.axis_index("wide"), 1, keepdims=False)
+    wide_flat, all_flat = joined_rows(wide_parts), joined_rows(all_parts)
+    flat, pair_backs = lax.optimization_barrier((jnp.concatenate([wide_flat, all_flat]), pair_backs))
+    flat = total(flat, wide_bits)
     (
+        mix_sums,
+        sum_up_bias,
+        sum_qv_bias,
         sum_out_bias,
         sum_ln1_gain,
         sum_ln1_shift,
         sum_down_bias,
         sum_ln2_gain,
         sum_ln2_shift,
-        sum_table,
-    ) = parted(total(flat[wide_flat.shape[0] :], narrow_bits), all_parts)
+    ) = parted(flat[: wide_flat.shape[0]], wide_parts)
+    owned_mix_bias = lax.dynamic_index_in_dim(mix_sums, lax.axis_index("wide"), 1, keepdims=False)
+    sum_table = parted(total(flat[wide_flat.shape[0] :], narrow_bits), all_parts)[0]
+    ffn_sums, attn_sums = (pair_end(mine, back) for mine, back in zip(pair_sums, pair_backs))
+    attn_sums = attn_sums.reshape(n_narrow, local_width, model_width)
     owned_vectors = table_grads[:, seq_length : seq_length + 5].T
     return (
         layer_out,
@@ -603,15 +1052,15 @@
         owned_vectors[1:3],
         owned_vectors[3],
         owned_vectors[4],
-        full(attn_sums[0]),
+        attn_sums[:3].transpose(0, 2, 1),
         sum_qv_bias,
-        full(attn_sums[1]),
+        attn_sums[3],
         sum_out_bias,
         sum_ln1_gain,
         sum_ln1_shift,
-        full(ffn_sums[0]),
+        ffn_sums[0],
         sum_up_bias,
-        full(ffn_sums[1]),
+        ffn_sums[1],
         sum_down_bias,
         sum_ln2_gain,
         sum_ln2_shift,

time: 651 us -> 549 us (0.84)
  waiting for transfers between devices: 259 us -> 152 us
  Pallas kernels: 38.3 us -> 87.3 us
  matrix products: 70.9 us -> 44.2 us
  blocking collectives: 41.7 us -> 16.8 us
  starting transfers between devices: 42 us -> 56.1 us
  local copies, waits for them, and re-layouts: 102 us -> 95 us
    reduce_scatter x2 -> x1, waiting for transfers between devices: 109 us -> 0.01 us  [per_device(): lax.psum_scatter(both, 'wide', scatter_dimension=0, axis_index_groups=out...]
    pallas_call x0 -> x9, Pallas kernels: none -> 48.8 us  [the longest x1 13.2 us: ffn_backward(): pl.pallas_call(functools.partial(ffn_backward_kernel, tile=tile), grid=(l...]
    all_gather x3 -> x0, blocking collectives: 24.7 us -> none  [the longest x1 8.71 us: per_device(): grad_ffn_rows = lax.all_gather(grad_ffn, 'narrow', axis=0, tiled=True)]
    dot_general x10, matrix products: 39.3 us -> 19.4 us  [the longest x4 12.3 us: weight_part(): jnp.einsum('tk,tzc->zkc', joined, mixed.reshape(group, outer, own_mix), p...]
    broadcast_in_dim x4 -> x1, local copies, waits for them, and re-layouts: 10.2 us -> 0.01 us  [per_device(): jnp.broadcast_to(up_bias[None], (16, units))]
    convert_element_type x13 -> x9, other arithmetic: 13.6 us -> 3.82 us  [full(): return values.astype(jnp.float32)]
    ppermute x46 -> x53, starting transfers between devices: 38.3 us -> 48 us  [swap(): return lax.ppermute(block, axis, [(i, i ^ 1 << bit) for i in range(size)])]
    concatenate x2 -> x8, other arithmetic: 1.4 us -> 10.9 us  [the longest x1 2.79 us: per_device(): jnp.concatenate([up_weight, down_weight, out_weight, jnp.broadcast_to(up_...]
  transfers between devices with their start and end apart: 52 -> 60, of which waited for: 31 -> 26; matrix products, arithmetic and copies ran while one was open for 27% -> 32% of each run, Pallas kernels for 6% -> 14%
where the time goes in v2:
time: 549 us; the launch traced here: 542 us
  waiting for transfers between devices  152 us (28%)
  local copies, waits for them, and re-layouts  95 us (17%)
  Pallas kernels  87.3 us (16%)
  other arithmetic  74.1 us (13%)
  starting transfers between devices  56.1 us (10%)
  matrix products  44.2 us (8%)
  blocking collectives  16.8 us (3%)
  between operations  16.5 us (3%)
    ppermute x53, waiting for transfers between devices, swap(): return lax.ppermute(block, axis, [(i, i ^ 1 << bit) for i in range(size)])  140 us
    ppermute x53, starting transfers between devices, swap(): return lax.ppermute(block, axis, [(i, i ^ 1 << bit) for i in range(size)])  48 us
    unnamed x292, local copies, waits for them, and re-layouts  34 us
    pallas_call x1, Pallas kernels, pool_backward(): pl.pallas_call(functools.partial(back_kernel, depth=depth, taps=taps), gr...  24.7 us
    pallas_call x1, Pallas kernels, pool_forward(): pl.pallas_call(functools.partial(pool_kernel, group=5), grid=(filters //...  13.8 us
    pallas_call x1, Pallas kernels, ffn_backward(): pl.pallas_call(functools.partial(ffn_backward_kernel, tile=tile), grid=(l...  13.2 us
    dot_general x4, matrix products, weight_part(): jnp.einsum('tk,tzc->zkc', joined, mixed.reshape(group, outer, own_mix), p...  12.3 us
  transfers between devices with their start and end apart: 60, of which 26 were waited for; matrix products, arithmetic and copies ran while one was open for 32% of the time, Pallas kernels for 14%

profile of v2, /device:TPU:0, one launch (start us, length us, event | category | flops | bytes accessed | tf_op | source)
XLA Modules:
  0.0 541.7 jit_solution(18282880727891324633)
XLA Ops:
  31.8 6.4 %concatenate.58.cols_t_ref = bf16[128,6400]{1,0:T(8,128)(2,1)} concatenate(bf16[16,6400]{1,0:T(8,128)(2,1)S(1)} %convolution_convert_fusion, bf16[16,6400]{1,0:T(8,128)(2,1)S(1)} %get-tuple-element.428, bf16[16,6400]{1,0:T(8,128)(2,1)S(1)} %get-tuple-element.424, bf16[16,6400]{1,0:T(8,128)(2,1)S(1)} %get-tuple-element.425, bf16[16,6400]{1,0:T(8,128)(2,1)S(1)} %get-tuple-element.426, ...), dimensions={0} | concatenate | bytes 3276800 | tf_op jit(solution)/shard_map/concatenate | solution.py:733
  48.9 33.2 %collective-permute-done.4 = bf16[8,66,128]{2,0,1:T(8,128)(2,1)S(1)} collective-permute-done((bf16[8,66,128]{2,0,1:T(8,128)(2,1)S(1)}, bf16[8,66,128]{2,0,1:T(8,128)(2,1)S(1)}, u32[]{:S(2)}, u32[]{:S(2)}) %collective-permute-start.4) | collective-permute-done | bytes 135200 | tf_op jit(solution)/shard_map/ppermute | solution.py:46
  82.6 7.6 %all-gather.5.cloned.1.call-done.refs_4_.refs_5_.refs_0_.refs_1_.refs_2_.refs_3_.refs_6_.refs_7_ = bf16[8,2048,128]{2,1,0:T(8,128)(2,1)} async-done(((bf16[1,2048,128]{2,1,0:T(8,128)(2,1)}), bf16[8,2048,128]{2,1,0:T(8,128)(2,1)}) %all-gather.5.cloned.1.call-update) | async-done | bytes 4194320 | tf_op jit(solution)/shard_map/all_gather | solution.py:681
  92.9 5.2 collective-permute-done.6
  98.2 13.8 %pool_forward.1.lse_ref = f32[128,2048]{1,0:T(8,128)S(1)} custom-call(bf16[50,128,128]{2,1,0:T(8,128)(2,1)S(1)} %bitcast.389, bf16[2048,128]{1,0:T(8,128)(2,1)S(1)} %fusion.56.filt_ref), custom_call_target="tpu_custom_call" | custom-call | flops 1000 | bytes 1000 | tf_op jit(solution)/shard_map/pool_forward/pallas_call | solution.py:150
  118.0 9.4 %collective-permute-done.9.refs_2_ = bf16[128,2048]{1,0:T(8,128)(2,1)S(1)} collective-permute-done((bf16[128,2048]{1,0:T(8,128)(2,1)S(1)}, bf16[128,2048]{1,0:T(8,128)(2,1)S(1)}, u32[]{:S(2)}, u32[]{:S(2)}) %collective-permute-start.9) | collective-permute-done | bytes 524320 | tf_op jit(solution)/shard_map/ppermute | solution.py:46
  127.4 5.6 %collective-permute-done.8 = bf16[4,24,2688]{2,1,0:T(8,128)(2,1)} collective-permute-done((bf16[4,24,2688]{2,1,0:T(8,128)(2,1)S(1)}, bf16[4,24,2688]{2,1,0:T(8,128)(2,1)}, u32[]{:S(2)}, u32[]{:S(2)}) %collective-permute-start.8) | collective-permute-done | bytes 516128 | tf_op jit(solution)/shard_map/ppermute | solution.py:46
  145.1 4.7 mix_forward.2
  156.4 12.7 %collective-permute-done.15.refs_2_ = bf16[512,512]{1,0:T(8,128)(2,1)} collective-permute-done((bf16[512,512]{1,0:T(8,128)(2,1)}, bf16[512,512]{1,0:T(8,128)(2,1)}, u32[]{:S(2)}, u32[]{:S(2)}) %collective-permute-start.15) | collective-permute-done | bytes 524320 | tf_op jit(solution)/shard_map/ppermute | solution.py:46
  173.6 5.8 %mix_forward.3 = (bf16[512,2048]{1,0:T(8,128)(2,1)S(1)}, bf16[512,512]{1,0:T(8,128)(2,1)S(1)}, f32[512,512]{1,0:T(8,128)S(1)}, f32[512,512]{1,0:T(8,128)S(1)}) custom-call(s32[2]{0:T(128)S(1)} %pad_add_fusion.place_ref, bf16[512,512]{1,0:T(8,128)(2,1)} %get-tuple-element.129.refs_0_, bf16[512,512]{1,0:T(8,128)(2,1)} %collective-permute-done.14.refs_1_, ...), custom_call_target="tpu_custom_call" | custom-call | flops 1000 | bytes 1000 | tf_op jit(solution)/shard_map/mix_forward/pallas_call | solution.py:291
  194.4 4.7 collective-permute-done.20
  202.5 9.1 %all_gather.22 = bf16[512,768]{1,0:T(8,128)(2,1)S(1)} all-gather(bf16[128,768]{1,0:T(8,128)(2,1)S(1)} %add_convert_fusion.5), channel_id=1, replica_groups=mesh['wide'=8,'narrow'=4] {'narrow'}, dimensions={0}, use_global_device_ids=true | all-gather | bytes 983040 | tf_op jit(solution)/shard_map/all_gather | solution.py:814
  222.6 5.3 collective-permute-done.22
  233.0 10.1 %ffn_forward.1 = (f32[512,768]{1,0:T(8,128)S(1)}, bf16[512,768]{1,0:T(8,128)(2,1)S(1)}) custom-call(bf16[512,768]{1,0:T(8,128)(2,1)S(1)} %fusion.33.x_ref, bf16[1744,768]{1,0:T(8,128)(2,1)} %pad_maximum_fusion.1.refs_0_.refs_1_.refs_2_, bf16[1744,768]{1,0:T(8,128)(2,1)} %pad_maximum_fusion.1.refs_0_.refs_1_.refs_2_, ...), custom_call_target="tpu_custom_call" | custom-call | flops 1000 | bytes 1000 | tf_op jit(solution)/shard_map/ffn_forward/pallas_call | solution.py:508
  248.6 13.2 %ffn_backward.1 = (f32[512,768]{1,0:T(8,128)S(1)}, bf16[512,768]{1,0:T(8,128)(2,1)S(1)}, f32[1,768]{1,0:T(1,128)S(1)}) custom-call(bf16[512,768]{1,0:T(8,128)(2,1)S(1)} %fusion.33.x_ref, bf16[512,768]{1,0:T(8,128)(2,1)S(1)} %get-tuple-element.360.grad_ref, bf16[1744,768]{1,0:T(8,128)(2,1)} %pad_maximum_fusion.1.refs_0_.refs_1_.refs_2_, ...), custom_call_target="tpu_custom_call" | custom-call | flops 1000 | bytes 1000 | tf_op jit(solution)/shard_map/ffn_backward/pallas_call | solution.py:551
  291.7 7.7 %all_gather.23 = bf16[512,768]{1,0:T(8,128)(2,1)S(1)} all-gather(bf16[128,768]{1,0:T(8,128)(2,1)S(1)} %get-tuple-element.362), channel_id=1, replica_groups=mesh['wide'=8,'narrow'=4] {'narrow'}, dimensions={0}, use_global_device_ids=true | all-gather | bytes 983040 | tf_op jit(solution)/shard_map/all_gather | solution.py:914
  339.1 5.0 fusion.23
  355.1 7.1 %collective-permute-done.35 = bf16[1,512,512]{2,1,0:T(8,128)(2,1)} collective-permute-done((bf16[1,512,512]{2,1,0:T(8,128)(2,1)}, bf16[1,512,512]{2,1,0:T(8,128)(2,1)}, u32[]{:S(2)}, u32[]{:S(2)}) %collective-permute-start.35) | collective-permute-done | bytes 524320 | tf_op jit(solution)/shard_map/ppermute | solution.py:46
  381.4 4.9 inner_rows.1
  408.3 8.7 %collective-permute-done.37 = bf16[1,128,2048]{2,1,0:T(8,128)(2,1)S(1)} collective-permute-done((bf16[1,128,2048]{2,1,0:T(8,128)(2,1)}, bf16[1,128,2048]{2,1,0:T(8,128)(2,1)S(1)}, u32[]{:S(2)}, u32[]{:S(2)}) %collective-permute-start.37) | collective-permute-done | bytes 524320 | tf_op jit(solution)/shard_map/ppermute | solution.py:46
  425.9 24.7 %pool_backward.1 = (f32[2048,128]{1,0:T(8,128)S(1)}, f32[272,128]{1,0:T(8,128)S(1)}) custom-call(bf16[50,128,128]{2,1,0:T(8,128)(2,1)S(1)} %bitcast.390, bf16[128,6400]{1,0:T(8,128)(2,1)} %concatenate.58.cols_t_ref, bf16[272,6400]{1,0:T(8,128)(2,1)} %fusion.1.hot_ref, bf16[2048,128]{1,0:T(8,128)(2,1)S(1)} %copy-done.16, f32[128,2048]{1,0:T(8,128)S(1)} %copy-done.20, ...), custom_call_target="tpu_custom_call" | custom-call | flops 1000 | bytes 1000 | tf_op jit(solution)/shard_map/pool_backward/pallas_call | solution.py:206
  452.6 5.2 collective-permute-done.50
  461.2 8.2 %collective-permute-done.51 = bf16[2,256,128]{2,1,0:T(8,128)(2,1)S(1)} collective-permute-done((bf16[2,256,128]{2,1,0:T(8,128)(2,1)S(1)}, bf16[2,256,128]{2,1,0:T(8,128)(2,1)S(1)}, u32[]{:S(2)}, u32[]{:S(2)}) %collective-permute-start.51) | collective-permute-done | bytes 131104 | tf_op jit(solution)/shard_map/ppermute | solution.py:46
  486.8 10.6 %collective-permute-done.44 = bf16[384,768]{1,0:T(8,128)(2,1)S(1)} collective-permute-done((bf16[384,768]{1,0:T(8,128)(2,1)S(1)}, bf16[384,768]{1,0:T(8,128)(2,1)S(1)}, u32[]{:S(2)}, u32[]{:S(2)}) %collective-permute-start.44) | collective-permute-done | bytes 589856 | tf_op jit(solution)/shard_map/ppermute | solution.py:46
  (673 shorter events, 296.4 us)
Async XLA Ops:
  7.3 82.9 %all-gather.5.cloned.1.call-start = ((), (), s32[]{:S(2)}) async-start(), calls=%async_computation.3 | async-start | bytes 4718592 | tf_op jit(solution)/shard_map/all_gather | solution.py:681
  9.6 159.5 %all-gather.9.cloned.1.call-start = ((), (), s32[]{:S(2)}) async-start(), calls=%async_computation.6 | async-start | bytes 4718592 | tf_op jit(solution)/shard_map/all_gather | solution.py:681
  19.5 78.7 %collective-permute-start.7 = (bf16[1744,768]{1,0:T(8,128)(2,1)}, bf16[1744,768]{1,0:T(8,128)(2,1)}, u32[]{:S(2)}, u32[]{:S(2)}) collective-permute-start(bf16[1744,768]{1,0:T(8,128)(2,1)} %pad_maximum_fusion.1.refs_0_.refs_1_.refs_2_), channel_id=1, source_target_pairs={{0,2},{1,3},{2,0},{3,1},{4,6},{5,7},{6,4},{7,5},{8,10},{9,11},{10,... | collective-permute-start | bytes 8036360 | tf_op jit(solution)/shard_map/ppermute | solution.py:46
  21.4 27.5 %collective-permute-start = (bf16[1,24,2688]{2,1,0:T(8,128)(2,1)S(1)}, bf16[1,24,2688]{2,1,0:T(8,128)(2,1)S(1)}, u32[]{:S(2)}, u32[]{:S(2)}) collective-permute-start(bf16[1,24,2688]{2,1,0:T(8,128)(2,1)S(1)} %fusion.85), channel_id=1, source_target_pairs={{0,16},{4,20},{8,24},{12,28},{16,0},{20,4},{24,8},{28,12},{1,17},{... | collective-permute-start | bytes 387080 | tf_op jit(solution)/shard_map/ppermute | solution.py:46
  48.3 33.9 %collective-permute-start.4 = (bf16[8,66,128]{2,0,1:T(8,128)(2,1)S(1)}, bf16[8,66,128]{2,0,1:T(8,128)(2,1)S(1)}, u32[]{:S(2)}, u32[]{:S(2)}) collective-permute-start(bf16[8,66,128]{2,0,1:T(8,128)(2,1)S(1)} %bitcast.441), channel_id=1, source_target_pairs={{0,2},{1,3},{2,0},{3,1},{4,6},{5,7},{6,4},{7,5},{8,10},{9,11},{10,... | collective-permute-start | bytes 405512 | tf_op jit(solution)/shard_map/ppermute | solution.py:46
  90.2 109.6 %all-gather.7.cloned.1.call-start = ((), (), s32[]{:S(2)}) async-start(), calls=%async_computation.4 | async-start | bytes 1966080 | tf_op jit(solution)/shard_map/all_gather | solution.py:768
  149.8 21.5 %collective-permute-start.17 = (bf16[1744,768]{1,0:T(8,128)(2,1)}, bf16[1744,768]{1,0:T(8,128)(2,1)}, u32[]{:S(2)}, u32[]{:S(2)}) collective-permute-start(bf16[1744,768]{1,0:T(8,128)(2,1)} %pad_maximum_fusion.1.refs_0_.refs_1_.refs_2_), channel_id=1, source_target_pairs={{0,1},{1,0},{2,3},{3,2},{4,5},{5,4},{6,7},{7,6},{8,9},{9,8},{10,11... | collective-permute-start | bytes 8036360 | tf_op jit(solution)/shard_map/ppermute | solution.py:46
  150.0 21.3 %collective-permute-start.18 = (bf16[1744,768]{1,0:T(8,128)(2,1)}, bf16[1744,768]{1,0:T(8,128)(2,1)}, u32[]{:S(2)}, u32[]{:S(2)}) collective-permute-start(bf16[1744,768]{1,0:T(8,128)(2,1)} %collective-permute-done.7.refs_3_.refs_4_.refs_5_), channel_id=1, source_target_pairs={{0,1},{1,0},{2,3},{3,2},{4,5},{5,4},{6,7},{7,6},{8,9},{9,8},{10,11... | collective-permute-start | bytes 8036360 | tf_op jit(solution)/shard_map/ppermute | solution.py:46
  185.7 47.3 %collective-permute-start.24 = (bf16[128,2048]{1,0:T(8,128)(2,1)S(1)}, bf16[128,2048]{1,0:T(8,128)(2,1)}, u32[]{:S(2)}, u32[]{:S(2)}) collective-permute-start(bf16[128,2048]{1,0:T(8,128)(2,1)S(1)} %get-tuple-element.375.refs_0_), channel_id=1, source_target_pairs={{0,4},{4,0},{8,12},{12,8},{16,20},{20,16},{24,28},{28,24},{1,5},{5... | collective-permute-start | bytes 1572872 | tf_op jit(solution)/shard_map/ppermute | solution.py:46
  186.7 46.2 %collective-permute-start.25 = (bf16[512,512]{1,0:T(8,128)(2,1)}, bf16[512,512]{1,0:T(8,128)(2,1)}, u32[]{:S(2)}, u32[]{:S(2)}) collective-permute-start(bf16[512,512]{1,0:T(8,128)(2,1)} %get-tuple-element.129.refs_0_), channel_id=1, source_target_pairs={{0,4},{4,0},{8,12},{12,8},{16,20},{20,16},{24,28},{28,24},{1,5},{5... | collective-permute-start | bytes 1572872 | tf_op jit(solution)/shard_map/ppermute | solution.py:46
  243.1 23.9 %collective-permute-start.30 = (bf16[512,512]{1,0:T(8,128)(2,1)}, bf16[512,512]{1,0:T(8,128)(2,1)S(1)}, u32[]{:S(2)}, u32[]{:S(2)}) collective-permute-start(bf16[512,512]{1,0:T(8,128)(2,1)} %collective-permute-done.25), channel_id=1, source_target_pairs={{0,2},{1,3},{2,0},{3,1},{4,6},{5,7},{6,4},{7,5},{8,10},{9,11},{10,... | collective-permute-start | bytes 1572872 | tf_op jit(solution)/shard_map/ppermute | solution.py:46
  243.5 25.9 %collective-permute-start.29 = (bf16[512,512]{1,0:T(8,128)(2,1)}, bf16[512,512]{1,0:T(8,128)(2,1)}, u32[]{:S(2)}, u32[]{:S(2)}) collective-permute-start(bf16[512,512]{1,0:T(8,128)(2,1)} %collective-permute-done.25), channel_id=1, source_target_pairs={{0,1},{1,0},{2,3},{3,2},{4,5},{5,4},{6,7},{7,6},{8,9},{9,8},{10,11... | collective-permute-start | bytes 1572872 | tf_op jit(solution)/shard_map/ppermute | solution.py:46
  243.8 25.3 %collective-permute-start.27 = (bf16[128,2048]{1,0:T(8,128)(2,1)}, bf16[128,2048]{1,0:T(8,128)(2,1)}, u32[]{:S(2)}, u32[]{:S(2)}) collective-permute-start(bf16[128,2048]{1,0:T(8,128)(2,1)} %collective-permute-done.24), channel_id=1, source_target_pairs={{0,2},{1,3},{2,0},{3,1},{4,6},{5,7},{6,4},{7,5},{8,10},{9,11},{10,... | collective-permute-start | bytes 1572872 | tf_op jit(solution)/shard_map/ppermute | solution.py:46
  245.4 23.9 %collective-permute-start.26 = (bf16[128,2048]{1,0:T(8,128)(2,1)}, bf16[128,2048]{1,0:T(8,128)(2,1)}, u32[]{:S(2)}, u32[]{:S(2)}) collective-permute-start(bf16[128,2048]{1,0:T(8,128)(2,1)} %collective-permute-done.24), channel_id=1, source_target_pairs={{0,1},{1,0},{2,3},{3,2},{4,5},{5,4},{6,7},{7,6},{8,9},{9,8},{10,11... | collective-permute-start | bytes 1572872 | tf_op jit(solution)/shard_map/ppermute | solution.py:46
  265.3 44.7 %collective-permute-start.41 = (bf16[768,768]{1,0:T(8,128)(2,1)S(1)}, bf16[768,768]{1,0:T(8,128)(2,1)}, u32[]{:S(2)}, u32[]{:S(2)}) collective-permute-start(bf16[768,768]{1,0:T(8,128)(2,1)S(1)} %fusion.36), channel_id=1, source_target_pairs={{0,4},{4,0},{8,12},{12,8},{16,20},{20,16},{24,28},{28,24},{1,5},{5... | collective-permute-start | bytes 3538952 | tf_op jit(solution)/shard_map/ppermute | solution.py:46
  279.9 30.2 %collective-permute-start.42 = (bf16[384,768]{1,0:T(8,128)(2,1)S(1)}, bf16[384,768]{1,0:T(8,128)(2,1)S(1)}, u32[]{:S(2)}, u32[]{:S(2)}) collective-permute-start(bf16[384,768]{1,0:T(8,128)(2,1)S(1)} %dynamic-slice_bitcast_fusion), channel_id=1, source_target_pairs={{0,4},{4,0},{8,12},{12,8},{16,20},{20,16},{24,28},{28,24},{1,5},{5... | collective-permute-start | bytes 1769480 | tf_op jit(solution)/shard_map/ppermute | solution.py:46
  306.7 37.4 %collective-permute-start.34 = (bf16[2,512,512]{2,1,0:T(8,128)(2,1)}, bf16[2,512,512]{2,1,0:T(8,128)(2,1)}, u32[]{:S(2)}, u32[]{:S(2)}) collective-permute-start(bf16[2,512,512]{2,1,0:T(8,128)(2,1)} %inner_columns.3), channel_id=1, source_target_pairs={{0,1},{1,0},{2,3},{3,2},{4,5},{5,4},{6,7},{7,6},{8,9},{9,8},{10,11... | collective-permute-start | bytes 3145736 | tf_op jit(solution)/shard_map/ppermute | solution.py:46
  322.4 27.4 %all-to-all-start = ((bf16[4,8,24,1152]{3,2,1,0:T(8,128)(2,1)}), bf16[4,8,24,1152]{3,2,1,0:T(8,128)(2,1)}, u32[]{:S(2)}, u32[]{:S(2)}) async-start(bf16[4,8,24,1152]{3,2,1,0:T(8,128)(2,1)} %copy.283), calls=%async_computation | async-start | bytes 3538944 | tf_op jit(solution)/shard_map/all_to_all | solution.py:920
  326.8 91.3 %all-reduce.9.cloned.1.call-start = ((), (), s32[]{:S(2)}) async-start(), calls=%async_computation.7 | async-start | bytes 3538944 | tf_op jit(solution)/shard_map/psum | solution.py:944
  334.6 35.9 %collective-permute-start.39 = (bf16[512,512]{1,0:T(8,128)(2,1)}, bf16[512,512]{1,0:T(8,128)(2,1)}, u32[]{:S(2)}, u32[]{:S(2)}) collective-permute-start(bf16[512,512]{1,0:T(8,128)(2,1)} %get-tuple-element.405), channel_id=1, source_target_pairs={{0,4},{4,0},{8,12},{12,8},{16,20},{20,16},{24,28},{28,24},{1,5},{5... | collective-permute-start | bytes 1572872 | tf_op jit(solution)/shard_map/ppermute | solution.py:46
  339.0 182.3 %reduce-scatter.2.cloned.1.call-start = ((), (), s32[]{:S(2)}) async-start(), calls=%async_computation.5 | async-start | bytes 5898240 | tf_op jit(solution)/shard_map/reduce_scatter | solution.py:974
  369.4 26.0 %collective-permute-start.38 = (bf16[512,512]{1,0:T(8,128)(2,1)}, bf16[512,512]{1,0:T(8,128)(2,1)}, u32[]{:S(2)}, u32[]{:S(2)}) collective-permute-start(bf16[512,512]{1,0:T(8,128)(2,1)} %get-tuple-element.404), channel_id=1, source_target_pairs={{0,4},{4,0},{8,12},{12,8},{16,20},{20,16},{24,28},{28,24},{1,5},{5... | collective-permute-start | bytes 1572872 | tf_op jit(solution)/shard_map/ppermute | solution.py:46
  459.1 38.3 %collective-permute-start.43 = (bf16[768,768]{1,0:T(8,128)(2,1)S(1)}, bf16[768,768]{1,0:T(8,128)(2,1)}, u32[]{:S(2)}, u32[]{:S(2)}) collective-permute-start(bf16[768,768]{1,0:T(8,128)(2,1)S(1)} %copy-done.66), channel_id=1, source_target_pairs={{0,4},{4,0},{8,12},{12,8},{16,20},{20,16},{24,28},{28,24},{1,5},{5... | collective-permute-start | bytes 3538952 | tf_op jit(solution)/shard_map/ppermute | solution.py:46
  460.7 36.7 %collective-permute-start.44 = (bf16[384,768]{1,0:T(8,128)(2,1)S(1)}, bf16[384,768]{1,0:T(8,128)(2,1)S(1)}, u32[]{:S(2)}, u32[]{:S(2)}) collective-permute-start(bf16[384,768]{1,0:T(8,128)(2,1)S(1)} %copy-done.75), channel_id=1, source_target_pairs={{0,4},{4,0},{8,12},{12,8},{16,20},{20,16},{24,28},{28,24},{1,5},{5... | collective-permute-start | bytes 1769480 | tf_op jit(solution)/shard_map/ppermute | solution.py:46
  (174 other events, 1409.0 us)
Sparse Core Ops, SparseCore 0:
  10.8 79.3 all-gather.4
  92.3 74.8 all-gather.8
  169.2 21.9 all-gather.6
  339.1 78.3 all-reduce.8
  419.8 90.0 reduce-scatter.1

commit v3 on v2

--- a/solution.py
+++ b/solution.py
@@ -464,6 +464,28 @@
         cost_estimate=LIGHT,
         name="inner_rows",
     )(place, mixed, *[weights] * (2 * blocks), direct)
+
+
+def widen_kernel(sums_ref, out_ref, *, parts):
+    filters, tile = out_ref.shape[1:]
+    outer = filters // (2 * parts * tile)
+    for z in range(outer):
+        for pair in range(2):
+            for m in range(parts):
+                at = ((z * 2 + pair) * parts + m) * tile
+                source = filters + ((m * 2 + pair) * outer + z) * tile
+                out_ref[0, at : at + tile, :] = sums_ref[:, at : at + tile].T
+                out_ref[1, at : at + tile, :] = sums_ref[:, source : source + tile].T
+
+
+def widen(sums, filters, parts):
+    return pl.pallas_call(
+        functools.partial(widen_kernel, parts=parts),
+        out_shape=jax.ShapeDtypeStruct((2, filters, sums.shape[0]), jnp.float32),
+        compiler_params=pltpu.CompilerParams(vmem_limit_bytes=16 * 2**20),
+        cost_estimate=LIGHT,
+        name="widen",
+    )(sums)
 
 
 def slope_of(values):
@@ -909,28 +931,30 @@
         ],
         axis=1,
     )
-    vector_grads = jnp.pad(vector_grads, ((0, 0), (0, LANES - vector_grads.shape[1])))
-    table_grads = jnp.concatenate([grad_position, vector_grads], axis=1)
+    vector_grads = jnp.pad(low(vector_grads), ((0, 0), (0, LANES - vector_grads.shape[1])))
     grad_proj_rows = lax.all_gather(grad_proj_low, "narrow", axis=0, tiled=True)
     grad_proj_weight = jnp.einsum(
         "gd,gh->dh", grad_proj_rows, proj_input, preferred_element_type=jnp.float32
     )
-    table_grads = jnp.concatenate([low(table_grads), low(grad_proj_weight)], axis=1)
-    table_grads = table_grads.reshape(n_wide, n_narrow, own_width, -1).transpose(1, 0, 2, 3)
+    table_grads = [
+        item.reshape(n_wide, n_narrow, own_width, -1).transpose(1, 0, 2, 3)
+        for item in (low(grad_position), vector_grads, low(grad_proj_weight))
+    ]
+    table_grads = jnp.concatenate(table_grads, axis=3)
     table_grads = lax.all_to_all(table_grads, "narrow", 0, 0, tiled=True)
     table_width = seq_length + LANES
     table_sums = jnp.sum(full(table_grads[..., :table_width]), axis=0)
     proj_parts = table_grads[..., table_width:].transpose(1, 0, 2, 3)
-    rest_grads = [item.reshape(n_wide, -1, LANES) for item in (low(table_sums), proj_parts)]
-    table_rows = rest_grads[0].shape[1]
-    rest_grads = jnp.concatenate(rest_grads, axis=1)
+    rest_grads = [item.reshape(n_wide, LANES, -1) for item in (low(table_sums), proj_parts)]
+    table_columns = rest_grads[0].shape[2]
+    rest_grads = jnp.concatenate(rest_grads, axis=2)
     grad_hidden = jnp.dot(grad_proj_rows, proj_own, preferred_element_type=jnp.float32)
 
     mix_bias_grads = [None, None]
 
     def weight_part(joined, mixed):
         return jnp.einsum(
-            "tk,tzc->zkc",
+            "tk,tzc->zck",
             joined,
             mixed.reshape(group, outer, own_mix),
             preferred_element_type=jnp.float32,
@@ -961,11 +985,10 @@
 
     rest_grads = low(halved(after(rest_grads, direct), *wide_bits[0]))
     weight_first = pair_weight(0, mixed, met)
-    both = [item.reshape(outer, -1, LANES) for item in (weight_first, weight_second)]
-    weight_rows = both[0].shape[1]
-    both = jnp.concatenate(both + [rest_grads], axis=1)
+    both = [item.reshape(outer, LANES, -1) for item in (weight_first, weight_second)]
+    weight_columns = both[0].shape[2]
+    both = jnp.concatenate(both + [rest_grads], axis=2)
     grad_features, both, pair_sums = lax.optimization_barrier((grad_features, both, pair_sums))
-    pair_backs = [swap(item, "wide", 0) for item in pair_sums]
 
     grad_pooled = jax.vjp(smooth_gelu, pooled)[1](grad_features)[0]
     filt_grads, hot_grads = pool_backward(
@@ -973,26 +996,20 @@
     )
     both = lax.psum_scatter(both, "wide", scatter_dimension=0, axis_index_groups=outer_groups)
     both = full(both)
-    owned_highway = jnp.stack(
-        [
-            unordered(both[:weight_rows].reshape(filters, own_mix)),
-            ungrouped(both[weight_rows : 2 * weight_rows].reshape(filters, own_mix)),
+    if plain:
+        owned_highway = widen(both, filters, n_narrow)
+    else:
+        owned_highway = [
+            both[:, at * weight_columns : (at + 1) * weight_columns].reshape(own_mix, filters).T
+            for at in range(2)
         ]
-    )
-    owned_rest = both[2 * weight_rows :]
-    table_grads = owned_rest[:table_rows].reshape(own_width, table_width)
-    owned_proj = owned_rest[table_rows:].reshape(n_narrow, own_width, own_hidden).transpose(0, 2, 1)
+        owned_highway = jnp.stack([unordered(owned_highway[0]), ungrouped(owned_highway[1])])
+    owned_rest = both[:, 2 * weight_columns :]
+    table_grads = owned_rest[:, :table_columns].reshape(own_width, table_width)
+    owned_proj = owned_rest[:, table_columns:].reshape(n_narrow, own_width, own_hidden).transpose(0, 2, 1)
     owned_proj = ungrouped(owned_proj.reshape(filters, own_width))
     filt_grads = unordered(low(jnp.where(tap_keep | is_bias, filt_grads, 0.0)))
-    filt_grads = fold(filt_grads.reshape(n_wide, -1, LANES), wide_bits)
-    owned_filt = lax.all_to_all(
-        low(filt_grads).reshape(n_narrow, own_filters, LANES), "narrow", 0, 0, tiled=True
-    )
-    owned_filt = jnp.sum(full(owned_filt), axis=0)
-    owned_conv = owned_filt[:, :tap_rows].T
-    owned_conv_bias = owned_filt[:, tap_rows + tap_count]
     grad_table = hot_grads[:vocab, :tap_rows].reshape(vocab, tap_count, char_depth).sum(axis=1)
-
     mix_bias_grads = jnp.stack(mix_bias_grads).reshape(2, 2, outer, own_mix)
     swapped = jnp.stack([jnp.where(me_pair == 0, mix_bias_grads[:, y], mix_bias_grads[:, 1 - y]) for y in range(2)], axis=2)
     mix_bias_grads = swapped.reshape(2, n_wide, own_mix)
@@ -1021,8 +1038,20 @@
         return done
 
     wide_flat, all_flat = joined_rows(wide_parts), joined_rows(all_parts)
-    flat, pair_backs = lax.optimization_barrier((jnp.concatenate([wide_flat, all_flat]), pair_backs))
-    flat = total(flat, wide_bits)
+    flat = total(jnp.concatenate([wide_flat, all_flat]), wide_bits[:1])
+    filt_grads = halved(filt_grads.reshape(n_wide, -1, LANES), *wide_bits[0])
+    flat, filt_grads = lax.optimization_barrier((flat, filt_grads))
+    filt_grads = fold(filt_grads, wide_bits[1:])
+    owned_filt = lax.all_to_all(
+        low(filt_grads).reshape(n_narrow, own_filters, LANES), "narrow", 0, 0, tiled=True
+    )
+    owned_filt = jnp.sum(full(owned_filt), axis=0)
+    owned_conv = owned_filt[:, :tap_rows].T
+    owned_conv_bias = owned_filt[:, tap_rows + tap_count]
+
+    flat, pair_backs = lax.optimization_barrier(
+        (total(flat, wide_bits[1:]), [swap(item, "wide", 0) for item in pair_sums])
+    )
     (
         mix_sums,
         sum_up_bias,

time: 549 us -> 529 us (0.964)
  local copies, waits for them, and re-layouts: 95 us -> 82.6 us
    unnamed x292 -> x295, local copies, waits for them, and re-layouts: 34 us -> 30.9 us
  transfers between devices with their start and end apart: 60 -> 60, of which waited for: 26 -> 26; matrix products, arithmetic and copies ran while one was open for 32% -> 31% of each run, Pallas kernels for 14% -> 14%
where the time goes in v3:
time: 529 us; the launch traced here: 522 us
  waiting for transfers between devices  148 us (28%)
  Pallas kernels  89.8 us (17%)
  local copies, waits for them, and re-layouts  82.6 us (16%)
  other arithmetic  70.6 us (13%)
  starting transfers between devices  53.8 us (10%)
  matrix products  43.6 us (8%)
  blocking collectives  17.2 us (3%)
  between operations  16.9 us (3%)
    ppermute x53, waiting for transfers between devices, swap(): return lax.ppermute(block, axis, [(i, i ^ 1 << bit) for i in range(size)])  137 us
    ppermute x53, starting transfers between devices, swap(): return lax.ppermute(block, axis, [(i, i ^ 1 << bit) for i in range(size)])  45.7 us
    unnamed x295, local copies, waits for them, and re-layouts  30.9 us
    pallas_call x1, Pallas kernels, pool_backward(): pl.pallas_call(functools.partial(back_kernel, depth=depth, taps=taps), gr...  25.4 us
    pallas_call x1, Pallas kernels, pool_forward(): pl.pallas_call(functools.partial(pool_kernel, group=5), grid=(filters //...  13.7 us
    pallas_call x1, Pallas kernels, ffn_backward(): pl.pallas_call(functools.partial(ffn_backward_kernel, tile=tile), grid=(l...  13.3 us
    dot_general x4, matrix products, weight_part(): jnp.einsum('tk,tzc->zck', joined, mixed.reshape(group, outer, own_mix), p...  12.3 us
  transfers between devices with their start and end apart: 60, of which 26 were waited for; matrix products, arithmetic and copies ran while one was open for 31% of the time, Pallas kernels for 14%

profile of v3, /device:TPU:0, one launch (start us, length us, event | category | flops | bytes accessed | tf_op | source)
XLA Modules:
  0.0 522.3 jit_solution(9348130995079032443)
XLA Ops:
  31.8 6.4 %concatenate.55.cols_t_ref = bf16[128,6400]{1,0:T(8,128)(2,1)} concatenate(bf16[16,6400]{1,0:T(8,128)(2,1)S(1)} %convolution_convert_fusion, bf16[16,6400]{1,0:T(8,128)(2,1)S(1)} %get-tuple-element.404, bf16[16,6400]{1,0:T(8,128)(2,1)S(1)} %get-tuple-element.400, bf16[16,6400]{1,0:T(8,128)(2,1)S(1)} %get-tuple-element.401, bf16[16,6400]{1,0:T(8,128)(2,1)S(1)} %get-tuple-element.402, ...), dimensions={0} | concatenate | bytes 3276800 | tf_op jit(solution)/shard_map/concatenate | solution.py:755
  48.9 33.3 %collective-permute-done.4 = bf16[8,66,128]{2,0,1:T(8,128)(2,1)S(1)} collective-permute-done((bf16[8,66,128]{2,0,1:T(8,128)(2,1)S(1)}, bf16[8,66,128]{2,0,1:T(8,128)(2,1)S(1)}, u32[]{:S(2)}, u32[]{:S(2)}) %collective-permute-start.4) | collective-permute-done | bytes 135200 | tf_op jit(solution)/shard_map/ppermute | solution.py:46
  82.6 7.6 %all-gather.5.cloned.1.call-done.refs_4_.refs_5_.refs_0_.refs_1_.refs_2_.refs_3_.refs_6_.refs_7_ = bf16[8,2048,128]{2,1,0:T(8,128)(2,1)} async-done(((bf16[1,2048,128]{2,1,0:T(8,128)(2,1)}), bf16[8,2048,128]{2,1,0:T(8,128)(2,1)}) %all-gather.5.cloned.1.call-update) | async-done | bytes 4194320 | tf_op jit(solution)/shard_map/all_gather | solution.py:703
  93.0 5.2 collective-permute-done.6
  98.3 13.7 %pool_forward.1.lse_ref = f32[128,2048]{1,0:T(8,128)S(1)} custom-call(bf16[50,128,128]{2,1,0:T(8,128)(2,1)S(1)} %bitcast.396, bf16[2048,128]{1,0:T(8,128)(2,1)S(1)} %fusion.50.filt_ref), custom_call_target="tpu_custom_call" | custom-call | flops 1000 | bytes 1000 | tf_op jit(solution)/shard_map/pool_forward/pallas_call | solution.py:150
  118.1 9.4 %collective-permute-done.9.refs_2_ = bf16[128,2048]{1,0:T(8,128)(2,1)S(1)} collective-permute-done((bf16[128,2048]{1,0:T(8,128)(2,1)S(1)}, bf16[128,2048]{1,0:T(8,128)(2,1)S(1)}, u32[]{:S(2)}, u32[]{:S(2)}) %collective-permute-start.9) | collective-permute-done | bytes 524320 | tf_op jit(solution)/shard_map/ppermute | solution.py:46
  127.4 5.7 %collective-permute-done.8 = bf16[4,24,2688]{2,1,0:T(8,128)(2,1)} collective-permute-done((bf16[4,24,2688]{2,1,0:T(8,128)(2,1)S(1)}, bf16[4,24,2688]{2,1,0:T(8,128)(2,1)}, u32[]{:S(2)}, u32[]{:S(2)}) %collective-permute-start.8) | collective-permute-done | bytes 516128 | tf_op jit(solution)/shard_map/ppermute | solution.py:46
  145.2 4.7 mix_forward.2
  156.5 12.7 %collective-permute-done.15.refs_2_ = bf16[512,512]{1,0:T(8,128)(2,1)} collective-permute-done((bf16[512,512]{1,0:T(8,128)(2,1)}, bf16[512,512]{1,0:T(8,128)(2,1)}, u32[]{:S(2)}, u32[]{:S(2)}) %collective-permute-start.15) | collective-permute-done | bytes 524320 | tf_op jit(solution)/shard_map/ppermute | solution.py:46
  173.8 5.8 %mix_forward.3 = (bf16[512,2048]{1,0:T(8,128)(2,1)S(1)}, bf16[512,512]{1,0:T(8,128)(2,1)S(1)}, f32[512,512]{1,0:T(8,128)S(1)}, f32[512,512]{1,0:T(8,128)S(1)}) custom-call(s32[2]{0:T(128)S(1)} %pad_add_fusion.place_ref, bf16[512,512]{1,0:T(8,128)(2,1)} %get-tuple-element.131.refs_0_, bf16[512,512]{1,0:T(8,128)(2,1)} %collective-permute-done.14.refs_1_, ...), custom_call_target="tpu_custom_call" | custom-call | flops 1000 | bytes 1000 | tf_op jit(solution)/shard_map/mix_forward/pallas_call | solution.py:291
  194.4 4.8 collective-permute-done.20
  202.6 9.1 %all_gather.22 = bf16[512,768]{1,0:T(8,128)(2,1)S(1)} all-gather(bf16[128,768]{1,0:T(8,128)(2,1)S(1)} %add_convert_fusion.5), channel_id=1, replica_groups=mesh['wide'=8,'narrow'=4] {'narrow'}, dimensions={0}, use_global_device_ids=true | all-gather | bytes 983040 | tf_op jit(solution)/shard_map/all_gather | solution.py:836
  222.8 5.3 %collective-permute-done.22 = bf16[512,192]{0,1:T(8,128)(2,1)S(1)} collective-permute-done((bf16[512,192]{0,1:T(8,128)(2,1)S(1)}, bf16[512,192]{0,1:T(8,128)(2,1)S(1)}, u32[]{:S(2)}, u32[]{:S(2)}) %collective-permute-start.22) | collective-permute-done | bytes 196640 | tf_op jit(solution)/shard_map/ppermute | solution.py:46
  233.1 10.1 %ffn_forward.1 = (f32[512,768]{1,0:T(8,128)S(1)}, bf16[512,768]{1,0:T(8,128)(2,1)S(1)}) custom-call(bf16[512,768]{1,0:T(8,128)(2,1)S(1)} %fusion.27.x_ref, bf16[1744,768]{1,0:T(8,128)(2,1)} %pad_maximum_fusion.1.refs_0_.refs_1_.refs_2_, bf16[1744,768]{1,0:T(8,128)(2,1)} %pad_maximum_fusion.1.refs_0_.refs_1_.refs_2_, ...), custom_call_target="tpu_custom_call" | custom-call | flops 1000 | bytes 1000 | tf_op jit(solution)/shard_map/ffn_forward/pallas_call | solution.py:530
  248.8 13.3 %ffn_backward.1 = (f32[512,768]{1,0:T(8,128)S(1)}, bf16[512,768]{1,0:T(8,128)(2,1)S(1)}, f32[1,768]{1,0:T(1,128)S(1)}) custom-call(bf16[512,768]{1,0:T(8,128)(2,1)S(1)} %fusion.27.x_ref, bf16[512,768]{1,0:T(8,128)(2,1)S(1)} %get-tuple-element.340.grad_ref, bf16[1744,768]{1,0:T(8,128)(2,1)} %pad_maximum_fusion.1.refs_0_.refs_1_.refs_2_, ...), custom_call_target="tpu_custom_call" | custom-call | flops 1000 | bytes 1000 | tf_op jit(solution)/shard_map/ffn_backward/pallas_call | solution.py:573
  292.7 8.1 %all_gather.23 = bf16[512,768]{1,0:T(8,128)(2,1)S(1)} all-gather(bf16[128,768]{1,0:T(8,128)(2,1)S(1)} %get-tuple-element.342), channel_id=1, replica_groups=mesh['wide'=8,'narrow'=4] {'narrow'}, dimensions={0}, use_global_device_ids=true | all-gather | bytes 983040 | tf_op jit(solution)/shard_map/all_gather | solution.py:935
  318.5 4.4 all-to-all-start
  335.3 5.0 fusion.19
  352.3 6.1 %collective-permute-done.35 = bf16[1,512,512]{2,1,0:T(8,128)(2,1)} collective-permute-done((bf16[1,512,512]{2,1,0:T(8,128)(2,1)}, bf16[1,512,512]{2,1,0:T(8,128)(2,1)}, u32[]{:S(2)}, u32[]{:S(2)}) %collective-permute-start.35) | collective-permute-done | bytes 524320 | tf_op jit(solution)/shard_map/ppermute | solution.py:46
  378.5 4.9 inner_rows.1
  402.7 9.1 %collective-permute-done.37 = bf16[1,128,2048]{2,1,0:T(8,128)(2,1)S(1)} collective-permute-done((bf16[1,128,2048]{2,1,0:T(8,128)(2,1)}, bf16[1,128,2048]{2,1,0:T(8,128)(2,1)S(1)}, u32[]{:S(2)}, u32[]{:S(2)}) %collective-permute-start.37) | collective-permute-done | bytes 524320 | tf_op jit(solution)/shard_map/ppermute | solution.py:46
  420.1 25.4 %pool_backward.1 = (f32[2048,128]{1,0:T(8,128)S(1)}, f32[272,128]{1,0:T(8,128)S(1)}) custom-call(bf16[50,128,128]{2,1,0:T(8,128)(2,1)S(1)} %bitcast.397, bf16[128,6400]{1,0:T(8,128)(2,1)} %concatenate.55.cols_t_ref, bf16[272,6400]{1,0:T(8,128)(2,1)} %fusion.1.hot_ref, bf16[2048,128]{1,0:T(8,128)(2,1)S(1)} %copy-done.16, f32[128,2048]{1,0:T(8,128)S(1)} %copy-done.20, ...), custom_call_target="tpu_custom_call" | custom-call | flops 1000 | bytes 1000 | tf_op jit(solution)/shard_map/pool_backward/pallas_call | solution.py:206
  456.3 9.4 %collective-permute-done.51 = bf16[2,256,128]{2,1,0:T(8,128)(2,1)S(1)} collective-permute-done((bf16[2,256,128]{2,1,0:T(8,128)(2,1)S(1)}, bf16[2,256,128]{2,1,0:T(8,128)(2,1)S(1)}, u32[]{:S(2)}, u32[]{:S(2)}) %collective-permute-start.51) | collective-permute-done | bytes 131104 | tf_op jit(solution)/shard_map/ppermute | solution.py:46
  486.1 8.5 %collective-permute-done.48 = bf16[384,768]{1,0:T(8,128)(2,1)S(1)} collective-permute-done((bf16[384,768]{1,0:T(8,128)(2,1)}, bf16[384,768]{1,0:T(8,128)(2,1)S(1)}, u32[]{:S(2)}, u32[]{:S(2)}) %collective-permute-start.48) | collective-permute-done | bytes 589856 | tf_op jit(solution)/shard_map/ppermute | solution.py:46
  (673 shorter events, 277.7 us)
Async XLA Ops:
  7.3 82.9 %all-gather.5.cloned.1.call-start = ((), (), s32[]{:S(2)}) async-start(), calls=%async_computation.3 | async-start | bytes 4718592 | tf_op jit(solution)/shard_map/all_gather | solution.py:703
  9.6 159.6 %all-gather.9.cloned.1.call-start = ((), (), s32[]{:S(2)}) async-start(), calls=%async_computation.6 | async-start | bytes 4718592 | tf_op jit(solution)/shard_map/all_gather | solution.py:703
  19.5 78.7 %collective-permute-start.7 = (bf16[1744,768]{1,0:T(8,128)(2,1)}, bf16[1744,768]{1,0:T(8,128)(2,1)}, u32[]{:S(2)}, u32[]{:S(2)}) collective-permute-start(bf16[1744,768]{1,0:T(8,128)(2,1)} %pad_maximum_fusion.1.refs_0_.refs_1_.refs_2_), channel_id=1, source_target_pairs={{0,2},{1,3},{2,0},{3,1},{4,6},{5,7},{6,4},{7,5},{8,10},{9,11},{10,... | collective-permute-start | bytes 8036360 | tf_op jit(solution)/shard_map/ppermute | solution.py:46
  21.4 27.5 %collective-permute-start = (bf16[1,24,2688]{2,1,0:T(8,128)(2,1)S(1)}, bf16[1,24,2688]{2,1,0:T(8,128)(2,1)S(1)}, u32[]{:S(2)}, u32[]{:S(2)}) collective-permute-start(bf16[1,24,2688]{2,1,0:T(8,128)(2,1)S(1)} %fusion.79), channel_id=1, source_target_pairs={{0,16},{4,20},{8,24},{12,28},{16,0},{20,4},{24,8},{28,12},{1,17},{... | collective-permute-start | bytes 387080 | tf_op jit(solution)/shard_map/ppermute | solution.py:46
  48.3 33.9 %collective-permute-start.4 = (bf16[8,66,128]{2,0,1:T(8,128)(2,1)S(1)}, bf16[8,66,128]{2,0,1:T(8,128)(2,1)S(1)}, u32[]{:S(2)}, u32[]{:S(2)}) collective-permute-start(bf16[8,66,128]{2,0,1:T(8,128)(2,1)S(1)} %bitcast.452), channel_id=1, source_target_pairs={{0,2},{1,3},{2,0},{3,1},{4,6},{5,7},{6,4},{7,5},{8,10},{9,11},{10,... | collective-permute-start | bytes 405512 | tf_op jit(solution)/shard_map/ppermute | solution.py:46
  90.2 109.8 %all-gather.7.cloned.1.call-start = ((), (), s32[]{:S(2)}) async-start(), calls=%async_computation.4 | async-start | bytes 1966080 | tf_op jit(solution)/shard_map/all_gather | solution.py:790
  150.0 21.5 %collective-permute-start.17 = (bf16[1744,768]{1,0:T(8,128)(2,1)}, bf16[1744,768]{1,0:T(8,128)(2,1)}, u32[]{:S(2)}, u32[]{:S(2)}) collective-permute-start(bf16[1744,768]{1,0:T(8,128)(2,1)} %pad_maximum_fusion.1.refs_0_.refs_1_.refs_2_), channel_id=1, source_target_pairs={{0,1},{1,0},{2,3},{3,2},{4,5},{5,4},{6,7},{7,6},{8,9},{9,8},{10,11... | collective-permute-start | bytes 8036360 | tf_op jit(solution)/shard_map/ppermute | solution.py:46
  150.1 21.3 %collective-permute-start.18 = (bf16[1744,768]{1,0:T(8,128)(2,1)}, bf16[1744,768]{1,0:T(8,128)(2,1)}, u32[]{:S(2)}, u32[]{:S(2)}) collective-permute-start(bf16[1744,768]{1,0:T(8,128)(2,1)} %collective-permute-done.7.refs_3_.refs_4_.refs_5_), channel_id=1, source_target_pairs={{0,1},{1,0},{2,3},{3,2},{4,5},{5,4},{6,7},{7,6},{8,9},{9,8},{10,11... | collective-permute-start | bytes 8036360 | tf_op jit(solution)/shard_map/ppermute | solution.py:46
  185.7 47.4 %collective-permute-start.24 = (bf16[128,2048]{1,0:T(8,128)(2,1)S(1)}, bf16[128,2048]{1,0:T(8,128)(2,1)}, u32[]{:S(2)}, u32[]{:S(2)}) collective-permute-start(bf16[128,2048]{1,0:T(8,128)(2,1)S(1)} %get-tuple-element.355.refs_0_), channel_id=1, source_target_pairs={{0,4},{4,0},{8,12},{12,8},{16,20},{20,16},{24,28},{28,24},{1,5},{5... | collective-permute-start | bytes 1572872 | tf_op jit(solution)/shard_map/ppermute | solution.py:46
  186.8 46.3 %collective-permute-start.25 = (bf16[512,512]{1,0:T(8,128)(2,1)}, bf16[512,512]{1,0:T(8,128)(2,1)}, u32[]{:S(2)}, u32[]{:S(2)}) collective-permute-start(bf16[512,512]{1,0:T(8,128)(2,1)} %get-tuple-element.131.refs_0_), channel_id=1, source_target_pairs={{0,4},{4,0},{8,12},{12,8},{16,20},{20,16},{24,28},{28,24},{1,5},{5... | collective-permute-start | bytes 1572872 | tf_op jit(solution)/shard_map/ppermute | solution.py:46
  243.3 23.9 %collective-permute-start.30 = (bf16[512,512]{1,0:T(8,128)(2,1)}, bf16[512,512]{1,0:T(8,128)(2,1)S(1)}, u32[]{:S(2)}, u32[]{:S(2)}) collective-permute-start(bf16[512,512]{1,0:T(8,128)(2,1)} %collective-permute-done.25), channel_id=1, source_target_pairs={{0,2},{1,3},{2,0},{3,1},{4,6},{5,7},{6,4},{7,5},{8,10},{9,11},{10,... | collective-permute-start | bytes 1572872 | tf_op jit(solution)/shard_map/ppermute | solution.py:46
  243.6 25.9 %collective-permute-start.29 = (bf16[512,512]{1,0:T(8,128)(2,1)}, bf16[512,512]{1,0:T(8,128)(2,1)}, u32[]{:S(2)}, u32[]{:S(2)}) collective-permute-start(bf16[512,512]{1,0:T(8,128)(2,1)} %collective-permute-done.25), channel_id=1, source_target_pairs={{0,1},{1,0},{2,3},{3,2},{4,5},{5,4},{6,7},{7,6},{8,9},{9,8},{10,11... | collective-permute-start | bytes 1572872 | tf_op jit(solution)/shard_map/ppermute | solution.py:46
  243.9 25.3 %collective-permute-start.27 = (bf16[128,2048]{1,0:T(8,128)(2,1)}, bf16[128,2048]{1,0:T(8,128)(2,1)}, u32[]{:S(2)}, u32[]{:S(2)}) collective-permute-start(bf16[128,2048]{1,0:T(8,128)(2,1)} %collective-permute-done.24), channel_id=1, source_target_pairs={{0,2},{1,3},{2,0},{3,1},{4,6},{5,7},{6,4},{7,5},{8,10},{9,11},{10,... | collective-permute-start | bytes 1572872 | tf_op jit(solution)/shard_map/ppermute | solution.py:46
  245.6 23.9 %collective-permute-start.26 = (bf16[128,2048]{1,0:T(8,128)(2,1)}, bf16[128,2048]{1,0:T(8,128)(2,1)}, u32[]{:S(2)}, u32[]{:S(2)}) collective-permute-start(bf16[128,2048]{1,0:T(8,128)(2,1)} %collective-permute-done.24), channel_id=1, source_target_pairs={{0,1},{1,0},{2,3},{3,2},{4,5},{5,4},{6,7},{7,6},{8,9},{9,8},{10,11... | collective-permute-start | bytes 1572872 | tf_op jit(solution)/shard_map/ppermute | solution.py:46
  265.5 38.8 %collective-permute-start.41 = (bf16[768,768]{1,0:T(8,128)(2,1)S(1)}, bf16[768,768]{1,0:T(8,128)(2,1)S(1)}, u32[]{:S(2)}, u32[]{:S(2)}) collective-permute-start(bf16[768,768]{1,0:T(8,128)(2,1)S(1)} %fusion.30), channel_id=1, source_target_pairs={{0,4},{4,0},{8,12},{12,8},{16,20},{20,16},{24,28},{28,24},{1,5},{5... | collective-permute-start | bytes 3538952 | tf_op jit(solution)/shard_map/ppermute | solution.py:46
  279.0 27.6 %collective-permute-start.42 = (bf16[384,768]{1,0:T(8,128)(2,1)S(1)}, bf16[384,768]{1,0:T(8,128)(2,1)S(1)}, u32[]{:S(2)}, u32[]{:S(2)}) collective-permute-start(bf16[384,768]{1,0:T(8,128)(2,1)S(1)} %dynamic-slice_bitcast_fusion), channel_id=1, source_target_pairs={{0,4},{4,0},{8,12},{12,8},{16,20},{20,16},{24,28},{28,24},{1,5},{5... | collective-permute-start | bytes 1769480 | tf_op jit(solution)/shard_map/ppermute | solution.py:46
  312.8 27.5 %collective-permute-start.34 = (bf16[2,512,512]{2,1,0:T(8,128)(2,1)}, bf16[2,512,512]{2,1,0:T(8,128)(2,1)}, u32[]{:S(2)}, u32[]{:S(2)}) collective-permute-start(bf16[2,512,512]{2,1,0:T(8,128)(2,1)} %inner_columns.3), channel_id=1, source_target_pairs={{0,1},{1,0},{2,3},{3,2},{4,5},{5,4},{6,7},{7,6},{8,9},{9,8},{10,11... | collective-permute-start | bytes 3145736 | tf_op jit(solution)/shard_map/ppermute | solution.py:46
  318.5 27.4 %all-to-all-start = ((bf16[4,8,24,1152]{3,2,1,0:T(8,128)(2,1)}), bf16[4,8,24,1152]{3,2,1,0:T(8,128)(2,1)}, u32[]{:S(2)}, u32[]{:S(2)}) async-start(bf16[4,8,24,1152]{3,2,1,0:T(8,128)(2,1)} %pad_maximum_fusion.3), calls=%async_computation | async-start | bytes 3538944 | tf_op jit(solution)/shard_map/all_to_all | solution.py:944
  322.9 91.2 %all-reduce.9.cloned.1.call-start = ((), (), s32[]{:S(2)}) async-start(), calls=%async_computation.7 | async-start | bytes 3538944 | tf_op jit(solution)/shard_map/psum | solution.py:968
  330.7 35.6 %collective-permute-start.39 = (bf16[512,512]{1,0:T(8,128)(2,1)}, bf16[512,512]{1,0:T(8,128)(2,1)}, u32[]{:S(2)}, u32[]{:S(2)}) collective-permute-start(bf16[512,512]{1,0:T(8,128)(2,1)} %get-tuple-element.383), channel_id=1, source_target_pairs={{0,4},{4,0},{8,12},{12,8},{16,20},{20,16},{24,28},{28,24},{1,5},{5... | collective-permute-start | bytes 1572872 | tf_op jit(solution)/shard_map/ppermute | solution.py:46
  335.2 172.5 %reduce-scatter.2.cloned.1.call-start = ((), (), s32[]{:S(2)}) async-start(), calls=%async_computation.5 | async-start | bytes 5898240 | tf_op jit(solution)/shard_map/reduce_scatter | solution.py:997
  365.2 24.8 %collective-permute-start.38 = (bf16[512,512]{1,0:T(8,128)(2,1)}, bf16[512,512]{1,0:T(8,128)(2,1)}, u32[]{:S(2)}, u32[]{:S(2)}) collective-permute-start(bf16[512,512]{1,0:T(8,128)(2,1)} %get-tuple-element.382), channel_id=1, source_target_pairs={{0,4},{4,0},{8,12},{12,8},{16,20},{20,16},{24,28},{28,24},{1,5},{5... | collective-permute-start | bytes 1572872 | tf_op jit(solution)/shard_map/ppermute | solution.py:46
  455.6 39.8 %collective-permute-start.47 = (bf16[768,768]{1,0:T(8,128)(2,1)S(1)}, bf16[768,768]{1,0:T(8,128)(2,1)}, u32[]{:S(2)}, u32[]{:S(2)}) collective-permute-start(bf16[768,768]{1,0:T(8,128)(2,1)S(1)} %copy-done.69), channel_id=1, source_target_pairs={{0,4},{4,0},{8,12},{12,8},{16,20},{20,16},{24,28},{28,24},{1,5},{5... | collective-permute-start | bytes 3538952 | tf_op jit(solution)/shard_map/ppermute | solution.py:46
  470.7 23.9 %collective-permute-start.48 = (bf16[384,768]{1,0:T(8,128)(2,1)}, bf16[384,768]{1,0:T(8,128)(2,1)S(1)}, u32[]{:S(2)}, u32[]{:S(2)}) collective-permute-start(bf16[384,768]{1,0:T(8,128)(2,1)} %get-tuple-element.188), channel_id=1, source_target_pairs={{0,4},{4,0},{8,12},{12,8},{16,20},{20,16},{24,28},{28,24},{1,5},{5... | collective-permute-start | bytes 1769480 | tf_op jit(solution)/shard_map/ppermute | solution.py:46
  (176 other events, 1429.0 us)
Sparse Core Ops, SparseCore 0:
  10.8 79.3 all-gather.4
  92.3 74.9 all-gather.8
  169.3 21.9 all-gather.6
  335.3 78.7 all-reduce.8
  416.4 90.6 reduce-scatter.1

commit v4 on v3

--- a/solution.py
+++ b/solution.py
@@ -309,7 +309,7 @@
             jax.ShapeDtypeStruct((rows, 2 * piece), jnp.float32),
             jax.ShapeDtypeStruct((rows, 2 * piece), jnp.float32),
         ],
-        compiler_params=pltpu.CompilerParams(vmem_limit_bytes=40 * 2**20),
+        compiler_params=pltpu.CompilerParams(vmem_limit_bytes=60 * 2**20),
         cost_estimate=LIGHT,
         name="mix_forward",
     )(place, *parts, weights, weights, bias)
@@ -493,97 +493,103 @@
     return phi + values * (0.3989422804014327 * jnp.exp(-0.5 * values * values))
 
 
+def weight_copies(part_refs, up_ref, down_ref, bias_ref, sems):
+    units = up_ref.shape[1]
+    copies = []
+    for k, part in enumerate(part_refs):
+        last = part.shape[0] - 16
+        copies.append(
+            (
+                pltpu.make_async_copy(part.at[pl.ds(0, units)], up_ref.at[k], sems.at[3 * k]),
+                pltpu.make_async_copy(part.at[pl.ds(units, units)], down_ref.at[k], sems.at[3 * k + 1]),
+                pltpu.make_async_copy(part.at[pl.ds(last, 16)], bias_ref.at[k], sems.at[3 * k + 2]),
+            )
+        )
+    for part_copies in copies:
+        for copy in part_copies:
+            copy.start()
+    return copies
+
+
 def ffn_forward_kernel(x_ref, *refs, tile):
-    out_ref, own_ref = refs[-2:]
-    step = pl.program_id(0)
-    for k, (up_ref, down_ref, bias_ref) in enumerate(zip(refs[:-2:3], refs[1:-2:3], refs[2:-2:3])):
-
-        @pl.when(step == k)
-        def _(k=k, up_ref=up_ref, down_ref=down_ref, bias_ref=bias_ref):
-            for first in range(0, x_ref.shape[0], tile):
-                at = slice(first, first + tile)
-                value = jnp.dot(x_ref[at, :], up_ref[...], preferred_element_type=jnp.float32)
-                active = low(gelu_parts(value + full(bias_ref[0:1, :]))[1])
-                added = jnp.dot(active, down_ref[...], preferred_element_type=jnp.float32)
-                if k == 0:
-                    out_ref[at, :] = added
-                    own_ref[at, :] = active
-                else:
-                    out_ref[at, :] += added
-
-
-def ffn_operands(parts, units):
+    part_refs, (out_ref, own_ref, up_ref, down_ref, bias_ref, sems) = refs[:-6], refs[-6:]
+    copies = weight_copies(part_refs, up_ref, down_ref, bias_ref, sems)
+    for k, part_copies in enumerate(copies):
+        for copy in part_copies:
+            copy.wait()
+        for first in range(0, x_ref.shape[0], tile):
+            at = slice(first, first + tile)
+            value = jnp.dot(x_ref[at, :], up_ref[k], preferred_element_type=jnp.float32)
+            active = low(gelu_parts(value + full(bias_ref[k, 0:1, :]))[1])
+            added = jnp.dot(active, down_ref[k], preferred_element_type=jnp.float32)
+            if k == 0:
+                out_ref[at, :] = added
+                own_ref[at, :] = active
+            else:
+                out_ref[at, :] += added
+
+
+def ffn_call(kernel, operands, parts, units, outs, name):
     width = parts[0].shape[1]
-    last = (parts[0].shape[0] - 16) // 16
-    specs = [
-        pl.BlockSpec((units, width), lambda k: (0, 0)),
-        pl.BlockSpec((units, width), lambda k: (1, 0)),
-        pl.BlockSpec((16, width), lambda k: (last, 0)),
-    ]
-    return specs * len(parts), [part for part in parts for _ in range(3)]
+    vmem = pl.BlockSpec(memory_space=pltpu.VMEM)
+    return pl.pallas_call(
+        kernel,
+        in_specs=[vmem] * len(operands) + [pl.BlockSpec(memory_space=pl.ANY)] * len(parts),
+        out_specs=[vmem] * len(outs),
+        out_shape=outs,
+        scratch_shapes=[
+            pltpu.VMEM((len(parts), units, width), jnp.bfloat16),
+            pltpu.VMEM((len(parts), units, width), jnp.bfloat16),
+            pltpu.VMEM((len(parts), 16, width), jnp.bfloat16),
+            pltpu.SemaphoreType.DMA((3 * len(parts),)),
+        ],
+        compiler_params=pltpu.CompilerParams(vmem_limit_bytes=40 * 2**20),
+        cost_estimate=LIGHT,
+        name=name,
+    )(*operands, *parts)
 
 
 def ffn_forward(x, parts, units, tile=256):
     rows, width = x.shape
-    whole = lambda shape: pl.BlockSpec(shape, lambda k: (0,) * len(shape))
-    specs, operands = ffn_operands(parts, units)
-    return pl.pallas_call(
-        functools.partial(ffn_forward_kernel, tile=tile),
-        grid=(len(parts),),
-        in_specs=[whole(x.shape)] + specs,
-        out_specs=[whole((rows, width)), whole((rows, units))],
-        out_shape=[
-            jax.ShapeDtypeStruct((rows, width), jnp.float32),
-            jax.ShapeDtypeStruct((rows, units), jnp.bfloat16),
-        ],
-        compiler_params=pltpu.CompilerParams(vmem_limit_bytes=48 * 2**20),
-        cost_estimate=LIGHT,
-        name="ffn_forward",
-    )(x, *operands)
+    outs = [
+        jax.ShapeDtypeStruct((rows, width), jnp.float32),
+        jax.ShapeDtypeStruct((rows, units), jnp.bfloat16),
+    ]
+    kernel = functools.partial(ffn_forward_kernel, tile=tile)
+    return ffn_call(kernel, [x], parts, units, outs, "ffn_forward")
 
 
 def ffn_backward_kernel(x_ref, grad_ref, *refs, tile):
-    out_ref, own_ref, sums_ref = refs[-3:]
-    step = pl.program_id(0)
-    for k, (up_ref, down_ref, bias_ref) in enumerate(zip(refs[:-3:3], refs[1:-3:3], refs[2:-3:3])):
-
-        @pl.when(step == k)
-        def _(k=k, up_ref=up_ref, down_ref=down_ref, bias_ref=bias_ref):
-            sums = jnp.zeros(sums_ref.shape, jnp.float32)
-            for first in range(0, x_ref.shape[0], tile):
-                at = slice(first, first + tile)
-                value = jnp.dot(x_ref[at, :], up_ref[...], preferred_element_type=jnp.float32)
-                value = value + full(bias_ref[0:1, :])
-                inner = low(dot_nt(grad_ref[at, :], down_ref[...]) * slope_of(value))
-                added = dot_nt(inner, up_ref[...])
-                if k == 0:
-                    out_ref[at, :] = added
-                    own_ref[at, :] = inner
-                    sums = sums + jnp.sum(full(inner), axis=0, keepdims=True)
-                else:
-                    out_ref[at, :] += added
+    part_refs, (out_ref, own_ref, sums_ref, up_ref, down_ref, bias_ref, sems) = refs[:-7], refs[-7:]
+    copies = weight_copies(part_refs, up_ref, down_ref, bias_ref, sems)
+    sums = jnp.zeros(sums_ref.shape, jnp.float32)
+    for k, part_copies in enumerate(copies):
+        for copy in part_copies:
+            copy.wait()
+        for first in range(0, x_ref.shape[0], tile):
+            at = slice(first, first + tile)
+            value = jnp.dot(x_ref[at, :], up_ref[k], preferred_element_type=jnp.float32)
+            value = value + full(bias_ref[k, 0:1, :])
+            inner = low(dot_nt(grad_ref[at, :], down_ref[k]) * slope_of(value))
+            added = dot_nt(inner, up_ref[k])
             if k == 0:
-                sums_ref[...] = sums
+                out_ref[at, :] = added
+                own_ref[at, :] = inner
+                sums = sums + jnp.sum(full(inner), axis=0, keepdims=True)
+            else:
+                out_ref[at, :] += added
+    sums_ref[...] = sums
 
 
 def ffn_backward(x, parts, units, grad, tile=256):
     rows, width = x.shape
-    whole = lambda shape: pl.BlockSpec(shape, lambda k: (0,) * len(shape))
-    specs, operands = ffn_operands(parts, units)
-    return pl.pallas_call(
-        functools.partial(ffn_backward_kernel, tile=tile),
-        grid=(len(parts),),
-        in_specs=[whole(x.shape), whole(grad.shape)] + specs,
-        out_specs=[whole((rows, width)), whole((rows, units)), whole((1, units))],
-        out_shape=[
-            jax.ShapeDtypeStruct((rows, width), jnp.float32),
-            jax.ShapeDtypeStruct((rows, units), jnp.bfloat16),
-            jax.ShapeDtypeStruct((1, units), jnp.float32),
-        ],
-        compiler_params=pltpu.CompilerParams(vmem_limit_bytes=48 * 2**20),
-        cost_estimate=LIGHT,
-        name="ffn_backward",
-    )(x, grad, *operands)
+    outs = [
+        jax.ShapeDtypeStruct((rows, width), jnp.float32),
+        jax.ShapeDtypeStruct((rows, units), jnp.bfloat16),
+        jax.ShapeDtypeStruct((1, units), jnp.float32),
+    ]
+    kernel = functools.partial(ffn_backward_kernel, tile=tile)
+    return ffn_call(kernel, [x, grad], parts, units, outs, "ffn_backward")
 
 
 def masked_scores(query_heads, key_heads, keep_mask, score_scale):
@@ -818,8 +824,8 @@
             encoder_parts = encoder_parts + [
                 swap(item, "narrow", 0) for item in after(encoder_parts, hidden)
             ]
-            parts, encoder_parts = lax.optimization_barrier((parts, encoder_parts))
-    rest, proj_input = lax.optimization_barrier((rest, hidden))
+            parts, encoder_parts, rest = lax.optimization_barrier((parts, encoder_parts, rest))
+    proj_input = hidden
     rest = rest.reshape(n_wide * n_narrow * own_width, -1)
     model_width = rest.shape[0]
     proj_own = rest[:, :own_hidden]

time: 529 us -> 515 us (0.974)
  local copies, waits for them, and re-layouts: 82.6 us -> 66.9 us
    unnamed x295 -> x269, local copies, waits for them, and re-layouts: 30.9 us -> 17.6 us
    pallas_call x2, Pallas kernels: 10.5 us -> 16 us  [mix_forward(): pl.pallas_call(functools.partial(mix_kernel, parts=len(parts), by_rows=by...]
  transfers between devices with their start and end apart: 60 -> 60, of which waited for: 26 -> 27; matrix products, arithmetic and copies ran while one was open for 31% -> 31% of each run, Pallas kernels for 14% -> 15%
where the time goes in v4:
time: 515 us; the launch traced here: 509 us
  waiting for transfers between devices  147 us (29%)
  Pallas kernels  89.9 us (17%)
  other arithmetic  72.6 us (14%)
  local copies, waits for them, and re-layouts  66.9 us (13%)
  starting transfers between devices  57 us (11%)
  matrix products  42.8 us (8%)
  between operations  16.6 us (3%)
  blocking collectives  16.2 us (3%)
    ppermute x53, waiting for transfers between devices, swap(): return lax.ppermute(block, axis, [(i, i ^ 1 << bit) for i in range(size)])  133 us
    ppermute x53, starting transfers between devices, swap(): return lax.ppermute(block, axis, [(i, i ^ 1 << bit) for i in range(size)])  46 us
    pallas_call x1, Pallas kernels, pool_backward(): pl.pallas_call(functools.partial(back_kernel, depth=depth, taps=taps), gr...  25.3 us
    pallas_call x2, Pallas kernels, ffn_call(): pl.pallas_call(kernel, in_specs=[vmem] * len(operands) + [pl.BlockSpec(me...  18.6 us
    unnamed x269, local copies, waits for them, and re-layouts  17.6 us
    pallas_call x2, Pallas kernels, mix_forward(): pl.pallas_call(functools.partial(mix_kernel, parts=len(parts), by_rows=by...  16 us
    pallas_call x1, Pallas kernels, pool_forward(): pl.pallas_call(functools.partial(pool_kernel, group=5), grid=(filters //...  13.8 us
    dot_general x4, matrix products, weight_part(): jnp.einsum('tk,tzc->zck', joined, mixed.reshape(group, outer, own_mix), p...  12.1 us
  transfers between devices with their start and end apart: 60, of which 27 were waited for; matrix products, arithmetic and copies ran while one was open for 31% of the time, Pallas kernels for 15%

profile of v4, /device:TPU:0, one launch (start us, length us, event | category | flops | bytes accessed | tf_op | source)
XLA Modules:
  0.0 508.6 jit_solution(2153648644461398483)
XLA Ops:
  32.3 6.4 %concatenate.53.cols_t_ref = bf16[128,6400]{1,0:T(8,128)(2,1)} concatenate(bf16[16,6400]{1,0:T(8,128)(2,1)S(1)} %convolution_convert_fusion, bf16[16,6400]{1,0:T(8,128)(2,1)S(1)} %get-tuple-element.402, bf16[16,6400]{1,0:T(8,128)(2,1)S(1)} %get-tuple-element.398, bf16[16,6400]{1,0:T(8,128)(2,1)S(1)} %get-tuple-element.399, bf16[16,6400]{1,0:T(8,128)(2,1)S(1)} %get-tuple-element.400, ...), dimensions={0} | concatenate | bytes 3276800 | tf_op jit(solution)/shard_map/concatenate | solution.py:761
  48.9 34.3 %collective-permute-done.3 = bf16[8,66,128]{2,0,1:T(8,128)(2,1)S(1)} collective-permute-done((bf16[8,66,128]{2,0,1:T(8,128)(2,1)S(1)}, bf16[8,66,128]{2,0,1:T(8,128)(2,1)S(1)}, u32[]{:S(2)}, u32[]{:S(2)}) %collective-permute-start.3) | collective-permute-done | bytes 135200 | tf_op jit(solution)/shard_map/ppermute | solution.py:46
  83.6 5.2 %all-gather.5.cloned.1.call-done.refs_4_.refs_5_.refs_0_.refs_1_.refs_2_.refs_3_.refs_6_.refs_7_ = bf16[8,2048,128]{2,1,0:T(8,128)(2,1)} async-done(((bf16[1,2048,128]{2,1,0:T(8,128)(2,1)}), bf16[8,2048,128]{2,1,0:T(8,128)(2,1)}) %all-gather.5.cloned.1.call-update) | async-done | bytes 4194320 | tf_op jit(solution)/shard_map/all_gather | solution.py:709
  92.5 5.0 collective-permute-done.15
  97.6 13.8 %pool_forward.1.lse_ref = f32[128,2048]{1,0:T(8,128)S(1)} custom-call(bf16[50,128,128]{2,1,0:T(8,128)(2,1)S(1)} %bitcast.396, bf16[2048,128]{1,0:T(8,128)(2,1)S(1)} %fusion.50.filt_ref), custom_call_target="tpu_custom_call" | custom-call | flops 1000 | bytes 1000 | tf_op jit(solution)/shard_map/pool_forward/pallas_call | solution.py:150
  117.3 9.6 %collective-permute-done.7.refs_2_ = bf16[128,2048]{1,0:T(8,128)(2,1)S(1)} collective-permute-done((bf16[128,2048]{1,0:T(8,128)(2,1)}, bf16[128,2048]{1,0:T(8,128)(2,1)S(1)}, u32[]{:S(2)}, u32[]{:S(2)}) %collective-permute-start.7) | collective-permute-done | bytes 524320 | tf_op jit(solution)/shard_map/ppermute | solution.py:46
  126.9 6.7 %collective-permute-done.16 = bf16[4,24,2688]{2,1,0:T(8,128)(2,1)S(1)} collective-permute-done((bf16[4,24,2688]{2,1,0:T(8,128)(2,1)S(1)}, bf16[4,24,2688]{2,1,0:T(8,128)(2,1)S(1)}, u32[]{:S(2)}, u32[]{:S(2)}) %collective-permute-start.16) | collective-permute-done | bytes 516128 | tf_op jit(solution)/shard_map/ppermute | solution.py:46
  138.4 8.0 %mix_forward.2 = (bf16[512,2048]{1,0:T(8,128)(2,1)}, bf16[512,512]{1,0:T(8,128)(2,1)}, f32[512,512]{1,0:T(8,128)}, f32[512,512]{1,0:T(8,128)}) custom-call(s32[2]{0:T(128)} %pad_add_fusion.place_ref, bf16[128,2048]{1,0:T(8,128)(2,1)} %get-tuple-element.353.refs_0_, bf16[128,2048]{1,0:T(8,128)(2,1)} %copy-done.50, bf16[128,2048]{1,0:T(8,128)(2,1)} %copy-done.48, ...), custom_call_target="tpu_custom_call" | custom-call | flops 1000 | bytes 1000 | tf_op jit(solution)/shard_map/mix_forward/pallas_call | solution.py:291
  151.6 12.1 %collective-permute-done.10.refs_2_ = bf16[512,512]{1,0:T(8,128)(2,1)} collective-permute-done((bf16[512,512]{1,0:T(8,128)(2,1)}, bf16[512,512]{1,0:T(8,128)(2,1)}, u32[]{:S(2)}, u32[]{:S(2)}) %collective-permute-start.10) | collective-permute-done | bytes 524320 | tf_op jit(solution)/shard_map/ppermute | solution.py:46
  167.3 8.0 %mix_forward.3 = (bf16[512,2048]{1,0:T(8,128)(2,1)}, bf16[512,512]{1,0:T(8,128)(2,1)}, f32[512,512]{1,0:T(8,128)}, f32[512,512]{1,0:T(8,128)}) custom-call(s32[2]{0:T(128)} %pad_add_fusion.place_ref, bf16[512,512]{1,0:T(8,128)(2,1)} %get-tuple-element.130.refs_0_, bf16[512,512]{1,0:T(8,128)(2,1)} %collective-permute-done.9.refs_1_, ...), custom_call_target="tpu_custom_call" | custom-call | flops 1000 | bytes 1000 | tf_op jit(solution)/shard_map/mix_forward/pallas_call | solution.py:291
  188.2 6.0 %collective-permute-done.20 = bf16[1,128,768]{2,1,0:T(8,128)(2,1)S(1)} collective-permute-done((bf16[1,128,768]{2,1,0:T(8,128)(2,1)S(1)}, bf16[1,128,768]{2,1,0:T(8,128)(2,1)S(1)}, u32[]{:S(2)}, u32[]{:S(2)}) %collective-permute-start.20) | collective-permute-done | bytes 196640 | tf_op jit(solution)/shard_map/ppermute | solution.py:46
  195.2 8.0 %all_gather.22 = bf16[512,768]{1,0:T(8,128)(2,1)S(1)} all-gather(bf16[128,768]{1,0:T(8,128)(2,1)S(1)} %add_convert_fusion.5), channel_id=1, replica_groups=mesh['wide'=8,'narrow'=4] {'narrow'}, dimensions={0}, use_global_device_ids=true | all-gather | bytes 983040 | tf_op jit(solution)/shard_map/all_gather | solution.py:842
  212.5 4.2 collective-permute-done.22
  221.9 7.7 %ffn_forward.1 = (f32[512,768]{1,0:T(8,128)S(1)}, bf16[512,768]{1,0:T(8,128)(2,1)S(1)}) custom-call(bf16[512,768]{1,0:T(8,128)(2,1)S(1)} %fusion.27.x_ref, bf16[1744,768]{1,0:T(8,128)(2,1)} %pad_maximum_fusion.1.refs_0_, bf16[1744,768]{1,0:T(8,128)(2,1)} %collective-permute-done.5.refs_1_, bf16[1744,768]{1,0:T(8,128)(2,1)} %collective-permute-done.12.refs_2_, ...), custom_call_target="tpu_custom_call" | custom-call | flops 1000 | bytes 1000 | tf_op jit(solution)/shard_map/ffn_forward/pallas_call | solution.py:535
  236.9 10.9 %ffn_backward.1 = (f32[512,768]{1,0:T(8,128)S(1)}, bf16[512,768]{1,0:T(8,128)(2,1)S(1)}, f32[1,768]{1,0:T(1,128)S(1)}) custom-call(bf16[512,768]{1,0:T(8,128)(2,1)S(1)} %fusion.27.x_ref, bf16[512,768]{1,0:T(8,128)(2,1)S(1)} %get-tuple-element.338.grad_ref, bf16[1744,768]{1,0:T(8,128)(2,1)} %pad_maximum_fusion.1.refs_0_, ...), custom_call_target="tpu_custom_call" | custom-call | flops 1000 | bytes 1000 | tf_op jit(solution)/shard_map/ffn_backward/pallas_call | solution.py:535
  277.8 8.2 %all_gather.23 = bf16[512,768]{1,0:T(8,128)(2,1)S(1)} all-gather(bf16[128,768]{1,0:T(8,128)(2,1)S(1)} %get-tuple-element.340), channel_id=1, replica_groups=mesh['wide'=8,'narrow'=4] {'narrow'}, dimensions={0}, use_global_device_ids=true | all-gather | bytes 983040 | tf_op jit(solution)/shard_map/all_gather | solution.py:941
  304.9 4.4 all-to-all-start
  320.3 4.9 fusion.19
  337.6 7.0 %collective-permute-done.35 = bf16[1,512,512]{2,1,0:T(8,128)(2,1)} collective-permute-done((bf16[1,512,512]{2,1,0:T(8,128)(2,1)}, bf16[1,512,512]{2,1,0:T(8,128)(2,1)}, u32[]{:S(2)}, u32[]{:S(2)}) %collective-permute-start.35) | collective-permute-done | bytes 524320 | tf_op jit(solution)/shard_map/ppermute | solution.py:46
  368.5 4.9 inner_rows.1
  389.3 10.1 %collective-permute-done.37 = bf16[1,128,2048]{2,1,0:T(8,128)(2,1)} collective-permute-done((bf16[1,128,2048]{2,1,0:T(8,128)(2,1)S(1)}, bf16[1,128,2048]{2,1,0:T(8,128)(2,1)}, u32[]{:S(2)}, u32[]{:S(2)}) %collective-permute-start.37) | collective-permute-done | bytes 524320 | tf_op jit(solution)/shard_map/ppermute | solution.py:46
  406.7 25.3 %pool_backward.1 = (f32[2048,128]{1,0:T(8,128)S(1)}, f32[272,128]{1,0:T(8,128)S(1)}) custom-call(bf16[50,128,128]{2,1,0:T(8,128)(2,1)S(1)} %bitcast.397, bf16[128,6400]{1,0:T(8,128)(2,1)} %concatenate.53.cols_t_ref, bf16[272,6400]{1,0:T(8,128)(2,1)} %fusion.1.hot_ref, bf16[2048,128]{1,0:T(8,128)(2,1)S(1)} %copy-done.10, f32[128,2048]{1,0:T(8,128)S(1)} %copy-done.12, ...), custom_call_target="tpu_custom_call" | custom-call | flops 1000 | bytes 1000 | tf_op jit(solution)/shard_map/pool_backward/pallas_call | solution.py:206
  441.8 10.4 %collective-permute-done.51 = bf16[2,256,128]{2,1,0:T(8,128)(2,1)S(1)} collective-permute-done((bf16[2,256,128]{2,1,0:T(8,128)(2,1)S(1)}, bf16[2,256,128]{2,1,0:T(8,128)(2,1)S(1)}, u32[]{:S(2)}, u32[]{:S(2)}) %collective-permute-start.51) | collective-permute-done | bytes 131104 | tf_op jit(solution)/shard_map/ppermute | solution.py:46
  465.4 6.1 %all-to-all-start.1 = ((bf16[4,64,128]{2,1,0:T(8,128)(2,1)}), bf16[4,64,128]{2,1,0:T(8,128)(2,1)S(1)}, u32[]{:S(2)}, u32[]{:S(2)}) async-start(bf16[4,64,128]{2,1,0:T(8,128)(2,1)} %bitcast.150), calls=%async_computation.1 | async-start | bytes 131072 | tf_op jit(solution)/shard_map/all_to_all | solution.py:1051
  (647 shorter events, 265.0 us)
Async XLA Ops:
  7.3 81.5 %all-gather.5.cloned.1.call-start = ((), (), s32[]{:S(2)}) async-start(), calls=%async_computation.3 | async-start | bytes 4718592 | tf_op jit(solution)/shard_map/all_gather | solution.py:709
  9.7 156.9 %all-gather.9.cloned.1.call-start = ((), (), s32[]{:S(2)}) async-start(), calls=%async_computation.6 | async-start | bytes 4718592 | tf_op jit(solution)/shard_map/all_gather | solution.py:709
  17.6 31.2 %collective-permute-start.14 = (bf16[1,24,2688]{2,1,0:T(8,128)(2,1)S(1)}, bf16[1,24,2688]{2,1,0:T(8,128)(2,1)S(1)}, u32[]{:S(2)}, u32[]{:S(2)}) collective-permute-start(bf16[1,24,2688]{2,1,0:T(8,128)(2,1)S(1)} %fusion.79), channel_id=1, source_target_pairs={{0,16},{4,20},{8,24},{12,28},{16,0},{20,4},{24,8},{28,12},{1,17},{... | collective-permute-start | bytes 387080 | tf_op jit(solution)/shard_map/ppermute | solution.py:46
  20.6 77.0 %collective-permute-start.5 = (bf16[1744,768]{1,0:T(8,128)(2,1)}, bf16[1744,768]{1,0:T(8,128)(2,1)}, u32[]{:S(2)}, u32[]{:S(2)}) collective-permute-start(bf16[1744,768]{1,0:T(8,128)(2,1)} %pad_maximum_fusion.1.refs_0_), channel_id=1, source_target_pairs={{0,2},{1,3},{2,0},{3,1},{4,6},{5,7},{6,4},{7,5},{8,10},{9,11},{10,... | collective-permute-start | bytes 8036360 | tf_op jit(solution)/shard_map/ppermute | solution.py:46
  48.2 34.9 %collective-permute-start.3 = (bf16[8,66,128]{2,0,1:T(8,128)(2,1)S(1)}, bf16[8,66,128]{2,0,1:T(8,128)(2,1)S(1)}, u32[]{:S(2)}, u32[]{:S(2)}) collective-permute-start(bf16[8,66,128]{2,0,1:T(8,128)(2,1)S(1)} %bitcast.452), channel_id=1, source_target_pairs={{0,2},{1,3},{2,0},{3,1},{4,6},{5,7},{6,4},{7,5},{8,10},{9,11},{10,... | collective-permute-start | bytes 405512 | tf_op jit(solution)/shard_map/ppermute | solution.py:46
  88.8 105.5 %all-gather.7.cloned.1.call-start = ((), (), s32[]{:S(2)}) async-start(), calls=%async_computation.4 | async-start | bytes 1966080 | tf_op jit(solution)/shard_map/all_gather | solution.py:796
  146.4 20.8 %collective-permute-start.12 = (bf16[1744,768]{1,0:T(8,128)(2,1)}, bf16[1744,768]{1,0:T(8,128)(2,1)}, u32[]{:S(2)}, u32[]{:S(2)}) collective-permute-start(bf16[1744,768]{1,0:T(8,128)(2,1)} %pad_maximum_fusion.1.refs_0_), channel_id=1, source_target_pairs={{0,1},{1,0},{2,3},{3,2},{4,5},{5,4},{6,7},{7,6},{8,9},{9,8},{10,11... | collective-permute-start | bytes 8036360 | tf_op jit(solution)/shard_map/ppermute | solution.py:46
  146.6 20.7 %collective-permute-start.13 = (bf16[1744,768]{1,0:T(8,128)(2,1)}, bf16[1744,768]{1,0:T(8,128)(2,1)}, u32[]{:S(2)}, u32[]{:S(2)}) collective-permute-start(bf16[1744,768]{1,0:T(8,128)(2,1)} %collective-permute-done.5.refs_1_), channel_id=1, source_target_pairs={{0,1},{1,0},{2,3},{3,2},{4,5},{5,4},{6,7},{7,6},{8,9},{9,8},{10,11... | collective-permute-start | bytes 8036360 | tf_op jit(solution)/shard_map/ppermute | solution.py:46
  183.9 38.0 %collective-permute-start.24 = (bf16[128,2048]{1,0:T(8,128)(2,1)}, bf16[128,2048]{1,0:T(8,128)(2,1)}, u32[]{:S(2)}, u32[]{:S(2)}) collective-permute-start(bf16[128,2048]{1,0:T(8,128)(2,1)} %get-tuple-element.353.refs_0_), channel_id=1, source_target_pairs={{0,4},{4,0},{8,12},{12,8},{16,20},{20,16},{24,28},{28,24},{1,5},{5... | collective-permute-start | bytes 1572872 | tf_op jit(solution)/shard_map/ppermute | solution.py:46
  184.5 37.4 %collective-permute-start.25 = (bf16[512,512]{1,0:T(8,128)(2,1)}, bf16[512,512]{1,0:T(8,128)(2,1)}, u32[]{:S(2)}, u32[]{:S(2)}) collective-permute-start(bf16[512,512]{1,0:T(8,128)(2,1)} %get-tuple-element.130.refs_0_), channel_id=1, source_target_pairs={{0,4},{4,0},{8,12},{12,8},{16,20},{20,16},{24,28},{28,24},{1,5},{5... | collective-permute-start | bytes 1572872 | tf_op jit(solution)/shard_map/ppermute | solution.py:46
  229.6 23.6 %collective-permute-start.30 = (bf16[512,512]{1,0:T(8,128)(2,1)}, bf16[512,512]{1,0:T(8,128)(2,1)S(1)}, u32[]{:S(2)}, u32[]{:S(2)}) collective-permute-start(bf16[512,512]{1,0:T(8,128)(2,1)} %collective-permute-done.25), channel_id=1, source_target_pairs={{0,2},{1,3},{2,0},{3,1},{4,6},{5,7},{6,4},{7,5},{8,10},{9,11},{10,... | collective-permute-start | bytes 1572872 | tf_op jit(solution)/shard_map/ppermute | solution.py:46
  231.0 25.2 %collective-permute-start.29 = (bf16[512,512]{1,0:T(8,128)(2,1)}, bf16[512,512]{1,0:T(8,128)(2,1)S(1)}, u32[]{:S(2)}, u32[]{:S(2)}) collective-permute-start(bf16[512,512]{1,0:T(8,128)(2,1)} %collective-permute-done.25), channel_id=1, source_target_pairs={{0,1},{1,0},{2,3},{3,2},{4,5},{5,4},{6,7},{7,6},{8,9},{9,8},{10,11... | collective-permute-start | bytes 1572872 | tf_op jit(solution)/shard_map/ppermute | solution.py:46
  231.3 24.2 %collective-permute-start.27 = (bf16[128,2048]{1,0:T(8,128)(2,1)}, bf16[128,2048]{1,0:T(8,128)(2,1)S(1)}, u32[]{:S(2)}, u32[]{:S(2)}) collective-permute-start(bf16[128,2048]{1,0:T(8,128)(2,1)} %collective-permute-done.24), channel_id=1, source_target_pairs={{0,2},{1,3},{2,0},{3,1},{4,6},{5,7},{6,4},{7,5},{8,10},{9,11},{10,... | collective-permute-start | bytes 1572872 | tf_op jit(solution)/shard_map/ppermute | solution.py:46
  231.9 24.4 %collective-permute-start.26 = (bf16[128,2048]{1,0:T(8,128)(2,1)}, bf16[128,2048]{1,0:T(8,128)(2,1)}, u32[]{:S(2)}, u32[]{:S(2)}) collective-permute-start(bf16[128,2048]{1,0:T(8,128)(2,1)} %collective-permute-done.24), channel_id=1, source_target_pairs={{0,1},{1,0},{2,3},{3,2},{4,5},{5,4},{6,7},{7,6},{8,9},{9,8},{10,11... | collective-permute-start | bytes 1572872 | tf_op jit(solution)/shard_map/ppermute | solution.py:46
  251.8 37.7 %collective-permute-start.41 = (bf16[768,768]{1,0:T(8,128)(2,1)S(1)}, bf16[768,768]{1,0:T(8,128)(2,1)S(1)}, u32[]{:S(2)}, u32[]{:S(2)}) collective-permute-start(bf16[768,768]{1,0:T(8,128)(2,1)S(1)} %fusion.30), channel_id=1, source_target_pairs={{0,4},{4,0},{8,12},{12,8},{16,20},{20,16},{24,28},{28,24},{1,5},{5... | collective-permute-start | bytes 3538952 | tf_op jit(solution)/shard_map/ppermute | solution.py:46
  264.4 28.5 %collective-permute-start.42 = (bf16[384,768]{1,0:T(8,128)(2,1)S(1)}, bf16[384,768]{1,0:T(8,128)(2,1)S(1)}, u32[]{:S(2)}, u32[]{:S(2)}) collective-permute-start(bf16[384,768]{1,0:T(8,128)(2,1)S(1)} %dynamic-slice_bitcast_fusion), channel_id=1, source_target_pairs={{0,4},{4,0},{8,12},{12,8},{16,20},{20,16},{24,28},{28,24},{1,5},{5... | collective-permute-start | bytes 1769480 | tf_op jit(solution)/shard_map/ppermute | solution.py:46
  299.8 25.4 %collective-permute-start.34 = (bf16[2,512,512]{2,1,0:T(8,128)(2,1)}, bf16[2,512,512]{2,1,0:T(8,128)(2,1)}, u32[]{:S(2)}, u32[]{:S(2)}) collective-permute-start(bf16[2,512,512]{2,1,0:T(8,128)(2,1)} %inner_columns.3), channel_id=1, source_target_pairs={{0,1},{1,0},{2,3},{3,2},{4,5},{5,4},{6,7},{7,6},{8,9},{9,8},{10,11... | collective-permute-start | bytes 3145736 | tf_op jit(solution)/shard_map/ppermute | solution.py:46
  304.9 27.2 %all-to-all-start = ((bf16[4,8,24,1152]{3,2,1,0:T(8,128)(2,1)}), bf16[4,8,24,1152]{3,2,1,0:T(8,128)(2,1)}, u32[]{:S(2)}, u32[]{:S(2)}) async-start(bf16[4,8,24,1152]{3,2,1,0:T(8,128)(2,1)} %pad_maximum_fusion.3), calls=%async_computation | async-start | bytes 3538944 | tf_op jit(solution)/shard_map/all_to_all | solution.py:950
  309.3 91.3 %all-reduce.9.cloned.1.call-start = ((), (), s32[]{:S(2)}) async-start(), calls=%async_computation.7 | async-start | bytes 3538944 | tf_op jit(solution)/shard_map/psum | solution.py:974
  314.7 41.2 %collective-permute-start.39 = (bf16[512,512]{1,0:T(8,128)(2,1)}, bf16[512,512]{1,0:T(8,128)(2,1)}, u32[]{:S(2)}, u32[]{:S(2)}) collective-permute-start(bf16[512,512]{1,0:T(8,128)(2,1)} %get-tuple-element.381), channel_id=1, source_target_pairs={{0,4},{4,0},{8,12},{12,8},{16,20},{20,16},{24,28},{28,24},{1,5},{5... | collective-permute-start | bytes 1572872 | tf_op jit(solution)/shard_map/ppermute | solution.py:46
  320.1 174.2 %reduce-scatter.2.cloned.1.call-start = ((), (), s32[]{:S(2)}) async-start(), calls=%async_computation.5 | async-start | bytes 5898240 | tf_op jit(solution)/shard_map/reduce_scatter | solution.py:1003
  352.5 25.7 %collective-permute-start.38 = (bf16[512,512]{1,0:T(8,128)(2,1)}, bf16[512,512]{1,0:T(8,128)(2,1)}, u32[]{:S(2)}, u32[]{:S(2)}) collective-permute-start(bf16[512,512]{1,0:T(8,128)(2,1)} %get-tuple-element.380), channel_id=1, source_target_pairs={{0,4},{4,0},{8,12},{12,8},{16,20},{20,16},{24,28},{28,24},{1,5},{5... | collective-permute-start | bytes 1572872 | tf_op jit(solution)/shard_map/ppermute | solution.py:46
  441.5 38.4 %collective-permute-start.47 = (bf16[768,768]{1,0:T(8,128)(2,1)S(1)}, bf16[768,768]{1,0:T(8,128)(2,1)}, u32[]{:S(2)}, u32[]{:S(2)}) collective-permute-start(bf16[768,768]{1,0:T(8,128)(2,1)S(1)} %copy-done.39), channel_id=1, source_target_pairs={{0,4},{4,0},{8,12},{12,8},{16,20},{20,16},{24,28},{28,24},{1,5},{5... | collective-permute-start | bytes 3538952 | tf_op jit(solution)/shard_map/ppermute | solution.py:46
  458.7 21.2 %collective-permute-start.48 = (bf16[384,768]{1,0:T(8,128)(2,1)S(1)}, bf16[384,768]{1,0:T(8,128)(2,1)S(1)}, u32[]{:S(2)}, u32[]{:S(2)}) collective-permute-start(bf16[384,768]{1,0:T(8,128)(2,1)S(1)} %copy-done.45), channel_id=1, source_target_pairs={{0,4},{4,0},{8,12},{12,8},{16,20},{20,16},{24,28},{28,24},{1,5},{5... | collective-permute-start | bytes 1769480 | tf_op jit(solution)/shard_map/ppermute | solution.py:46
  (163 other events, 1521.0 us)
Sparse Core Ops, SparseCore 0:
  10.9 77.8 all-gather.4
  90.9 75.5 all-gather.8
  168.1 17.3 all-gather.6
  320.2 78.1 all-reduce.8
  400.8 93.4 reduce-scatter.1

commit v5 on v4

--- a/solution.py
+++ b/solution.py
@@ -824,7 +824,12 @@
             encoder_parts = encoder_parts + [
                 swap(item, "narrow", 0) for item in after(encoder_parts, hidden)
             ]
-            parts, encoder_parts, rest = lax.optimization_barrier((parts, encoder_parts, rest))
+            encoder_vectors = [
+                full(item) for item in (out_bias, ln1_gain, ln1_shift, down_bias, ln2_gain, ln2_shift, qv_bias)
+            ]
+            parts, encoder_parts, rest, encoder_vectors = lax.optimization_barrier(
+                (parts, encoder_parts, rest, encoder_vectors)
+            )
     proj_input = hidden
     rest = rest.reshape(n_wide * n_narrow * own_width, -1)
     model_width = rest.shape[0]
@@ -839,15 +844,16 @@
     summed = projected + proj_shift + dot_nt(position_hot, position_rows) + type_rows
     first_state, first_pull = jax.vjp(layer_norm, summed, first_gain, first_shift)
 
+    out_bias, ln1_gain, ln1_shift, down_bias, ln2_gain, ln2_shift, qv_bias = encoder_vectors
     gathered = lax.all_gather(low(first_state), "narrow", axis=0, tiled=True)
     group_rows = gathered.shape[0]
     qkv_out = jnp.einsum("gd,kdc->kgc", gathered, qkv_weight, preferred_element_type=jnp.float32)
     local_width = qkv_out.shape[2]
     head_count = local_width // HEAD_DIM
     seq_shape = (group_rows, head_count, HEAD_DIM)
-    query_heads = low(qkv_out[0] + full(qv_bias[0])).reshape(seq_shape)
+    query_heads = low(qkv_out[0] + qv_bias[0]).reshape(seq_shape)
     key_heads = low(qkv_out[1]).reshape(seq_shape)
-    value_heads = low(qkv_out[2] + full(qv_bias[1])).reshape(seq_shape)
+    value_heads = low(qkv_out[2] + qv_bias[1]).reshape(seq_shape)
     score_scale = HEAD_DIM ** (-0.5)
     keep_mask = key_mask[0]
     context, row_peak, row_total = attend(query_heads, key_heads, value_heads, keep_mask, score_scale)
@@ -859,17 +865,17 @@
     def own_words(rows):
         return lax.dynamic_slice_in_dim(rows, me_narrow * word_total, word_total, 0)
 
-    attn_branch = full(out_bias)
+    attn_branch = out_bias
     for k, part in zip(near_order, near_parts(context_rows, "narrow")):
         weight = encoder_parts[k][2 * units : 2 * units + local_width]
         attn_branch = attn_branch + jnp.dot(part, weight, preferred_element_type=jnp.float32)
     second_state, second_pull = jax.vjp(
-        layer_norm, full(gathered) + attn_branch, full(ln1_gain), full(ln1_shift)
+        layer_norm, full(gathered) + attn_branch, ln1_gain, ln1_shift
     )
     pair_parts, ffn_input = lax.optimization_barrier((pair_parts, low(second_state)))
     ffn_branch, activated = ffn_forward(ffn_input, encoder_parts, units)
     layer_out, third_pull = jax.vjp(
-        layer_norm, second_state + (ffn_branch + full(down_bias)), full(ln2_gain), full(ln2_shift)
+        layer_norm, second_state + (ffn_branch + down_bias), ln2_gain, ln2_shift
     )
     layer_out = own_words(layer_out)
 
@@ -942,9 +948,36 @@
     grad_proj_weight = jnp.einsum(
         "gd,gh->dh", grad_proj_rows, proj_input, preferred_element_type=jnp.float32
     )
+    grad_hidden = jnp.dot(grad_proj_rows, proj_own, preferred_element_type=jnp.float32)
+
+    mix_bias_grads = [None, None]
+
+    def weight_part(joined, mixed):
+        return jnp.einsum(
+            "tk,tzc->zck",
+            joined,
+            mixed.reshape(group, outer, own_mix),
+            preferred_element_type=jnp.float32,
+        )
+
+    def pair_weight(layer_index, mixed, met):
+        joined = highway_saved[layer_index][0]
+        return low(weight_part(joined, mixed[0]) + weight_part(pair_joined[layer_index], met))
+
+    ffn_received, attn_received = after((ffn_received, attn_received), grad_hidden)
+    pair_sums = lax.psum(
+        (low(full(ffn_kept) + full(ffn_received)), low(full(attn_kept) + full(attn_received))),
+        "wide",
+        axis_index_groups=outer_groups,
+    )
+    joined, kept_a, kept_t = highway_saved[1]
+    mixed, direct, mix_bias_grads[1] = mix_back(corner, grad_hidden, kept_a, kept_t, joined, n_narrow, False)
+    met = swap(mixed[1], "wide", 0)
+    sent = inner_columns(corner, mixed, mix_weights[1], 1, n_narrow, jnp.bfloat16)
+    kept = inner_columns(corner, mixed, mix_weights[1], 0, n_narrow, jnp.float32)
     table_grads = [
         item.reshape(n_wide, n_narrow, own_width, -1).transpose(1, 0, 2, 3)
-        for item in (low(grad_position), vector_grads, low(grad_proj_weight))
+        for item in after((low(grad_position), vector_grads, low(grad_proj_weight)), kept)
     ]
     table_grads = jnp.concatenate(table_grads, axis=3)
     table_grads = lax.all_to_all(table_grads, "narrow", 0, 0, tiled=True)
@@ -954,33 +987,6 @@
     rest_grads = [item.reshape(n_wide, LANES, -1) for item in (low(table_sums), proj_parts)]
     table_columns = rest_grads[0].shape[2]
     rest_grads = jnp.concatenate(rest_grads, axis=2)
-    grad_hidden = jnp.dot(grad_proj_rows, proj_own, preferred_element_type=jnp.float32)
-
-    mix_bias_grads = [None, None]
-
-    def weight_part(joined, mixed):
-        return jnp.einsum(
-            "tk,tzc->zck",
-            joined,
-            mixed.reshape(group, outer, own_mix),
-            preferred_element_type=jnp.float32,
-        )
-
-    def pair_weight(layer_index, mixed, met):
-        joined = highway_saved[layer_index][0]
-        return low(weight_part(joined, mixed[0]) + weight_part(pair_joined[layer_index], met))
-
-    ffn_received, attn_received = after((ffn_received, attn_received), grad_hidden)
-    pair_sums = lax.psum(
-        (low(full(ffn_kept) + full(ffn_received)), low(full(attn_kept) + full(attn_received))),
-        "wide",
-        axis_index_groups=outer_groups,
-    )
-    joined, kept_a, kept_t = highway_saved[1]
-    mixed, direct, mix_bias_grads[1] = mix_back(corner, grad_hidden, kept_a, kept_t, joined, n_narrow, False)
-    met = swap(mixed[1], "wide", 0)
-    sent = inner_columns(corner, mixed, mix_weights[1], 1, n_narrow, jnp.bfloat16)
-    kept = inner_columns(corner, mixed, mix_weights[1], 0, n_narrow, jnp.float32)
     grad_hidden = direct + fold_near(sent, kept, "narrow")
     weight_second = pair_weight(1, mixed, after(met, grad_hidden))
     joined, kept_a, kept_t = highway_saved[0]
@@ -989,7 +995,7 @@
     sent, kept = inner_rows(corner, mixed, mix_weights[0], direct, n_narrow, plain)
     grad_features = fold_near(sent, kept, "narrow")
 
-    rest_grads = low(halved(after(rest_grads, direct), *wide_bits[0]))
+    rest_grads = low(halved(rest_grads, *wide_bits[0]))
     weight_first = pair_weight(0, mixed, met)
     both = [item.reshape(outer, LANES, -1) for item in (weight_first, weight_second)]
     weight_columns = both[0].shape[2]

time: 515 us -> 510 us (level)
  other arithmetic: 72.6 us -> 80.8 us
  local copies, waits for them, and re-layouts: 66.9 us -> 59.6 us
    ppermute x53, waiting for transfers between devices: 133 us -> 125 us  [swap(): return lax.ppermute(block, axis, [(i, i ^ 1 << bit) for i in range(size)])]
    convert_element_type x10 -> x11, other arithmetic: 8.27 us -> 12.3 us  [full(): return values.astype(jnp.float32)]
    unnamed x269 -> x256, local copies, waits for them, and re-layouts: 17.6 us -> 14.7 us
  transfers between devices with their start and end apart: 60 -> 60, of which waited for: 27 -> 26; matrix products, arithmetic and copies ran while one was open for 31% -> 33% of each run, Pallas kernels for 15% -> 16%
where the time goes in v5:
time: 510 us; the launch traced here: 503 us
  waiting for transfers between devices  142 us (28%)
  Pallas kernels  89.9 us (18%)
  other arithmetic  80.8 us (16%)
  local copies, waits for them, and re-layouts  59.6 us (12%)
  starting transfers between devices  54.2 us (11%)
  matrix products  44.3 us (9%)
  between operations  16.6 us (3%)
  blocking collectives  16.1 us (3%)
    ppermute x53, waiting for transfers between devices, swap(): return lax.ppermute(block, axis, [(i, i ^ 1 << bit) for i in range(size)])  125 us
    ppermute x53, starting transfers between devices, swap(): return lax.ppermute(block, axis, [(i, i ^ 1 << bit) for i in range(size)])  46 us
    pallas_call x1, Pallas kernels, pool_backward(): pl.pallas_call(functools.partial(back_kernel, depth=depth, taps=taps), gr...  25.3 us
    pallas_call x2, Pallas kernels, ffn_call(): pl.pallas_call(kernel, in_specs=[vmem] * len(operands) + [pl.BlockSpec(me...  18.6 us
    pallas_call x2, Pallas kernels, mix_forward(): pl.pallas_call(functools.partial(mix_kernel, parts=len(parts), by_rows=by...  16 us
    unnamed x256, local copies, waits for them, and re-layouts  14.7 us
    pallas_call x1, Pallas kernels, pool_forward(): pl.pallas_call(functools.partial(pool_kernel, group=5), grid=(filters //...  13.8 us
    convert_element_type x11, other arithmetic, full(): return values.astype(jnp.float32)  12.3 us
  transfers between devices with their start and end apart: 60, of which 26 were waited for; matrix products, arithmetic and copies ran while one was open for 33% of the time, Pallas kernels for 16%

profile of v5, /device:TPU:0, one launch (start us, length us, event | category | flops | bytes accessed | tf_op | source)
XLA Modules:
  0.0 503.1 jit_solution(7486249330881853071)
XLA Ops:
  13.2 4.0 collective-permute-start
  32.3 6.4 %concatenate.58.cols_t_ref = bf16[128,6400]{1,0:T(8,128)(2,1)} concatenate(bf16[16,6400]{1,0:T(8,128)(2,1)S(1)} %convolution_convert_fusion, bf16[16,6400]{1,0:T(8,128)(2,1)S(1)} %get-tuple-element.420, bf16[16,6400]{1,0:T(8,128)(2,1)S(1)} %get-tuple-element.416, bf16[16,6400]{1,0:T(8,128)(2,1)S(1)} %get-tuple-element.417, bf16[16,6400]{1,0:T(8,128)(2,1)S(1)} %get-tuple-element.418, ...), dimensions={0} | concatenate | bytes 3276800 | tf_op jit(solution)/shard_map/concatenate | solution.py:761
  48.9 34.3 %collective-permute-done.3 = bf16[8,66,128]{2,0,1:T(8,128)(2,1)S(1)} collective-permute-done((bf16[8,66,128]{2,0,1:T(8,128)(2,1)S(1)}, bf16[8,66,128]{2,0,1:T(8,128)(2,1)S(1)}, u32[]{:S(2)}, u32[]{:S(2)}) %collective-permute-start.3) | collective-permute-done | bytes 135200 | tf_op jit(solution)/shard_map/ppermute | solution.py:46
  83.6 5.2 %all-gather.5.cloned.1.call-done.refs_4_.refs_5_.refs_0_.refs_1_.refs_2_.refs_3_.refs_6_.refs_7_ = bf16[8,2048,128]{2,1,0:T(8,128)(2,1)} async-done(((bf16[1,2048,128]{2,1,0:T(8,128)(2,1)}), bf16[8,2048,128]{2,1,0:T(8,128)(2,1)}) %all-gather.5.cloned.1.call-update) | async-done | bytes 4194320 | tf_op jit(solution)/shard_map/all_gather | solution.py:709
  92.5 5.0 collective-permute-done.15
  97.6 13.8 %pool_forward.1.lse_ref = f32[128,2048]{1,0:T(8,128)S(1)} custom-call(bf16[50,128,128]{2,1,0:T(8,128)(2,1)S(1)} %bitcast.399, bf16[2048,128]{1,0:T(8,128)(2,1)S(1)} %fusion.50.filt_ref), custom_call_target="tpu_custom_call" | custom-call | flops 1000 | bytes 1000 | tf_op jit(solution)/shard_map/pool_forward/pallas_call | solution.py:150
  117.3 9.6 %collective-permute-done.7.refs_2_ = bf16[128,2048]{1,0:T(8,128)(2,1)S(1)} collective-permute-done((bf16[128,2048]{1,0:T(8,128)(2,1)}, bf16[128,2048]{1,0:T(8,128)(2,1)S(1)}, u32[]{:S(2)}, u32[]{:S(2)}) %collective-permute-start.7) | collective-permute-done | bytes 524320 | tf_op jit(solution)/shard_map/ppermute | solution.py:46
  126.9 6.7 %collective-permute-done.16 = bf16[4,24,2688]{2,1,0:T(8,128)(2,1)S(1)} collective-permute-done((bf16[4,24,2688]{2,1,0:T(8,128)(2,1)S(1)}, bf16[4,24,2688]{2,1,0:T(8,128)(2,1)S(1)}, u32[]{:S(2)}, u32[]{:S(2)}) %collective-permute-start.16) | collective-permute-done | bytes 516128 | tf_op jit(solution)/shard_map/ppermute | solution.py:46
  138.4 8.0 %mix_forward.2 = (bf16[512,2048]{1,0:T(8,128)(2,1)}, bf16[512,512]{1,0:T(8,128)(2,1)}, f32[512,512]{1,0:T(8,128)}, f32[512,512]{1,0:T(8,128)}) custom-call(s32[2]{0:T(128)} %pad_add_fusion.place_ref, bf16[128,2048]{1,0:T(8,128)(2,1)} %get-tuple-element.371.refs_0_, bf16[128,2048]{1,0:T(8,128)(2,1)} %copy-done.52, bf16[128,2048]{1,0:T(8,128)(2,1)} %copy-done.50, ...), custom_call_target="tpu_custom_call" | custom-call | flops 1000 | bytes 1000 | tf_op jit(solution)/shard_map/mix_forward/pallas_call | solution.py:291
  157.9 5.8 %collective-permute-done.10.refs_2_ = bf16[512,512]{1,0:T(8,128)(2,1)} collective-permute-done((bf16[512,512]{1,0:T(8,128)(2,1)}, bf16[512,512]{1,0:T(8,128)(2,1)}, u32[]{:S(2)}, u32[]{:S(2)}) %collective-permute-start.10) | collective-permute-done | bytes 524320 | tf_op jit(solution)/shard_map/ppermute | solution.py:46
  167.3 8.0 %mix_forward.3 = (bf16[512,2048]{1,0:T(8,128)(2,1)}, bf16[512,512]{1,0:T(8,128)(2,1)}, f32[512,512]{1,0:T(8,128)}, f32[512,512]{1,0:T(8,128)}) custom-call(s32[2]{0:T(128)} %pad_add_fusion.place_ref, bf16[512,512]{1,0:T(8,128)(2,1)} %get-tuple-element.139.refs_0_, bf16[512,512]{1,0:T(8,128)(2,1)} %collective-permute-done.9.refs_1_, ...), custom_call_target="tpu_custom_call" | custom-call | flops 1000 | bytes 1000 | tf_op jit(solution)/shard_map/mix_forward/pallas_call | solution.py:291
  186.7 4.2 collective-permute-done.20
  194.4 7.8 %all_gather.22 = bf16[512,768]{1,0:T(8,128)(2,1)S(1)} all-gather(bf16[128,768]{1,0:T(8,128)(2,1)S(1)} %add_convert_fusion.5), channel_id=1, replica_groups=mesh['wide'=8,'narrow'=4] {'narrow'}, dimensions={0}, use_global_device_ids=true | all-gather | bytes 983040 | tf_op jit(solution)/shard_map/all_gather | solution.py:848
  212.3 4.1 collective-permute-done.22
  221.5 7.7 %ffn_forward.1 = (f32[512,768]{1,0:T(8,128)S(1)}, bf16[512,768]{1,0:T(8,128)(2,1)S(1)}) custom-call(bf16[512,768]{1,0:T(8,128)(2,1)S(1)} %fusion.27.x_ref, bf16[1744,768]{1,0:T(8,128)(2,1)} %pad_maximum_fusion.1.refs_0_, bf16[1744,768]{1,0:T(8,128)(2,1)} %collective-permute-done.5.refs_1_, bf16[1744,768]{1,0:T(8,128)(2,1)} %collective-permute-done.12.refs_2_, ...), custom_call_target="tpu_custom_call" | custom-call | flops 1000 | bytes 1000 | tf_op jit(solution)/shard_map/ffn_forward/pallas_call | solution.py:535
  236.5 10.9 %ffn_backward.1 = (f32[512,768]{1,0:T(8,128)S(1)}, bf16[512,768]{1,0:T(8,128)(2,1)S(1)}, f32[1,768]{1,0:T(1,128)S(1)}) custom-call(bf16[512,768]{1,0:T(8,128)(2,1)S(1)} %fusion.27.x_ref, bf16[512,768]{1,0:T(8,128)(2,1)S(1)} %get-tuple-element.356.grad_ref, bf16[1744,768]{1,0:T(8,128)(2,1)} %pad_maximum_fusion.1.refs_0_, ...), custom_call_target="tpu_custom_call" | custom-call | flops 1000 | bytes 1000 | tf_op jit(solution)/shard_map/ffn_backward/pallas_call | solution.py:535
  277.3 8.3 %all_gather.23 = bf16[512,768]{1,0:T(8,128)(2,1)S(1)} all-gather(bf16[128,768]{1,0:T(8,128)(2,1)S(1)} %get-tuple-element.358), channel_id=1, replica_groups=mesh['wide'=8,'narrow'=4] {'narrow'}, dimensions={0}, use_global_device_ids=true | all-gather | bytes 983040 | tf_op jit(solution)/shard_map/all_gather | solution.py:947
  307.2 4.4 all-to-all-start
  319.0 4.9 fusion.19
  360.9 4.9 inner_rows.1
  381.2 11.8 %collective-permute-done.37 = bf16[1,128,2048]{2,1,0:T(8,128)(2,1)} collective-permute-done((bf16[1,128,2048]{2,1,0:T(8,128)(2,1)S(1)}, bf16[1,128,2048]{2,1,0:T(8,128)(2,1)}, u32[]{:S(2)}, u32[]{:S(2)}) %collective-permute-start.37) | collective-permute-done | bytes 524320 | tf_op jit(solution)/shard_map/ppermute | solution.py:46
  402.0 25.3 %pool_backward.1 = (f32[2048,128]{1,0:T(8,128)S(1)}, f32[272,128]{1,0:T(8,128)S(1)}) custom-call(bf16[50,128,128]{2,1,0:T(8,128)(2,1)S(1)} %bitcast.400, bf16[128,6400]{1,0:T(8,128)(2,1)} %concatenate.58.cols_t_ref, bf16[272,6400]{1,0:T(8,128)(2,1)} %fusion.1.hot_ref, bf16[2048,128]{1,0:T(8,128)(2,1)S(1)} %copy-done.9, f32[128,2048]{1,0:T(8,128)S(1)} %copy-done.11, ...), custom_call_target="tpu_custom_call" | custom-call | flops 1000 | bytes 1000 | tf_op jit(solution)/shard_map/pool_backward/pallas_call | solution.py:206
  438.2 9.1 %collective-permute-done.51 = bf16[2,256,128]{2,1,0:T(8,128)(2,1)S(1)} collective-permute-done((bf16[2,256,128]{2,1,0:T(8,128)(2,1)S(1)}, bf16[2,256,128]{2,1,0:T(8,128)(2,1)S(1)}, u32[]{:S(2)}, u32[]{:S(2)}) %collective-permute-start.51) | collective-permute-done | bytes 131104 | tf_op jit(solution)/shard_map/ppermute | solution.py:46
  467.0 9.4 %collective-permute-done.48 = bf16[384,768]{1,0:T(8,128)(2,1)S(1)} collective-permute-done((bf16[384,768]{1,0:T(8,128)(2,1)S(1)}, bf16[384,768]{1,0:T(8,128)(2,1)S(1)}, u32[]{:S(2)}, u32[]{:S(2)}) %collective-permute-start.48) | collective-permute-done | bytes 589856 | tf_op jit(solution)/shard_map/ppermute | solution.py:46
  (633 shorter events, 267.1 us)
Async XLA Ops:
  7.3 81.5 %all-gather.5.cloned.1.call-start = ((), (), s32[]{:S(2)}) async-start(), calls=%async_computation.3 | async-start | bytes 4718592 | tf_op jit(solution)/shard_map/all_gather | solution.py:709
  9.7 156.9 %all-gather.9.cloned.1.call-start = ((), (), s32[]{:S(2)}) async-start(), calls=%async_computation.6 | async-start | bytes 4718592 | tf_op jit(solution)/shard_map/all_gather | solution.py:709
  17.6 31.2 %collective-permute-start.14 = (bf16[1,24,2688]{2,1,0:T(8,128)(2,1)S(1)}, bf16[1,24,2688]{2,1,0:T(8,128)(2,1)S(1)}, u32[]{:S(2)}, u32[]{:S(2)}) collective-permute-start(bf16[1,24,2688]{2,1,0:T(8,128)(2,1)S(1)} %fusion.83), channel_id=1, source_target_pairs={{0,16},{4,20},{8,24},{12,28},{16,0},{20,4},{24,8},{28,12},{1,17},{... | collective-permute-start | bytes 387080 | tf_op jit(solution)/shard_map/ppermute | solution.py:46
  20.6 77.0 %collective-permute-start.5 = (bf16[1744,768]{1,0:T(8,128)(2,1)}, bf16[1744,768]{1,0:T(8,128)(2,1)}, u32[]{:S(2)}, u32[]{:S(2)}) collective-permute-start(bf16[1744,768]{1,0:T(8,128)(2,1)} %pad_maximum_fusion.1.refs_0_), channel_id=1, source_target_pairs={{0,2},{1,3},{2,0},{3,1},{4,6},{5,7},{6,4},{7,5},{8,10},{9,11},{10,... | collective-permute-start | bytes 8036360 | tf_op jit(solution)/shard_map/ppermute | solution.py:46
  48.3 34.9 %collective-permute-start.3 = (bf16[8,66,128]{2,0,1:T(8,128)(2,1)S(1)}, bf16[8,66,128]{2,0,1:T(8,128)(2,1)S(1)}, u32[]{:S(2)}, u32[]{:S(2)}) collective-permute-start(bf16[8,66,128]{2,0,1:T(8,128)(2,1)S(1)} %bitcast.453), channel_id=1, source_target_pairs={{0,2},{1,3},{2,0},{3,1},{4,6},{5,7},{6,4},{7,5},{8,10},{9,11},{10,... | collective-permute-start | bytes 405512 | tf_op jit(solution)/shard_map/ppermute | solution.py:46
  88.8 103.7 %all-gather.7.cloned.1.call-start = ((), (), s32[]{:S(2)}) async-start(), calls=%async_computation.4 | async-start | bytes 1966080 | tf_op jit(solution)/shard_map/all_gather | solution.py:796
  146.4 20.8 %collective-permute-start.12 = (bf16[1744,768]{1,0:T(8,128)(2,1)}, bf16[1744,768]{1,0:T(8,128)(2,1)}, u32[]{:S(2)}, u32[]{:S(2)}) collective-permute-start(bf16[1744,768]{1,0:T(8,128)(2,1)} %pad_maximum_fusion.1.refs_0_), channel_id=1, source_target_pairs={{0,1},{1,0},{2,3},{3,2},{4,5},{5,4},{6,7},{7,6},{8,9},{9,8},{10,11... | collective-permute-start | bytes 8036360 | tf_op jit(solution)/shard_map/ppermute | solution.py:46
  146.6 20.7 %collective-permute-start.13 = (bf16[1744,768]{1,0:T(8,128)(2,1)}, bf16[1744,768]{1,0:T(8,128)(2,1)}, u32[]{:S(2)}, u32[]{:S(2)}) collective-permute-start(bf16[1744,768]{1,0:T(8,128)(2,1)} %collective-permute-done.5.refs_1_), channel_id=1, source_target_pairs={{0,1},{1,0},{2,3},{3,2},{4,5},{5,4},{6,7},{7,6},{8,9},{9,8},{10,11... | collective-permute-start | bytes 8036360 | tf_op jit(solution)/shard_map/ppermute | solution.py:46
  178.8 42.7 %collective-permute-start.24 = (bf16[128,2048]{1,0:T(8,128)(2,1)}, bf16[128,2048]{1,0:T(8,128)(2,1)}, u32[]{:S(2)}, u32[]{:S(2)}) collective-permute-start(bf16[128,2048]{1,0:T(8,128)(2,1)} %get-tuple-element.371.refs_0_), channel_id=1, source_target_pairs={{0,4},{4,0},{8,12},{12,8},{16,20},{20,16},{24,28},{28,24},{1,5},{5... | collective-permute-start | bytes 1572872 | tf_op jit(solution)/shard_map/ppermute | solution.py:46
  179.3 42.2 %collective-permute-start.25 = (bf16[512,512]{1,0:T(8,128)(2,1)}, bf16[512,512]{1,0:T(8,128)(2,1)}, u32[]{:S(2)}, u32[]{:S(2)}) collective-permute-start(bf16[512,512]{1,0:T(8,128)(2,1)} %get-tuple-element.139.refs_0_), channel_id=1, source_target_pairs={{0,4},{4,0},{8,12},{12,8},{16,20},{20,16},{24,28},{28,24},{1,5},{5... | collective-permute-start | bytes 1572872 | tf_op jit(solution)/shard_map/ppermute | solution.py:46
  229.3 24.0 %collective-permute-start.30 = (bf16[512,512]{1,0:T(8,128)(2,1)}, bf16[512,512]{1,0:T(8,128)(2,1)S(1)}, u32[]{:S(2)}, u32[]{:S(2)}) collective-permute-start(bf16[512,512]{1,0:T(8,128)(2,1)} %collective-permute-done.25), channel_id=1, source_target_pairs={{0,2},{1,3},{2,0},{3,1},{4,6},{5,7},{6,4},{7,5},{8,10},{9,11},{10,... | collective-permute-start | bytes 1572872 | tf_op jit(solution)/shard_map/ppermute | solution.py:46
  230.8 24.5 %collective-permute-start.29 = (bf16[512,512]{1,0:T(8,128)(2,1)}, bf16[512,512]{1,0:T(8,128)(2,1)S(1)}, u32[]{:S(2)}, u32[]{:S(2)}) collective-permute-start(bf16[512,512]{1,0:T(8,128)(2,1)} %collective-permute-done.25), channel_id=1, source_target_pairs={{0,1},{1,0},{2,3},{3,2},{4,5},{5,4},{6,7},{7,6},{8,9},{9,8},{10,11... | collective-permute-start | bytes 1572872 | tf_op jit(solution)/shard_map/ppermute | solution.py:46
  231.1 24.0 %collective-permute-start.27 = (bf16[128,2048]{1,0:T(8,128)(2,1)}, bf16[128,2048]{1,0:T(8,128)(2,1)S(1)}, u32[]{:S(2)}, u32[]{:S(2)}) collective-permute-start(bf16[128,2048]{1,0:T(8,128)(2,1)} %collective-permute-done.24), channel_id=1, source_target_pairs={{0,2},{1,3},{2,0},{3,1},{4,6},{5,7},{6,4},{7,5},{8,10},{9,11},{10,... | collective-permute-start | bytes 1572872 | tf_op jit(solution)/shard_map/ppermute | solution.py:46
  231.6 23.8 %collective-permute-start.26 = (bf16[128,2048]{1,0:T(8,128)(2,1)}, bf16[128,2048]{1,0:T(8,128)(2,1)}, u32[]{:S(2)}, u32[]{:S(2)}) collective-permute-start(bf16[128,2048]{1,0:T(8,128)(2,1)} %collective-permute-done.24), channel_id=1, source_target_pairs={{0,1},{1,0},{2,3},{3,2},{4,5},{5,4},{6,7},{7,6},{8,9},{9,8},{10,11... | collective-permute-start | bytes 1572872 | tf_op jit(solution)/shard_map/ppermute | solution.py:46
  251.7 47.1 %collective-permute-start.41 = (bf16[768,768]{1,0:T(8,128)(2,1)S(1)}, bf16[768,768]{1,0:T(8,128)(2,1)}, u32[]{:S(2)}, u32[]{:S(2)}) collective-permute-start(bf16[768,768]{1,0:T(8,128)(2,1)S(1)} %fusion.30), channel_id=1, source_target_pairs={{0,4},{4,0},{8,12},{12,8},{16,20},{20,16},{24,28},{28,24},{1,5},{5... | collective-permute-start | bytes 3538952 | tf_op jit(solution)/shard_map/ppermute | solution.py:46
  265.1 33.6 %collective-permute-start.42 = (bf16[384,768]{1,0:T(8,128)(2,1)S(1)}, bf16[384,768]{1,0:T(8,128)(2,1)S(1)}, u32[]{:S(2)}, u32[]{:S(2)}) collective-permute-start(bf16[384,768]{1,0:T(8,128)(2,1)S(1)} %dynamic-slice_bitcast_fusion), channel_id=1, source_target_pairs={{0,4},{4,0},{8,12},{12,8},{16,20},{20,16},{24,28},{28,24},{1,5},{5... | collective-permute-start | bytes 1769480 | tf_op jit(solution)/shard_map/ppermute | solution.py:46
  299.6 24.3 %collective-permute-start.34 = (bf16[2,512,512]{2,1,0:T(8,128)(2,1)}, bf16[2,512,512]{2,1,0:T(8,128)(2,1)}, u32[]{:S(2)}, u32[]{:S(2)}) collective-permute-start(bf16[2,512,512]{2,1,0:T(8,128)(2,1)} %inner_columns.3), channel_id=1, source_target_pairs={{0,1},{1,0},{2,3},{3,2},{4,5},{5,4},{6,7},{7,6},{8,9},{9,8},{10,11... | collective-permute-start | bytes 3145736 | tf_op jit(solution)/shard_map/ppermute | solution.py:46
  307.2 27.1 %all-to-all-start = ((bf16[4,8,24,1152]{3,2,1,0:T(8,128)(2,1)}), bf16[4,8,24,1152]{3,2,1,0:T(8,128)(2,1)}, u32[]{:S(2)}, u32[]{:S(2)}) async-start(bf16[4,8,24,1152]{3,2,1,0:T(8,128)(2,1)} %pad_maximum_fusion.3), calls=%async_computation | async-start | bytes 3538944 | tf_op jit(solution)/shard_map/all_to_all | solution.py:983
  311.6 84.3 %all-reduce.9.cloned.1.call-start = ((), (), s32[]{:S(2)}) async-start(), calls=%async_computation.7 | async-start | bytes 3538944 | tf_op jit(solution)/shard_map/psum | solution.py:968
  312.7 42.6 %collective-permute-start.39 = (bf16[512,512]{1,0:T(8,128)(2,1)}, bf16[512,512]{1,0:T(8,128)(2,1)}, u32[]{:S(2)}, u32[]{:S(2)}) collective-permute-start(bf16[512,512]{1,0:T(8,128)(2,1)} %get-tuple-element.399), channel_id=1, source_target_pairs={{0,4},{4,0},{8,12},{12,8},{16,20},{20,16},{24,28},{28,24},{1,5},{5... | collective-permute-start | bytes 1572872 | tf_op jit(solution)/shard_map/ppermute | solution.py:46
  318.7 170.1 %reduce-scatter.2.cloned.1.call-start = ((), (), s32[]{:S(2)}) async-start(), calls=%async_computation.5 | async-start | bytes 5898240 | tf_op jit(solution)/shard_map/reduce_scatter | solution.py:1009
  339.6 29.2 %collective-permute-start.40 = (bf16[4,128,504]{2,1,0:T(8,128)(2,1)}, bf16[4,128,504]{2,1,0:T(8,128)(2,1)}, u32[]{:S(2)}, u32[]{:S(2)}) collective-permute-start(bf16[4,128,504]{2,1,0:T(8,128)(2,1)} %fusion.62), channel_id=1, source_target_pairs={{0,4},{4,0},{8,12},{12,8},{16,20},{20,16},{24,28},{28,24},{1,5},{5... | collective-permute-start | bytes 1548296 | tf_op jit(solution)/shard_map/ppermute | solution.py:46
  437.5 38.9 %collective-permute-start.47 = (bf16[768,768]{1,0:T(8,128)(2,1)S(1)}, bf16[768,768]{1,0:T(8,128)(2,1)}, u32[]{:S(2)}, u32[]{:S(2)}) collective-permute-start(bf16[768,768]{1,0:T(8,128)(2,1)S(1)} %copy-done.42), channel_id=1, source_target_pairs={{0,4},{4,0},{8,12},{12,8},{16,20},{20,16},{24,28},{28,24},{1,5},{5... | collective-permute-start | bytes 3538952 | tf_op jit(solution)/shard_map/ppermute | solution.py:46
  451.6 24.8 %collective-permute-start.48 = (bf16[384,768]{1,0:T(8,128)(2,1)S(1)}, bf16[384,768]{1,0:T(8,128)(2,1)S(1)}, u32[]{:S(2)}, u32[]{:S(2)}) collective-permute-start(bf16[384,768]{1,0:T(8,128)(2,1)S(1)} %copy-done.47), channel_id=1, source_target_pairs={{0,4},{4,0},{8,12},{12,8},{16,20},{20,16},{24,28},{28,24},{1,5},{5... | collective-permute-start | bytes 1769480 | tf_op jit(solution)/shard_map/ppermute | solution.py:46
  (157 other events, 1468.3 us)
Sparse Core Ops, SparseCore 0:
  10.9 77.8 all-gather.4
  90.9 75.5 all-gather.8
  168.1 17.3 all-gather.6
  318.8 76.9 all-reduce.8
  398.1 90.6 reduce-scatter.1
